TPU v7x, 32 devices: a whole 2x2x4 slice. The times are simulated.
32 devices in a mesh: psg: 16 (over z, y, x), qry: 2 (over core).
Axes of the slice: x: 2, y: 2, z: 4, core: 2. Of those that a mesh axis runs over, the one named last changes fastest.
Arguments:
- queries: bfloat16 [256, 32, 128], P(('psg', 'qry')), may hold values from -0.59765625 to 0.59765625
- cand_shard: int32 [256, 256, 1], P(('psg', 'qry')), may hold values from 0 to 31; in each aligned block of 256 rows (0 to 255, 256 to 511, ..., all dimensions but the last counted through in order) at most 16 rows name the same one
- cand_local: int32 [256, 256], P(('psg', 'qry')), may hold values from 0 to 63
- passages: bfloat16 [2048, 70, 128], P(('psg', 'qry')), may hold values from -0.59765625 to 0.59765625
- lengths: int32 [2048], P(('psg', 'qry')), may hold values from 8 to 70
Outputs:
- scores: float32 [256, 256], P(('psg', 'qry'))
Inputs may be any that keep to these rules, and one draw needn't show every extreme that they name: `cand_shard`: among the 256 candidates of one query no device is named more than 16 times, and some query names some device exactly 16 times; some devices hold far more candidates than others.
All inputs are finite; a program needn't handle non-finite values.
Results may differ from a plain program's by a relative error of at most 0.0003.
Values may be sent and summed in bfloat16 or wider, within the bound.
No kernel may reach another device: no remote copies, remote signals or barrier semaphores. Data moves between devices by JAX's collectives and lax.ppermute only.
A program may use at most 128 MiB of HBM per device.

v0:
```python
import jax
import jax.numpy as jnp
from jax import lax
from jax.sharding import PartitionSpec as P


def select_tiles(passage_row, passages, lengths):
    store_rows = passages.shape[0]
    token_slots = passages.shape[1]
    feature_dim = passages.shape[2]
    row_ids = jnp.arange(store_rows, dtype=jnp.int32)
    match_table = passage_row[..., None] == row_ids
    selector = match_table.astype(jnp.bfloat16)
    flat_store = passages.reshape(store_rows, token_slots * feature_dim)
    picked = jnp.dot(
        selector.reshape(-1, store_rows), flat_store, preferred_element_type=jnp.float32
    ).astype(jnp.bfloat16)
    picked = picked.reshape(passage_row.shape + (token_slots, feature_dim))
    token_counts = jnp.sum(jnp.where(match_table, lengths, 0), axis=-1)
    return (picked, token_counts)


def padded_block(query_matrix_rows, slot_lists, passages, lengths):
    passage_row = jnp.maximum(slot_lists, 0)
    passage_tile_block, token_counts = select_tiles(passage_row, passages, lengths)
    token_similarity = jnp.einsum(
        "ajs,aeks->aejk", query_matrix_rows, passage_tile_block, preferred_element_type=jnp.float32
    )
    positions = jnp.arange(passage_tile_block.shape[2], dtype=jnp.int32)
    valid_tokens = positions[None, None, None, :] < token_counts[:, :, None, None]
    maxsim_sum = jnp.sum(jnp.max(jnp.where(valid_tokens, token_similarity, -1e30), axis=3), axis=2)
    return jnp.where(slot_lists >= 0, maxsim_sum, 0.0)


def score_rows(query_matrix_rows, slot_lists, passages, lengths):
    row_count, capacity = slot_lists.shape
    block_rows = max(1, 512 // capacity)
    block_count = row_count // block_rows

    def tile_scores(tiles):
        return padded_block(tiles[0], tiles[1], passages, lengths)

    tiled = lax.map(
        tile_scores,
        (
            query_matrix_rows.reshape(
                block_count, block_rows, query_matrix_rows.shape[1], query_matrix_rows.shape[2]
            ),
            slot_lists.reshape(block_count, block_rows, capacity),
        ),
    )
    return tiled.reshape(row_count, capacity)


def body(queries, cand_shard, cand_local, passages, lengths):
    local_queries, pool_depth = cand_local.shape
    psg_count = lax.axis_size("psg")
    core_count = lax.axis_size("qry")
    devices_all = psg_count * core_count
    capacity = 2 * pool_depth // devices_all
    owner_device = cand_shard[:, :, 0]
    same_owner = owner_device[:, :, None] == owner_device[:, None, :]
    positions = jnp.arange(pool_depth, dtype=jnp.int32)
    before = positions[None, :] < positions[:, None]
    slot_rank = jnp.sum((same_owner & before[None]).astype(jnp.int32), axis=2)
    query_row = jnp.broadcast_to(
        jnp.arange(local_queries, dtype=jnp.int32)[:, None], owner_device.shape
    )
    outgoing = jnp.full((devices_all, local_queries, capacity), -1, jnp.int32)
    outgoing = outgoing.at[owner_device, query_row, slot_rank].set(cand_local)
    outgoing = outgoing.reshape(psg_count, core_count, local_queries, capacity)
    arrived = lax.all_to_all(
        lax.all_to_all(outgoing, "psg", split_axis=0, concat_axis=0, tiled=True),
        "qry",
        split_axis=1,
        concat_axis=1,
        tiled=True,
    )
    flat_lists = arrived.reshape(devices_all * local_queries, capacity)
    rescored_output = score_rows(
        lax.all_gather(queries, ("psg", "qry"), axis=0, tiled=True), flat_lists, passages, lengths
    )
    rescored_output = rescored_output.reshape(psg_count, core_count, local_queries, capacity)
    returned = lax.all_to_all(
        lax.all_to_all(rescored_output, "psg", split_axis=0, concat_axis=0, tiled=True),
        "qry",
        split_axis=1,
        concat_axis=1,
        tiled=True,
    )
    returned = returned.reshape(devices_all, local_queries, capacity)
    return returned[owner_device, query_row, slot_rank]


def solution(mesh):
    in_specs = (
        P(("psg", "qry"), None, None),
        P(("psg", "qry"), None, None),
        P(("psg", "qry"), None),
        P(("psg", "qry"), None, None),
        P(("psg", "qry")),
    )
    out_specs = P(("psg", "qry"), None)
    return jax.shard_map(body, mesh=mesh, in_specs=in_specs, out_specs=out_specs, check_vma=False)
```

profile of v0, /device:TPU:0, one launch (start us, length us, event | category | flops | bytes accessed | tf_op | source)
XLA Modules:
  0.0 379.3 jit_solution(15402435479183409291)
XLA Ops:
  6.5 0.7 all-gather.2.cloned.1.call-update
  7.3 0.7 copy.41
  8.0 0.8 convert_reduce_fusion
  8.8 0.7 or_bitcast_fusion
  9.5 0.7 multiply_reduce_fusion
  10.2 0.7 and_reduce_fusion
  11.0 0.7 copy.29
  11.7 8.1 %scatter_custom_fusion = s32[4096]{0:T(1024)S(1)} fusion(s32[2048]{0:T(1024)S(1)} %bitcast.72, s32[2048]{0:T(1024)S(1)} %bitcast.73, s32[]{:T(128)} %constant.7.clone.1), kind=kCustom, calls=%fused_computation.25 | custom fusion | bytes 16388
  19.9 0.7 reshape.97
  20.6 8.3 %all-to-all-start = ((s32[16,1,256]{2,1,0:T(1,128)}), s32[16,1,256]{2,1,0:T(1,128)S(1)}, u32[]{:S(2)}, u32[]{:S(2)}) async-start(s32[16,1,256]{2,1,0:T(1,128)} %reshape.97), calls=%async_computation | async-start | bytes 32768 | tf_op jit(solution)/shard_map/all_to_all | solution.py:73
  29.0 2.0 copy.22
  31.0 5.3 %all-to-all-done = s32[16,1,256]{2,1,0:T(1,128)S(1)} async-done(((s32[16,1,256]{2,1,0:T(1,128)}), s32[16,1,256]{2,1,0:T(1,128)S(1)}, u32[]{:S(2)}, u32[]{:S(2)}) %all-to-all-start) | async-done | bytes 16416 | tf_op jit(solution)/shard_map/all_to_all | solution.py:73
  36.3 0.6 broadcast.138
  36.9 0.7 reduce.5
  37.9 3.7 all_to_all.20
  41.6 0.7 reduce.6
  42.5 26.9 %all-gather.2.cloned.1.call-done = bf16[256,32,128]{2,1,0:T(8,128)(2,1)} async-done(((bf16[8,32,128]{2,1,0:T(8,128)(2,1)}), bf16[256,32,128]{2,1,0:T(8,128)(2,1)}) %all-gather.2.cloned.1.call-update) | async-done | bytes 2097168 | tf_op jit(solution)/shard_map/all_gather | solution.py:81
  69.4 271.0 %while.10 = (s32[]{:T(128)}, f32[8,32,16]{2,1,0:T(8,128)S(1)}, s32[8,32,16]{2,1,0:T(8,128)S(1)}, s32[64]{0:T(128)S(1)}, bf16[64,70,128]{2,1,0:T(8,128)(2,1)S(1)}...) while((s32[]{:T(128)}, f32[8,32,16]{2,1,0:T(8,128)S(1)}, s32[8,32,16]{2,1,0:T(8,128)S(1)}, ...), condition=%wide.region_6.7_spmd, body=%wide.region_2.6_spmd.sunk | while | flops 887853056 | bytes 38646628 | solution.py:43
  69.4 6.2 %convolution_convert_fusion.2 = bf16[512,8960]{1,0:T(8,128)(2,1)} fusion(bf16[8,8,70,128]{3,2,1,0:T(8,128)(2,1)S(1)} %bitcast.61, s32[512]{0:T(512)S(1)} %max.22), kind=kOutput, calls=%fused_computation.2.clone.1 | convolution fusion | flops 591822848 | bytes 10323968 | tf_op jit(solution)/shard_map/while/body/eval_jaxpr/dot_general | solution.py:15
  75.6 14.4 %reshape.106 = bf16[32,16,70,128]{3,2,1,0:T(8,128)(2,1)} reshape(bf16[512,8960]{1,0:T(8,128)(2,1)} %convolution_convert_fusion.2) | data formatting | bytes 18350080 | tf_op jit(solution)/shard_map/while/body/eval_jaxpr/reshape | solution.py:18
  90.0 0.7 select_reduce_fusion.4
  90.9 12.1 %select_reduce_fusion.5 = f32[32,16,32]{2,1,0:T(8,128)S(1)} fusion(pred[32,16,70]{2,1,0:T(8,128)(4,1)S(1)} %iota_compare_fusion.8, bf16[32,16,70,128]{3,2,1,0:T(8,128)(2,1)} %reshape.106, bf16[8,32,32,128]{3,2,1,0:T(8,128)(2,1)} %get-tuple-element.135, s32[]{:T(128)} %get-tuple-element.122), kind=kOutput, calls=%fused_computation.3.clone.1 | convolution fusion | flops 295878656 | bytes 9801216 | tf_op jit(solution)/shard_map/while/body/eval_jaxpr/ajs,aeks->aejk/dot_general | solution.py:26
  103.0 0.1 reduce_sum.38
  103.3 6.2 %convolution_convert_fusion.2 = bf16[512,8960]{1,0:T(8,128)(2,1)} fusion(bf16[8,8,70,128]{3,2,1,0:T(8,128)(2,1)S(1)} %bitcast.61, s32[512]{0:T(512)S(1)} %max.22), kind=kOutput, calls=%fused_computation.2.clone.1 | convolution fusion | flops 591822848 | bytes 10323968 | tf_op jit(solution)/shard_map/while/body/eval_jaxpr/dot_general | solution.py:15
  109.5 14.4 %reshape.106 = bf16[32,16,70,128]{3,2,1,0:T(8,128)(2,1)} reshape(bf16[512,8960]{1,0:T(8,128)(2,1)} %convolution_convert_fusion.2) | data formatting | bytes 18350080 | tf_op jit(solution)/shard_map/while/body/eval_jaxpr/reshape | solution.py:18
  123.9 0.7 select_reduce_fusion.4
  124.6 0.1 iota_compare_fusion.8
  124.8 12.2 %select_reduce_fusion.5 = f32[32,16,32]{2,1,0:T(8,128)S(1)} fusion(pred[32,16,70]{2,1,0:T(8,128)(4,1)S(1)} %iota_compare_fusion.8, bf16[32,16,70,128]{3,2,1,0:T(8,128)(2,1)} %reshape.106, bf16[8,32,32,128]{3,2,1,0:T(8,128)(2,1)} %get-tuple-element.135, s32[]{:T(128)} %get-tuple-element.122), kind=kOutput, calls=%fused_computation.3.clone.1 | convolution fusion | flops 295878656 | bytes 9801216 | tf_op jit(solution)/shard_map/while/body/eval_jaxpr/ajs,aeks->aejk/dot_general | solution.py:26
  136.9 0.1 reduce_sum.38
  137.2 6.2 %convolution_convert_fusion.2 = bf16[512,8960]{1,0:T(8,128)(2,1)} fusion(bf16[8,8,70,128]{3,2,1,0:T(8,128)(2,1)S(1)} %bitcast.61, s32[512]{0:T(512)S(1)} %max.22), kind=kOutput, calls=%fused_computation.2.clone.1 | convolution fusion | flops 591822848 | bytes 10323968 | tf_op jit(solution)/shard_map/while/body/eval_jaxpr/dot_general | solution.py:15
  143.3 14.4 %reshape.106 = bf16[32,16,70,128]{3,2,1,0:T(8,128)(2,1)} reshape(bf16[512,8960]{1,0:T(8,128)(2,1)} %convolution_convert_fusion.2) | data formatting | bytes 18350080 | tf_op jit(solution)/shard_map/while/body/eval_jaxpr/reshape | solution.py:18
  157.8 0.7 select_reduce_fusion.4
  158.5 0.1 iota_compare_fusion.8
  158.6 12.2 %select_reduce_fusion.5 = f32[32,16,32]{2,1,0:T(8,128)S(1)} fusion(pred[32,16,70]{2,1,0:T(8,128)(4,1)S(1)} %iota_compare_fusion.8, bf16[32,16,70,128]{3,2,1,0:T(8,128)(2,1)} %reshape.106, bf16[8,32,32,128]{3,2,1,0:T(8,128)(2,1)} %get-tuple-element.135, s32[]{:T(128)} %get-tuple-element.122), kind=kOutput, calls=%fused_computation.3.clone.1 | convolution fusion | flops 295878656 | bytes 9801216 | tf_op jit(solution)/shard_map/while/body/eval_jaxpr/ajs,aeks->aejk/dot_general | solution.py:26
  170.8 0.1 reduce_sum.38
  171.1 6.2 %convolution_convert_fusion.2 = bf16[512,8960]{1,0:T(8,128)(2,1)} fusion(bf16[8,8,70,128]{3,2,1,0:T(8,128)(2,1)S(1)} %bitcast.61, s32[512]{0:T(512)S(1)} %max.22), kind=kOutput, calls=%fused_computation.2.clone.1 | convolution fusion | flops 591822848 | bytes 10323968 | tf_op jit(solution)/shard_map/while/body/eval_jaxpr/dot_general | solution.py:15
  177.2 14.4 %reshape.106 = bf16[32,16,70,128]{3,2,1,0:T(8,128)(2,1)} reshape(bf16[512,8960]{1,0:T(8,128)(2,1)} %convolution_convert_fusion.2) | data formatting | bytes 18350080 | tf_op jit(solution)/shard_map/while/body/eval_jaxpr/reshape | solution.py:18
  191.6 0.7 select_reduce_fusion.4
  192.5 12.2 %select_reduce_fusion.5 = f32[32,16,32]{2,1,0:T(8,128)S(1)} fusion(pred[32,16,70]{2,1,0:T(8,128)(4,1)S(1)} %iota_compare_fusion.8, bf16[32,16,70,128]{3,2,1,0:T(8,128)(2,1)} %reshape.106, bf16[8,32,32,128]{3,2,1,0:T(8,128)(2,1)} %get-tuple-element.135, s32[]{:T(128)} %get-tuple-element.122), kind=kOutput, calls=%fused_computation.3.clone.1 | convolution fusion | flops 295878656 | bytes 9801216 | tf_op jit(solution)/shard_map/while/body/eval_jaxpr/ajs,aeks->aejk/dot_general | solution.py:26
  204.9 6.2 %convolution_convert_fusion.2 = bf16[512,8960]{1,0:T(8,128)(2,1)} fusion(bf16[8,8,70,128]{3,2,1,0:T(8,128)(2,1)S(1)} %bitcast.61, s32[512]{0:T(512)S(1)} %max.22), kind=kOutput, calls=%fused_computation.2.clone.1 | convolution fusion | flops 591822848 | bytes 10323968 | tf_op jit(solution)/shard_map/while/body/eval_jaxpr/dot_general | solution.py:15
  211.1 14.4 %reshape.106 = bf16[32,16,70,128]{3,2,1,0:T(8,128)(2,1)} reshape(bf16[512,8960]{1,0:T(8,128)(2,1)} %convolution_convert_fusion.2) | data formatting | bytes 18350080 | tf_op jit(solution)/shard_map/while/body/eval_jaxpr/reshape | solution.py:18
  225.5 0.7 select_reduce_fusion.4
  226.4 12.2 %select_reduce_fusion.5 = f32[32,16,32]{2,1,0:T(8,128)S(1)} fusion(pred[32,16,70]{2,1,0:T(8,128)(4,1)S(1)} %iota_compare_fusion.8, bf16[32,16,70,128]{3,2,1,0:T(8,128)(2,1)} %reshape.106, bf16[8,32,32,128]{3,2,1,0:T(8,128)(2,1)} %get-tuple-element.135, s32[]{:T(128)} %get-tuple-element.122), kind=kOutput, calls=%fused_computation.3.clone.1 | convolution fusion | flops 295878656 | bytes 9801216 | tf_op jit(solution)/shard_map/while/body/eval_jaxpr/ajs,aeks->aejk/dot_general | solution.py:26
  238.8 6.2 %convolution_convert_fusion.2 = bf16[512,8960]{1,0:T(8,128)(2,1)} fusion(bf16[8,8,70,128]{3,2,1,0:T(8,128)(2,1)S(1)} %bitcast.61, s32[512]{0:T(512)S(1)} %max.22), kind=kOutput, calls=%fused_computation.2.clone.1 | convolution fusion | flops 591822848 | bytes 10323968 | tf_op jit(solution)/shard_map/while/body/eval_jaxpr/dot_general | solution.py:15
  245.0 14.4 %reshape.106 = bf16[32,16,70,128]{3,2,1,0:T(8,128)(2,1)} reshape(bf16[512,8960]{1,0:T(8,128)(2,1)} %convolution_convert_fusion.2) | data formatting | bytes 18350080 | tf_op jit(solution)/shard_map/while/body/eval_jaxpr/reshape | solution.py:18
  259.4 0.7 select_reduce_fusion.4
  260.2 12.2 %select_reduce_fusion.5 = f32[32,16,32]{2,1,0:T(8,128)S(1)} fusion(pred[32,16,70]{2,1,0:T(8,128)(4,1)S(1)} %iota_compare_fusion.8, bf16[32,16,70,128]{3,2,1,0:T(8,128)(2,1)} %reshape.106, bf16[8,32,32,128]{3,2,1,0:T(8,128)(2,1)} %get-tuple-element.135, s32[]{:T(128)} %get-tuple-element.122), kind=kOutput, calls=%fused_computation.3.clone.1 | convolution fusion | flops 295878656 | bytes 9801216 | tf_op jit(solution)/shard_map/while/body/eval_jaxpr/ajs,aeks->aejk/dot_general | solution.py:26
  272.7 6.2 %convolution_convert_fusion.2 = bf16[512,8960]{1,0:T(8,128)(2,1)} fusion(bf16[8,8,70,128]{3,2,1,0:T(8,128)(2,1)S(1)} %bitcast.61, s32[512]{0:T(512)S(1)} %max.22), kind=kOutput, calls=%fused_computation.2.clone.1 | convolution fusion | flops 591822848 | bytes 10323968 | tf_op jit(solution)/shard_map/while/body/eval_jaxpr/dot_general | solution.py:15
  278.8 14.4 %reshape.106 = bf16[32,16,70,128]{3,2,1,0:T(8,128)(2,1)} reshape(bf16[512,8960]{1,0:T(8,128)(2,1)} %convolution_convert_fusion.2) | data formatting | bytes 18350080 | tf_op jit(solution)/shard_map/while/body/eval_jaxpr/reshape | solution.py:18
  293.3 0.7 select_reduce_fusion.4
  294.1 12.2 %select_reduce_fusion.5 = f32[32,16,32]{2,1,0:T(8,128)S(1)} fusion(pred[32,16,70]{2,1,0:T(8,128)(4,1)S(1)} %iota_compare_fusion.8, bf16[32,16,70,128]{3,2,1,0:T(8,128)(2,1)} %reshape.106, bf16[8,32,32,128]{3,2,1,0:T(8,128)(2,1)} %get-tuple-element.135, s32[]{:T(128)} %get-tuple-element.122), kind=kOutput, calls=%fused_computation.3.clone.1 | convolution fusion | flops 295878656 | bytes 9801216 | tf_op jit(solution)/shard_map/while/body/eval_jaxpr/ajs,aeks->aejk/dot_general | solution.py:26
  306.6 6.2 %convolution_convert_fusion.2 = bf16[512,8960]{1,0:T(8,128)(2,1)} fusion(bf16[8,8,70,128]{3,2,1,0:T(8,128)(2,1)S(1)} %bitcast.61, s32[512]{0:T(512)S(1)} %max.22), kind=kOutput, calls=%fused_computation.2.clone.1 | convolution fusion | flops 591822848 | bytes 10323968 | tf_op jit(solution)/shard_map/while/body/eval_jaxpr/dot_general | solution.py:15
  312.7 14.4 %reshape.106 = bf16[32,16,70,128]{3,2,1,0:T(8,128)(2,1)} reshape(bf16[512,8960]{1,0:T(8,128)(2,1)} %convolution_convert_fusion.2) | data formatting | bytes 18350080 | tf_op jit(solution)/shard_map/while/body/eval_jaxpr/reshape | solution.py:18
  327.1 0.7 select_reduce_fusion.4
  328.0 12.2 %select_reduce_fusion.5 = f32[32,16,32]{2,1,0:T(8,128)S(1)} fusion(pred[32,16,70]{2,1,0:T(8,128)(4,1)S(1)} %iota_compare_fusion.8, bf16[32,16,70,128]{3,2,1,0:T(8,128)(2,1)} %reshape.106, bf16[8,32,32,128]{3,2,1,0:T(8,128)(2,1)} %get-tuple-element.135, s32[]{:T(128)} %get-tuple-element.122), kind=kOutput, calls=%fused_computation.3.clone.1 | convolution fusion | flops 295878656 | bytes 9801216 | tf_op jit(solution)/shard_map/while/body/eval_jaxpr/ajs,aeks->aejk/dot_general | solution.py:26
  340.3 0.7 reshape.101
  341.0 4.5 %all-to-all-start.2 = ((f32[16,1,256]{2,1,0:T(1,128)}), f32[16,1,256]{2,1,0:T(1,128)S(1)}, u32[]{:S(2)}, u32[]{:S(2)}) async-start(f32[16,1,256]{2,1,0:T(1,128)} %reshape.101), calls=%async_computation.2 | async-start | bytes 32768 | tf_op jit(solution)/shard_map/all_to_all | solution.py:85
  345.5 7.3 %all-to-all-done.2 = f32[16,1,256]{2,1,0:T(1,128)S(1)} async-done(((f32[16,1,256]{2,1,0:T(1,128)}), f32[16,1,256]{2,1,0:T(1,128)S(1)}, u32[]{:S(2)}, u32[]{:S(2)}) %all-to-all-start.2) | async-done | bytes 16416 | tf_op jit(solution)/shard_map/all_to_all | solution.py:85
  352.8 0.5 broadcast.140
  353.4 0.7 reduce.7
  354.3 3.7 all_to_all.21
  358.0 0.7 reduce.8
  358.8 13.0 %gather_fusion = f32[2048]{0:T(1024)S(1)} fusion(f32[32,8,16]{2,1,0:T(8,128)S(1)} %bitcast.59, s32[2048]{0:T(1024)S(1)} %bitcast.60), kind=kCustom, calls=%fused_computation | custom fusion | bytes 40960 | tf_op jit(solution)/shard_map/gather | solution.py:92
  371.8 0.6 reshape.85
  (64 shorter events, 3.2 us)
Async XLA Ops:
  6.5 62.8 %all-gather.2.cloned.1.call-start = ((), (), s32[]{:S(2)}) async-start(), calls=%async_computation.4 | async-start | bytes 2162688 | tf_op jit(solution)/shard_map/all_gather | solution.py:81
  8.0 61.4 %copy-start = (s32[64]{0:T(128)S(1)}, s32[64]{0:T(128)}, u32[]{:S(2)}) copy-start(s32[64]{0:T(128)} %param.11) | copy-start | bytes 772
  20.6 15.7 %all-to-all-start = ((s32[16,1,256]{2,1,0:T(1,128)}), s32[16,1,256]{2,1,0:T(1,128)S(1)}, u32[]{:S(2)}, u32[]{:S(2)}) async-start(s32[16,1,256]{2,1,0:T(1,128)} %reshape.97), calls=%async_computation | async-start | bytes 32768 | tf_op jit(solution)/shard_map/all_to_all | solution.py:73
  341.0 11.8 %all-to-all-start.2 = ((f32[16,1,256]{2,1,0:T(1,128)}), f32[16,1,256]{2,1,0:T(1,128)S(1)}, u32[]{:S(2)}, u32[]{:S(2)}) async-start(f32[16,1,256]{2,1,0:T(1,128)} %reshape.101), calls=%async_computation.2 | async-start | bytes 32768 | tf_op jit(solution)/shard_map/all_to_all | solution.py:85
Sparse Core Ops, SparseCore 0:
  10.2 59.0 all-gather.1
where the time goes:
time: 382 us; the launch traced here: 379 us
  matrix products  146 us (38%)
  local copies, waits for them, and re-layouts  144 us (38%)
  waiting for transfers between devices  40.2 us (11%)
  other arithmetic  13.9 us (4%)
  between operations  13.6 us (4%)
  starting transfers between devices  12.8 us (3%)
  blocking collectives  7.45 us (2%)
    reshape x8, local copies, waits for them, and re-layouts, select_tiles(): picked = picked.reshape(passage_row.shape + (token_slots, feature_dim))  115 us
    dot_general x8, matrix products, padded_block(): jnp.einsum('ajs,aeks->aejk', query_matrix_rows, passage_tile_block, prefe...  97.2 us
    dot_general x8, matrix products, select_tiles(): jnp.dot(selector.reshape(-1, store_rows), flat_store, preferred_element_t...  49.3 us
    all_gather x1, waiting for transfers between devices, body(): lax.all_gather(queries, ('psg', 'qry'), axis=0, tiled=True)  26.9 us
    gather x2, local copies, waits for them, and re-layouts, body(): return returned[owner_device, query_row, slot_rank]  13.6 us
    unnamed x16, local copies, waits for them, and re-layouts  11.6 us
    all_to_all x1, starting transfers between devices, body(): lax.all_to_all(outgoing, 'psg', split_axis=0, concat_axis=0, tiled=True)  8.31 us
  transfers between devices with their start and end apart: 3, of which 3 were waited for; matrix products, arithmetic and copies ran while one was open for 5% of the time, Pallas kernels for 0%

commit v1 on v0

v1 whole, which is shorter than its diff:
```python
import functools

import jax
import jax.numpy as jnp
from jax import lax
from jax.experimental import pallas as pl
from jax.experimental.pallas import tpu as pltpu
from jax.sharding import PartitionSpec as P

CONTRACT_LAST = (((1,), (1,)), ((), ()))
VMEM = pl.BlockSpec(memory_space=pltpu.VMEM)
SMEM = pl.BlockSpec(memory_space=pltpu.SMEM)
TOKENS = 32
BLOCKS = 4


def maxsim(rows, own_ref, sib_ref):
    tokens, store, dim = own_ref.shape
    width = 2 * store
    best = None
    for j in range(0, tokens, 2):
        weights = jnp.concatenate(
            [own_ref[j], sib_ref[j], own_ref[j + 1], sib_ref[j + 1]], axis=0
        )
        products = lax.dot_general(
            rows, weights, CONTRACT_LAST, preferred_element_type=jnp.float32
        )
        pair = jnp.maximum(products[:, :width], products[:, width:])
        best = pair if best is None else jnp.maximum(best, pair)
    return best


def score_kernel(ids_ref, own_ref, sib_ref, a_ref, b_ref, table_in_ref, out_ref):
    out_ref[...] = table_in_ref[...]
    blocks, half_rows, dim = a_ref.shape
    step = min(blocks, BLOCKS)
    count = half_rows // TOKENS

    def chunk(start):
        rows = jnp.concatenate(
            [ref[pl.ds(start, step)].reshape(-1, dim) for ref in (a_ref, b_ref)], axis=0
        )
        sums = maxsim(rows, own_ref, sib_ref).reshape(2, step, count, TOKENS, -1).sum(axis=3)
        for part in range(2):
            for k in range(step):
                out_ref[ids_ref[part, start + k], part * count : (part + 1) * count, :] = sums[part, k]

    if blocks == step:
        chunk(0)
    else:
        pl.loop(0, blocks, step=step)(chunk)


def score(me, a_blocks, b_blocks, own, sib, a, b, table):
    ids = me ^ jnp.array([a_blocks, b_blocks], jnp.int32)
    return pl.pallas_call(
        score_kernel,
        out_shape=jax.ShapeDtypeStruct(table.shape, jnp.float32),
        in_specs=[SMEM] + [VMEM] * 5,
        out_specs=VMEM,
        input_output_aliases={5: 0},
        compiler_params=pltpu.CompilerParams(vmem_limit_bytes=48 << 20),
        name="score",
    )(ids, own, sib, a, b, table)


def pick_kernel(core_ref, table_ref, shard_ref, local_ref, out_ref):
    chips, rows, width = table_ref.shape
    store = width // 2
    for half in range(shard_ref.shape[1] // 128):
        lanes = slice(half * 128, half * 128 + 128)
        shard = shard_ref[:, lanes]
        chip = shard // 2
        lane = ((shard % 2) ^ core_ref[0]) * store + local_ref[:, lanes]
        total = jnp.zeros(lane.shape, jnp.float32)
        for k in range(chips):
            found = jnp.take_along_axis(table_ref[k], lane, axis=1)
            total = jnp.where(chip == k, found, total)
        out_ref[:, lanes] = total


def body(queries, cand_shard, cand_local, passages, lengths):
    me = lax.axis_index("psg").astype(jnp.int32)
    core = lax.axis_index("qry").reshape(1).astype(jnp.int32)
    chips = lax.axis_size("psg")
    local, qlen, dim = queries.shape
    store, plen, _ = passages.shape

    def swap(a, bits):
        return lax.ppermute(a, "psg", [(i, i ^ bits) for i in range(chips)])

    valid = jnp.arange(plen)[None, :, None] < lengths[:, None, None]
    own = jnp.where(valid, passages, passages[:, :1]).transpose(1, 0, 2)
    sib = lax.ppermute(own, "qry", [(0, 1), (1, 0)])

    half = local * qlen // 2
    rows = queries.reshape(1, 2, half, dim)
    if chips == 16:
        column = jnp.concatenate([rows] + [swap(rows, z) for z in (4, 8, 12)], axis=0)
    else:
        column, bit = rows, 4
        while bit < chips:
            column = jnp.concatenate([column, swap(column, bit)], axis=0)
            bit *= 2
    near = list(range(0, chips, 4))
    beside = [[n ^ k for n in near] for k in range(4)]
    a, b = column[:, 0], column[:, 1]
    a1, b1 = swap(a, 1), swap(b, 2)
    a2 = swap(jnp.concatenate([a, a1]), 2)
    b2 = swap(jnp.concatenate([b, b1]), 1)
    table = jnp.zeros((chips, local, 2 * store), jnp.float32)
    table = score(me, beside[0], beside[0], own, sib, a, b, table)
    table = score(me, beside[1], beside[2], own, sib, a1, b1, table)
    table = score(me, beside[2] + beside[3], beside[1] + beside[3], own, sib, a2, b2, table)
    returned = lax.all_to_all(table, "psg", split_axis=0, concat_axis=0, tiled=True)
    return pl.pallas_call(
        pick_kernel,
        out_shape=jax.ShapeDtypeStruct(cand_local.shape, jnp.float32),
        in_specs=[SMEM, VMEM, VMEM, VMEM],
        out_specs=VMEM,
        name="pick",
    )(core, returned, cand_shard[:, :, 0], cand_local)


def solution(mesh):
    in_specs = (
        P(("psg", "qry"), None, None),
        P(("psg", "qry"), None, None),
        P(("psg", "qry"), None),
        P(("psg", "qry"), None, None),
        P(("psg", "qry")),
    )
    out_specs = P(("psg", "qry"), None)
    return jax.shard_map(body, mesh=mesh, in_specs=in_specs, out_specs=out_specs, check_vma=False)
```

time: 382 us -> 60.6 us (0.16)
  matrix products: 146 us -> 0 us
  local copies, waits for them, and re-layouts: 144 us -> 2.62 us
  waiting for transfers between devices: 40.2 us -> 13 us
  Pallas kernels: 0 us -> 26.1 us
  between operations: 13.6 us -> 0.13 us
  other arithmetic: 13.9 us -> 2.63 us
  blocking collectives: 7.45 us -> 0 us
    dot_general x16 -> x0, matrix products: 146 us -> none  [the longest x8 97.2 us: padded_block(): jnp.einsum('ajs,aeks->aejk', query_matrix_rows, passage_tile_block, prefe...]
    reshape x8 -> x0, local copies, waits for them, and re-layouts: 115 us -> none  [select_tiles(): picked = picked.reshape(passage_row.shape + (token_slots, feature_dim))]
    all_gather x1 -> x0, waiting for transfers between devices: 26.9 us -> none  [body(): lax.all_gather(queries, ('psg', 'qry'), axis=0, tiled=True)]
    pallas_call x0 -> x4, Pallas kernels: none -> 26.1 us  [the longest x3 24.5 us: score(): pl.pallas_call(score_kernel, out_shape=jax.ShapeDtypeStruct(table.shape,...]
    gather x2 -> x0, local copies, waits for them, and re-layouts: 13.6 us -> none  [body(): return returned[owner_device, query_row, slot_rank]]
    ppermute x0 -> x8, starting transfers between devices: none -> 10.7 us  [the longest x7 10.6 us: swap(): return lax.ppermute(a, 'psg', [(i, i ^ bits) for i in range(chips)])]
    unnamed x16 -> x13, local copies, waits for them, and re-layouts: 11.6 us -> 1.25 us
    all_to_all x2 -> x1, starting transfers between devices: 12.8 us -> 5.02 us  [body(): lax.all_to_all(table, 'psg', split_axis=0, concat_axis=0, tiled=True)]
  transfers between devices with their start and end apart: 3 -> 9, of which waited for: 3 -> 5; matrix products, arithmetic and copies ran while one was open for 5% -> 8% of each run, Pallas kernels for 0% -> 21%
where the time goes in v1:
time: 60.6 us; the launch traced here: 60.2 us
  Pallas kernels  26.1 us (43%)
  starting transfers between devices  15.7 us (26%)
  waiting for transfers between devices  13 us (21%)
  other arithmetic  2.63 us (4%)
  local copies, waits for them, and re-layouts  2.62 us (4%)
    pallas_call x3, Pallas kernels, score(): pl.pallas_call(score_kernel, out_shape=jax.ShapeDtypeStruct(table.shape,...  24.5 us
    ppermute x7, starting transfers between devices, swap(): return lax.ppermute(a, 'psg', [(i, i ^ bits) for i in range(chips)])  10.6 us
    all_to_all x1, waiting for transfers between devices, body(): lax.all_to_all(table, 'psg', split_axis=0, concat_axis=0, tiled=True)  6.92 us
    ppermute x7, waiting for transfers between devices, swap(): return lax.ppermute(a, 'psg', [(i, i ^ bits) for i in range(chips)])  6.03 us
    all_to_all x1, starting transfers between devices, body(): lax.all_to_all(table, 'psg', split_axis=0, concat_axis=0, tiled=True)  5.02 us
    transpose x1, other arithmetic, body(): own = jnp.where(valid, passages, passages[:, :1]).transpose(1, 0, 2)  1.87 us
    pallas_call x1, Pallas kernels, body(): pl.pallas_call(pick_kernel, out_shape=jax.ShapeDtypeStruct(cand_local.sha...  1.57 us
    unnamed x13, local copies, waits for them, and re-layouts  1.25 us
  transfers between devices with their start and end apart: 9, of which 5 were waited for; matrix products, arithmetic and copies ran while one was open for 8% of the time, Pallas kernels for 21%

profile of v1, /device:TPU:0, one launch (start us, length us, event | category | flops | bytes accessed | tf_op | source)
XLA Modules:
  0.0 60.2 jit_solution(10323463349006380592)
XLA Ops:
  0.0 3.0 %collective-permute-start.1 = (bf16[1,2,128,128]{3,2,0,1:T(8,128)(2,1)}, bf16[1,2,128,128]{3,2,0,1:T(8,128)(2,1)S(1)}, u32[]{:S(2)}, u32[]{:S(2)}) collective-permute-start(bf16[1,2,128,128]{3,2,0,1:T(8,128)(2,1)} %bitcast.13), channel_id=1, source_target_pairs={{0,8},{2,10},{4,12},{6,14},{8,0},{10,2},{12,4},{14,6},{16,24},{18,... | collective-permute-start | bytes 196616 | tf_op jit(solution)/shard_map/ppermute | solution.py:90
  3.0 2.6 %collective-permute-start.2 = (bf16[1,2,128,128]{3,2,0,1:T(8,128)(2,1)}, bf16[1,2,128,128]{3,2,0,1:T(8,128)(2,1)S(1)}, u32[]{:S(2)}, u32[]{:S(2)}) collective-permute-start(bf16[1,2,128,128]{3,2,0,1:T(8,128)(2,1)} %bitcast.14), channel_id=1, source_target_pairs={{0,16},{2,18},{4,20},{6,22},{8,24},{10,26},{12,28},{14,30},{16,0},... | collective-permute-start | bytes 196616 | tf_op jit(solution)/shard_map/ppermute | solution.py:90
  5.6 0.0 collective-permute-start.3
  5.6 0.7 %slice_bitcast_fusion.2 = bf16[64,128]{1,0:T(8,128)(2,1)S(1)} fusion(bf16[64,70,128]{2,0,1:T(8,128)(2,1)} %param.11), kind=kLoop, calls=%fused_computation.7 | loop fusion | bytes 32768 | tf_op jit(solution)/shard_map/jit(_where)/broadcast_in_dim | solution.py:93
  6.3 0.7 %iota_compare_fusion = pred[64,70]{0,1:T(8,128)(4,1)S(1)} fusion(s32[64]{0:T(128)} %param.12), kind=kLoop, calls=%fused_computation.6 | loop fusion | flops 4480 | bytes 4736 | tf_op jit(solution)/shard_map/lt | solution.py:92
  7.0 0.0 copy-start.1
  7.0 0.0 copy-start.5
  7.0 1.9 %select_bitcast_fusion.own_ref = bf16[70,64,128]{2,1,0:T(8,128)(2,1)S(1)} fusion(bf16[64,70,128]{2,0,1:T(8,128)(2,1)} %param.11, pred[64,70]{0,1:T(8,128)(4,1)S(1)} %iota_compare_fusion, bf16[64,128]{1,0:T(8,128)(2,1)S(1)} %slice_bitcast_fusion.2), kind=kLoop, calls=%fused_computation | loop fusion | flops 573440 | bytes 2314624 | tf_op jit(solution)/shard_map/transpose | solution.py:93
  8.9 0.0 copy-start.4
  8.9 0.0 copy-start.3
  8.9 0.1 collective-permute-start
  9.0 0.0 collective-permute-done.1
  9.0 1.5 %collective-permute-done.2 = bf16[1,2,128,128]{3,2,0,1:T(8,128)(2,1)S(1)} collective-permute-done((bf16[1,2,128,128]{3,2,0,1:T(8,128)(2,1)}, bf16[1,2,128,128]{3,2,0,1:T(8,128)(2,1)S(1)}, u32[]{:S(2)}, u32[]{:S(2)}) %collective-permute-start.2) | collective-permute-done | bytes 65568 | tf_op jit(solution)/shard_map/ppermute | solution.py:90
  10.5 1.4 %collective-permute-done.3 = bf16[1,2,128,128]{3,2,0,1:T(8,128)(2,1)S(1)} collective-permute-done((bf16[1,2,128,128]{3,2,0,1:T(8,128)(2,1)}, bf16[1,2,128,128]{3,2,0,1:T(8,128)(2,1)S(1)}, u32[]{:S(2)}, u32[]{:S(2)}) %collective-permute-start.3) | collective-permute-done | bytes 65568 | tf_op jit(solution)/shard_map/ppermute | solution.py:90
  11.9 0.0 copy-done.1
  12.0 1.6 %collective-permute-start.4 = (bf16[4,128,128]{2,1,0:T(8,128)(2,1)S(1)}, bf16[4,128,128]{2,1,0:T(8,128)(2,1)S(1)}, u32[]{:S(2)}, u32[]{:S(2)}) collective-permute-start(bf16[4,128,128]{2,1,0:T(8,128)(2,1)S(1)} %get-tuple-element.6.a_ref), channel_id=1, source_target_pairs={{0,2},{2,0},{4,6},{6,4},{8,10},{10,8},{12,14},{14,12},{16,18},{18,... | collective-permute-start | bytes 393224 | tf_op jit(solution)/shard_map/ppermute | solution.py:90
  13.5 1.5 %collective-permute-start.6 = (bf16[4,128,128]{2,1,0:T(8,128)(2,1)S(1)}, bf16[4,128,128]{2,1,0:T(8,128)(2,1)S(1)}, u32[]{:S(2)}, u32[]{:S(2)}) collective-permute-start(bf16[4,128,128]{2,1,0:T(8,128)(2,1)S(1)} %get-tuple-element.5.b_ref), channel_id=1, source_target_pairs={{0,4},{2,6},{4,0},{6,2},{8,12},{10,14},{12,8},{14,10},{16,20},{18,... | collective-permute-start | bytes 393224 | tf_op jit(solution)/shard_map/ppermute | solution.py:90
  15.1 0.0 copy-done.5
  15.1 2.0 %collective-permute-done.4.a_ref = bf16[4,128,128]{2,1,0:T(8,128)(2,1)S(1)} collective-permute-done((bf16[4,128,128]{2,1,0:T(8,128)(2,1)S(1)}, bf16[4,128,128]{2,1,0:T(8,128)(2,1)S(1)}, u32[]{:S(2)}, u32[]{:S(2)}) %collective-permute-start.4) | collective-permute-done | bytes 131104 | tf_op jit(solution)/shard_map/ppermute | solution.py:90
  17.0 1.6 %collective-permute-start.5 = (bf16[8,128,128]{2,1,0:T(8,128)(2,1)S(1)}, bf16[8,128,128]{2,1,0:T(8,128)(2,1)S(1)}, u32[]{:S(2)}, u32[]{:S(2)}) collective-permute-start(bf16[8,128,128]{2,1,0:T(8,128)(2,1)S(1)} %pad_maximum_fusion.1), channel_id=1, source_target_pairs={{0,4},{2,6},{4,0},{6,2},{8,12},{10,14},{12,8},{14,10},{16,20},{18,... | collective-permute-start | bytes 786440 | tf_op jit(solution)/shard_map/ppermute | solution.py:90
  18.6 1.2 %collective-permute-done.6.b_ref = bf16[4,128,128]{2,1,0:T(8,128)(2,1)S(1)} collective-permute-done((bf16[4,128,128]{2,1,0:T(8,128)(2,1)S(1)}, bf16[4,128,128]{2,1,0:T(8,128)(2,1)S(1)}, u32[]{:S(2)}, u32[]{:S(2)}) %collective-permute-start.6) | collective-permute-done | bytes 131104 | tf_op jit(solution)/shard_map/ppermute | solution.py:90
  19.9 0.4 collective-permute-start.7
  20.2 0.0 copy-done.4
  20.2 0.0 copy-done.3
  20.2 0.0 collective-permute-done.sib_ref
  20.2 0.6 %broadcast_in_dim.26.table_in_ref = f32[16,8,128]{2,1,0:T(8,128)} broadcast(f32[]{:T(128)} %constant.15.clone.1), dimensions={} | broadcast | bytes 65540 | tf_op jit(solution)/shard_map/broadcast_in_dim | solution.py:111
  20.9 6.4 %score.3.table_in_ref = f32[16,8,128]{2,1,0:T(8,128)} custom-call(s32[2,4]{1,0:T(2,128)S(1)} %broadcast_xor_fusion.ids_ref, bf16[70,64,128]{2,1,0:T(8,128)(2,1)S(1)} %select_bitcast_fusion.own_ref, bf16[70,64,128]{2,1,0:T(8,128)(2,1)S(1)} %collective-permute-done.sib_ref, ...), custom_call_target="tpu_custom_call", output_to_operand_aliasing={{}: (5, {})} | custom-call | tf_op jit(solution)/shard_map/score/pallas_call | solution.py:56
  27.3 6.4 %score.4.table_in_ref = f32[16,8,128]{2,1,0:T(8,128)} custom-call(s32[2,4]{1,0:T(2,128)S(1)} %broadcast_xor_fusion.1.ids_ref, bf16[70,64,128]{2,1,0:T(8,128)(2,1)S(1)} %select_bitcast_fusion.own_ref, bf16[70,64,128]{2,1,0:T(8,128)(2,1)S(1)} %collective-permute-done.sib_ref, ...), custom_call_target="tpu_custom_call", output_to_operand_aliasing={{}: (5, {})} | custom-call | tf_op jit(solution)/shard_map/score/pallas_call | solution.py:56
  33.7 0.0 copy-start.2
  33.7 0.0 collective-permute-done.5.a_ref
  33.7 0.0 collective-permute-done.7.b_ref
  33.8 11.6 %score.5 = f32[16,8,128]{2,1,0:T(8,128)} custom-call(s32[2,8]{1,0:T(2,128)S(1)} %broadcast_xor_fusion.2.ids_ref, bf16[70,64,128]{2,1,0:T(8,128)(2,1)S(1)} %select_bitcast_fusion.own_ref, bf16[70,64,128]{2,1,0:T(8,128)(2,1)S(1)} %collective-permute-done.sib_ref, ...), custom_call_target="tpu_custom_call", output_to_operand_aliasing={{}: (5, {})} | custom-call | tf_op jit(solution)/shard_map/score/pallas_call | solution.py:56
  45.4 5.0 %all-to-all-start = ((f32[16,8,128]{2,1,0:T(8,128)}), f32[16,8,128]{2,1,0:T(8,128)S(1)}, u32[]{:S(2)}, u32[]{:S(2)}) async-start(f32[16,8,128]{2,1,0:T(8,128)} %score.5), calls=%async_computation | async-start | bytes 131072 | tf_op jit(solution)/shard_map/all_to_all | solution.py:115
  50.4 0.0 copy-done.2
  50.4 0.6 copy.14
  51.0 6.9 %all-to-all-done.table_ref = f32[16,8,128]{2,1,0:T(8,128)S(1)} async-done(((f32[16,8,128]{2,1,0:T(8,128)}), f32[16,8,128]{2,1,0:T(8,128)S(1)}, u32[]{:S(2)}, u32[]{:S(2)}) %all-to-all-start) | async-done | bytes 65568 | tf_op jit(solution)/shard_map/all_to_all | solution.py:115
  58.0 0.0 copy-start
  58.0 0.6 %copy-done = f32[16,8,128]{2,1,0:T(8,128)} copy-done((f32[16,8,128]{2,1,0:T(8,128)}, f32[16,8,128]{2,1,0:T(8,128)S(1)}, u32[]{:S(2)}) %copy-start) | copy-done | bytes 65560
  58.6 1.6 %pick.1 = f32[8,256]{1,0:T(8,128)} custom-call(s32[1]{0:T(128)} %bitcast.core_ref, f32[16,8,128]{2,1,0:T(8,128)} %copy-done, s32[8,256]{1,0:T(8,128)} %bitcast.17, s32[8,256]{1,0:T(8,128)} %local_ref.1), custom_call_target="tpu_custom_call" | custom-call | tf_op jit(solution)/shard_map/pick/pallas_call | solution.py:116
  (7 shorter events, 0.1 us)
Async XLA Ops:
  0.0 9.0 %collective-permute-start.1 = (bf16[1,2,128,128]{3,2,0,1:T(8,128)(2,1)}, bf16[1,2,128,128]{3,2,0,1:T(8,128)(2,1)S(1)}, u32[]{:S(2)}, u32[]{:S(2)}) collective-permute-start(bf16[1,2,128,128]{3,2,0,1:T(8,128)(2,1)} %bitcast.13), channel_id=1, source_target_pairs={{0,8},{2,10},{4,12},{6,14},{8,0},{10,2},{12,4},{14,6},{16,24},{18,... | collective-permute-start | bytes 196616 | tf_op jit(solution)/shard_map/ppermute | solution.py:90
  3.0 7.5 %collective-permute-start.2 = (bf16[1,2,128,128]{3,2,0,1:T(8,128)(2,1)}, bf16[1,2,128,128]{3,2,0,1:T(8,128)(2,1)S(1)}, u32[]{:S(2)}, u32[]{:S(2)}) collective-permute-start(bf16[1,2,128,128]{3,2,0,1:T(8,128)(2,1)} %bitcast.14), channel_id=1, source_target_pairs={{0,16},{2,18},{4,20},{6,22},{8,24},{10,26},{12,28},{14,30},{16,0},... | collective-permute-start | bytes 196616 | tf_op jit(solution)/shard_map/ppermute | solution.py:90
  5.6 6.3 %collective-permute-start.3 = (bf16[1,2,128,128]{3,2,0,1:T(8,128)(2,1)}, bf16[1,2,128,128]{3,2,0,1:T(8,128)(2,1)S(1)}, u32[]{:S(2)}, u32[]{:S(2)}) collective-permute-start(bf16[1,2,128,128]{3,2,0,1:T(8,128)(2,1)} %bitcast.15), channel_id=1, source_target_pairs={{0,24},{2,26},{4,28},{6,30},{8,16},{10,18},{12,20},{14,22},{16,8},... | collective-permute-start | bytes 196616 | tf_op jit(solution)/shard_map/ppermute | solution.py:90
  7.0 4.9 %copy-start.1 = (bf16[8,32,128]{2,1,0:T(8,128)(2,1)S(1)}, bf16[8,32,128]{2,1,0:T(8,128)(2,1)}, u32[]{:S(2)}) copy-start(bf16[8,32,128]{2,1,0:T(8,128)(2,1)} %param.8) | copy-start | bytes 196612
  7.0 8.1 %copy-start.5 = (s32[2,4]{1,0:T(2,128)S(1)}, s32[2,4]{1,0:T(2,128)}, u32[]{:S(2)}) copy-start(s32[2,4]{1,0:T(2,128)} %constant.16.clone) | copy-start | bytes 100
  8.9 11.3 %copy-start.4 = (s32[2,4]{1,0:T(2,128)S(1)}, s32[2,4]{1,0:T(2,128)}, u32[]{:S(2)}) copy-start(s32[2,4]{1,0:T(2,128)} %constant.17.clone) | copy-start | bytes 100
  8.9 11.3 %copy-start.3 = (s32[2,8]{1,0:T(2,128)S(1)}, s32[2,8]{1,0:T(2,128)}, u32[]{:S(2)}) copy-start(s32[2,8]{1,0:T(2,128)} %constant.18.clone) | copy-start | bytes 196
  8.9 11.3 %collective-permute-start = (bf16[70,64,128]{2,1,0:T(8,128)(2,1)S(1)}, bf16[70,64,128]{2,1,0:T(8,128)(2,1)S(1)}, u32[]{:S(2)}, u32[]{:S(2)}) collective-permute-start(bf16[70,64,128]{2,1,0:T(8,128)(2,1)S(1)} %select_bitcast_fusion.own_ref), channel_id=1, source_target_pairs={{0,1},{1,0},{2,3},{3,2},{4,5},{5,4},{6,7},{7,6},{8,9},{9,8},{10,11... | collective-permute-start | bytes 3440648 | tf_op jit(solution)/shard_map/ppermute | solution.py:94
  12.0 5.0 %collective-permute-start.4 = (bf16[4,128,128]{2,1,0:T(8,128)(2,1)S(1)}, bf16[4,128,128]{2,1,0:T(8,128)(2,1)S(1)}, u32[]{:S(2)}, u32[]{:S(2)}) collective-permute-start(bf16[4,128,128]{2,1,0:T(8,128)(2,1)S(1)} %get-tuple-element.6.a_ref), channel_id=1, source_target_pairs={{0,2},{2,0},{4,6},{6,4},{8,10},{10,8},{12,14},{14,12},{16,18},{18,... | collective-permute-start | bytes 393224 | tf_op jit(solution)/shard_map/ppermute | solution.py:90
  13.5 6.3 %collective-permute-start.6 = (bf16[4,128,128]{2,1,0:T(8,128)(2,1)S(1)}, bf16[4,128,128]{2,1,0:T(8,128)(2,1)S(1)}, u32[]{:S(2)}, u32[]{:S(2)}) collective-permute-start(bf16[4,128,128]{2,1,0:T(8,128)(2,1)S(1)} %get-tuple-element.5.b_ref), channel_id=1, source_target_pairs={{0,4},{2,6},{4,0},{6,2},{8,12},{10,14},{12,8},{14,10},{16,20},{18,... | collective-permute-start | bytes 393224 | tf_op jit(solution)/shard_map/ppermute | solution.py:90
  17.0 16.7 %collective-permute-start.5 = (bf16[8,128,128]{2,1,0:T(8,128)(2,1)S(1)}, bf16[8,128,128]{2,1,0:T(8,128)(2,1)S(1)}, u32[]{:S(2)}, u32[]{:S(2)}) collective-permute-start(bf16[8,128,128]{2,1,0:T(8,128)(2,1)S(1)} %pad_maximum_fusion.1), channel_id=1, source_target_pairs={{0,4},{2,6},{4,0},{6,2},{8,12},{10,14},{12,8},{14,10},{16,20},{18,... | collective-permute-start | bytes 786440 | tf_op jit(solution)/shard_map/ppermute | solution.py:90
  19.9 13.9 %collective-permute-start.7 = (bf16[8,128,128]{2,1,0:T(8,128)(2,1)S(1)}, bf16[8,128,128]{2,1,0:T(8,128)(2,1)S(1)}, u32[]{:S(2)}, u32[]{:S(2)}) collective-permute-start(bf16[8,128,128]{2,1,0:T(8,128)(2,1)S(1)} %pad_maximum_fusion.2), channel_id=1, source_target_pairs={{0,2},{2,0},{4,6},{6,4},{8,10},{10,8},{12,14},{14,12},{16,18},{18,... | collective-permute-start | bytes 786440 | tf_op jit(solution)/shard_map/ppermute | solution.py:90
  33.7 16.7 %copy-start.2 = (s32[8,256,1]{1,2,0:T(1,128)S(1)}, s32[8,256,1]{1,2,0:T(1,128)}, u32[]{:S(2)}) copy-start(s32[8,256,1]{1,2,0:T(1,128)} %param.9) | copy-start | bytes 24580
  45.4 12.6 %all-to-all-start = ((f32[16,8,128]{2,1,0:T(8,128)}), f32[16,8,128]{2,1,0:T(8,128)S(1)}, u32[]{:S(2)}, u32[]{:S(2)}) async-start(f32[16,8,128]{2,1,0:T(8,128)} %score.5), calls=%async_computation | async-start | bytes 131072 | tf_op jit(solution)/shard_map/all_to_all | solution.py:115
  58.0 0.6 %copy-start = (f32[16,8,128]{2,1,0:T(8,128)}, f32[16,8,128]{2,1,0:T(8,128)S(1)}, u32[]{:S(2)}) copy-start(f32[16,8,128]{2,1,0:T(8,128)S(1)} %all-to-all-done.table_ref) | copy-start | bytes 196612

commit v2 on v1

v2 whole, which is shorter than its diff:
```python
import functools

import jax
import jax.numpy as jnp
from jax import lax
from jax.experimental import pallas as pl
from jax.experimental.pallas import tpu as pltpu
from jax.sharding import PartitionSpec as P

VMEM = pl.BlockSpec(memory_space=pltpu.VMEM)
SMEM = pl.BlockSpec(memory_space=pltpu.SMEM)
TOKENS = 32
BLOCKS = 4
GROUPS = 2
CHUNK = 8
LANES = 128
LOWEST = -1e30


def prep_kernel(lengths_ref, passages_ref, out_ref):
    slots, store, dim = passages_ref.shape
    padded = out_ref.shape[0] - 2
    per_core = store // GROUPS
    shape = (store, 2 * store)
    along = jnp.broadcast_to(lengths_ref[...], shape)
    row = lax.broadcasted_iota(jnp.int32, shape, 0)
    lane = lax.broadcasted_iota(jnp.int32, shape, 1)
    lane = jnp.where(lane >= store, lane - store, lane)
    down = jnp.sum(jnp.where(lane == row, along, 0), axis=1, keepdims=True) // 2
    longer = (down > along) | ((down == along) & (row < lane))
    rank = jnp.sum(longer.astype(jnp.int32), axis=0, keepdims=True)
    sorted_lengths = jnp.sum(jnp.where(rank == row, along, 0), axis=1, keepdims=True) // 2

    square = (2 * store, 2 * store)
    row = lax.broadcasted_iota(jnp.int32, square, 0)
    lane = lax.broadcasted_iota(jnp.int32, square, 1)
    target = rank + jnp.where(lane >= store, store, 0)
    order = (target == row).astype(jnp.float32).astype(passages_ref.dtype)

    first = None
    for t in range(0, slots, 2):
        pair = passages_ref[t : t + 2].reshape(2 * store, dim)
        moved = jnp.dot(order, pair, preferred_element_type=jnp.float32).reshape(2, store, dim)
        first = moved[0] if first is None else first
        for k in range(2):
            out_ref[t + k] = jnp.where(t + k < sorted_lengths, moved[k], first).astype(out_ref.dtype)
    for t in range(slots, padded):
        out_ref[t] = first.astype(out_ref.dtype)
    place = rank + jnp.where(rank >= per_core, per_core, 0)
    for k, value in enumerate((sorted_lengths, place)):
        value = jnp.broadcast_to(value, (store, dim)).astype(jnp.float32)
        out_ref[padded + k] = value.astype(out_ref.dtype)


def prep(passages, lengths):
    store, slots, dim = passages.shape
    padded = -(-slots // CHUNK) * CHUNK
    return pl.pallas_call(
        prep_kernel,
        out_shape=jax.ShapeDtypeStruct((padded + 2, store, dim), passages.dtype),
        in_specs=[VMEM, VMEM],
        out_specs=VMEM,
        compiler_params=pltpu.CompilerParams(vmem_limit_bytes=12 << 20),
        name="prep",
    )(jnp.tile(lengths, 2).reshape(1, 2 * store), passages.transpose(1, 0, 2))


def chunk_counts(own, sib):
    per_core = own.shape[1] // GROUPS
    longest = [plane[-2, ::per_core, 0].astype(jnp.int32) for plane in (own, sib)]
    return (jnp.maximum(*longest) + CHUNK - 1) // CHUNK


def score_block(own_ref, sib_ref, read_rows, acc, sums, units, counts, write):
    half = acc[0].shape[1]
    per_core = own_ref.shape[1] // GROUPS
    width = 2 * per_core
    per_tile = 2 * LANES // width
    last = counts[0] + counts[1] - 1
    zeros = jnp.zeros((2 * LANES, LANES), own_ref.dtype)

    def where_of(step):
        group = (step >= counts[0]).astype(jnp.int32)
        return group, step - group * counts[0]

    def push(step):
        group, at = where_of(step)
        lanes = pl.ds(pl.multiple_of(group * per_core, per_core), per_core)
        for unit in range(2):
            parts = []
            for k in range(per_tile):
                slot = at * CHUNK + unit * per_tile + k
                parts += [own_ref[slot, lanes, :], sib_ref[slot, lanes, :]]
            tile = jnp.concatenate([jnp.concatenate(parts, axis=0), zeros], axis=1)
            pltpu.matmul_push_rhs(tile, 0, unit, transpose=True)

    def stream(part, load):
        rows = read_rows(part)
        rows = jnp.concatenate([rows, rows], axis=1)
        for unit in range(2):
            pltpu.matmul_acc_lhs(units[part][unit], rows, 0 if load else None)

    def pop(part, step):
        group, at = where_of(step)
        best = jnp.maximum(pltpu.matmul_pop(units[part][0]), pltpu.matmul_pop(units[part][1]))
        acc[part][group] = jnp.maximum(jnp.where(at == 0, LOWEST, acc[part][group]), best)

    push(0)
    stream(0, True)
    push(1)
    pop(0, 0)
    stream(1, False)

    def body(step, _):
        stream(0, True)
        pop(1, step - 1)
        push(step + 1)
        stream(1, False)
        pop(0, step)
        return 0

    lax.fori_loop(1, last, body, 0)
    stream(0, True)
    pop(1, last - 1)
    stream(1, False)
    pop(0, last)
    pop(1, last)

    for part in range(2):
        lane = lax.broadcasted_iota(jnp.int32, (half, LANES), 1) < width
        first, second = [
            jnp.maximum(acc[part][g, :, :LANES], acc[part][g, :, LANES:]) for g in range(GROUPS)
        ]
        turned = pltpu.roll(jnp.where(lane, second, first), width, 1)
        best = jnp.maximum(jnp.where(lane, first, second), turned)
        partial = best.reshape(half // TOKENS, TOKENS // 8, 8, LANES).sum(axis=1)
        sums[part, :] = partial.reshape(half * 8 // TOKENS, LANES)
        total = sums[part, pl.ds(0, half // TOKENS, stride=8), :]
        for k in range(1, 8):
            total = total + sums[part, pl.ds(k, half // TOKENS, stride=8), :]
        write(part, total)


def score_kernel(pieces, counts_ref, *refs):
    if pieces:
        ids_ref, *refs = refs
    own_ref, sib_ref, blocks_ref, *refs = refs
    earlier, (out_ref, acc_0, acc_1, sums) = refs[:pieces], refs[pieces:]
    blocks, rows, dim = blocks_ref.shape
    step = min(blocks, BLOCKS)
    planes, store, _ = own_ref.shape
    per_core = store // GROUPS
    for k, ref in enumerate(earlier):
        for block in range(blocks):
            out_ref[ids_ref[k, block]] = ref[block]

    lane = lax.broadcasted_iota(jnp.int32, (16, LANES), 1)
    position = jnp.where(
        lane < store,
        own_ref[planes - 1, :16].astype(jnp.float32),
        sib_ref[planes - 1, :16].astype(jnp.float32) + per_core,
    ).astype(jnp.int32)[:8]

    def run(*units):
        def chunk(start):
            def read_rows(part):
                return blocks_ref[pl.ds(start + part * (step // 2), step // 2)].reshape(-1, dim)

            def write(part, total):
                count = rows // TOKENS
                for k in range(step // 2):
                    block = start + part * (step // 2) + k
                    picked = jnp.take_along_axis(
                        total[k * count : (k + 1) * count], position, axis=1
                    )
                    out_ref[ids_ref[pieces, block] if pieces else block] = picked

            score_block(
                own_ref, sib_ref, read_rows, (acc_0, acc_1), sums,
                ((units[0], units[1]), (units[2], units[3])), [counts_ref[0], counts_ref[1]], write,
            )

        if blocks == step:
            chunk(0)
        else:
            pl.loop(0, blocks, step=step)(chunk)

    half = step // 2 * rows
    pl.run_scoped(run, *[pltpu.ACC(unit)((half, 2 * LANES), jnp.float32) for unit in (0, 1, 0, 1)])


def score(counts, own, sib, blocks, ids=None, earlier=()):
    count = blocks.shape[0]
    step = min(count, BLOCKS)
    half = step // 2 * blocks.shape[1]
    local = blocks.shape[1] // TOKENS
    scalars = [counts] if ids is None else [counts, ids]
    operands = [own, sib, blocks, *earlier]
    return pl.pallas_call(
        functools.partial(score_kernel, len(earlier)),
        out_shape=jax.ShapeDtypeStruct(
            (count * (1 + len(earlier)), local, 2 * own.shape[1]), jnp.float32
        ),
        in_specs=[SMEM] * len(scalars) + [VMEM] * len(operands),
        out_specs=VMEM,
        scratch_shapes=[
            pltpu.VMEM((GROUPS, half, 2 * LANES), jnp.float32),
            pltpu.VMEM((GROUPS, half, 2 * LANES), jnp.float32),
            pltpu.VMEM((2, half * 8 // TOKENS, LANES), jnp.float32),
        ],
        compiler_params=pltpu.CompilerParams(vmem_limit_bytes=12 << 20),
        cost_estimate=pl.CostEstimate(
            flops=8 * blocks.size * own.shape[0] * own.shape[1],
            bytes_accessed=4 * own.size,
            transcendentals=0,
        ),
        name="score",
    )(*scalars, *operands)


def pick_kernel(core_ref, table_ref, shard_ref, local_ref, out_ref):
    chips, rows, width = table_ref.shape
    store = width // 2
    for half in range(shard_ref.shape[1] // LANES):
        lanes = slice(half * LANES, half * LANES + LANES)
        shard = shard_ref[:, lanes]
        chip = shard // 2
        lane = ((shard % 2) ^ core_ref[0]) * store + local_ref[:, lanes]
        total = jnp.zeros(lane.shape, jnp.float32)
        for k in range(chips):
            found = jnp.take_along_axis(table_ref[k], lane, axis=1)
            total = jnp.where(chip == k, found, total)
        out_ref[:, lanes] = total


def body(queries, cand_shard, cand_local, passages, lengths):
    me = lax.axis_index("psg").astype(jnp.int32)
    core = lax.axis_index("qry").reshape(1).astype(jnp.int32)
    chips = lax.axis_size("psg")
    local, qlen, dim = queries.shape

    def swap(a, bits):
        return lax.ppermute(a, "psg", [(i, i ^ bits) for i in range(chips)])

    rows = queries.reshape(1, local * qlen, dim)
    if chips == 16:
        others = [swap(rows, z) for z in (4, 8, 12)]
        column = jnp.concatenate([rows] + others, axis=0)
    else:
        column, bit = rows, 4
        while bit < chips:
            column = jnp.concatenate([column, swap(column, bit)], axis=0)
            bit *= 2
    own = prep(passages, lengths)
    sib = lax.ppermute(own, "qry", [(0, 1), (1, 0)])
    counts = chunk_counts(own, sib)
    ids = (jnp.arange(0, chips, 4)[None, :] ^ jnp.arange(4)[:, None]).astype(jnp.int32) ^ me
    beside = [column] + [swap(column, k) for k in (1, 2, 3)]
    pieces = [score(counts, own, sib, beside[k]) for k in range(3)]
    table = score(counts, own, sib, beside[3], ids, pieces)
    returned = lax.all_to_all(table, "psg", split_axis=0, concat_axis=0, tiled=True)
    return pl.pallas_call(
        pick_kernel,
        out_shape=jax.ShapeDtypeStruct(cand_local.shape, jnp.float32),
        in_specs=[SMEM, VMEM, VMEM, VMEM],
        out_specs=VMEM,
        compiler_params=pltpu.CompilerParams(vmem_limit_bytes=4 << 20),
        name="pick",
    )(core, returned, cand_shard[:, :, 0], cand_local)


def solution(mesh):
    in_specs = (
        P(("psg", "qry"), None, None),
        P(("psg", "qry"), None, None),
        P(("psg", "qry"), None),
        P(("psg", "qry"), None, None),
        P(("psg", "qry")),
    )
    out_specs = P(("psg", "qry"), None)
    return jax.shard_map(body, mesh=mesh, in_specs=in_specs, out_specs=out_specs, check_vma=False)
```

time: 60.6 us -> 55.1 us (0.909)
  Pallas kernels: 26.1 us -> 22.9 us
  other arithmetic: 2.63 us -> 0.18 us
    pallas_call x3 -> x5, Pallas kernels: 24.5 us -> 22.2 us  [the longest x4 21.7 us: score(): pl.pallas_call(functools.partial(score_kernel, len(earlier)), out_shape=j...]
    transpose x1 -> x0, other arithmetic: 1.87 us -> none  [body(): own = jnp.where(valid, passages, passages[:, :1]).transpose(1, 0, 2)]
    ppermute x7 -> x6, starting transfers between devices: 10.6 us -> 8.91 us  [swap(): return lax.ppermute(a, 'psg', [(i, i ^ bits) for i in range(chips)])]
    all_to_all x1, starting transfers between devices: 5.02 us -> 6.58 us  [body(): lax.all_to_all(table, 'psg', split_axis=0, concat_axis=0, tiled=True)]
    broadcast_in_dim x2 -> x0, local copies, waits for them, and re-layouts: 1.35 us -> none  [the longest x1 0.72 us: body(): own = jnp.where(valid, passages, passages[:, :1]).transpose(1, 0, 2)]
    pallas_call x1, Pallas kernels: 1.57 us -> 0.72 us  [body(): pl.pallas_call(pick_kernel, out_shape=jax.ShapeDtypeStruct(cand_local.sha...]
    another operation x0 -> x2, local copies, waits for them, and re-layouts: none -> 0.74 us  [prep(): jnp.tile(lengths, 2).reshape(1, 2 * store)]
    lt x1 -> x0, other arithmetic: 0.67 us -> none  [body(): valid = jnp.arange(plen)[None, :, None] < lengths[:, None, None]]
  transfers between devices with their start and end apart: 9 -> 8, of which waited for: 5 -> 3; matrix products, arithmetic and copies ran while one was open for 8% -> 0% of each run, Pallas kernels for 21% -> 29%
where the time goes in v2:
time: 55.1 us; the launch traced here: 54.8 us
  Pallas kernels  22.9 us (42%)
  starting transfers between devices  16 us (29%)
  waiting for transfers between devices  13.6 us (25%)
  local copies, waits for them, and re-layouts  2.07 us (4%)
    pallas_call x4, Pallas kernels, score(): pl.pallas_call(functools.partial(score_kernel, len(earlier)), out_shape=j...  21.7 us
    ppermute x6, starting transfers between devices, swap(): return lax.ppermute(a, 'psg', [(i, i ^ bits) for i in range(chips)])  8.91 us
    all_to_all x1, waiting for transfers between devices, body(): lax.all_to_all(table, 'psg', split_axis=0, concat_axis=0, tiled=True)  7.51 us
    all_to_all x1, starting transfers between devices, body(): lax.all_to_all(table, 'psg', split_axis=0, concat_axis=0, tiled=True)  6.58 us
    ppermute x6, waiting for transfers between devices, swap(): return lax.ppermute(a, 'psg', [(i, i ^ bits) for i in range(chips)])  6.08 us
    unnamed x9, local copies, waits for them, and re-layouts  1.27 us
  transfers between devices with their start and end apart: 8, of which 3 were waited for; matrix products, arithmetic and copies ran while one was open for 0% of the time, Pallas kernels for 29%

profile of v2, /device:TPU:0, one launch (start us, length us, event | category | flops | bytes accessed | tf_op | source)
XLA Modules:
  0.0 54.8 jit_solution(3131367367426264292)
XLA Ops:
  0.0 0.7 %tile.2 = s32[2,64]{1,0:T(2,128)S(1)} broadcast(s32[64]{0:T(128)} %param.9), dimensions={1} | broadcast | bytes 768 | tf_op jit(solution)/shard_map/tile | solution.py:65
  0.7 0.1 reshape_tile.3.lengths_ref
  0.7 0.0 copy-start
  0.7 1.3 %copy-done = bf16[64,70,128]{2,0,1:T(8,128)(2,1)S(1)} copy-done((bf16[64,70,128]{2,0,1:T(8,128)(2,1)S(1)}, bf16[64,70,128]{2,0,1:T(8,128)(2,1)}, u32[]{:S(2)}) %copy-start) | copy-done | bytes 1146904
  2.0 0.0 copy-start.2
  2.0 0.6 %prep.1.refs_0_.refs_1_ = bf16[74,64,128]{2,1,0:T(8,128)(2,1)S(1)} custom-call(s32[1,128]{1,0:T(1,128)S(1)} %reshape_tile.3.lengths_ref, bf16[70,64,128]{2,1,0:T(8,128)(2,1)S(1)} %bitcast.6), custom_call_target="tpu_custom_call" | custom-call | tf_op jit(solution)/shard_map/prep/pallas_call | solution.py:58
  2.6 0.5 collective-permute-start
  3.1 0.0 copy-done.2
  3.1 2.8 %collective-permute-start.1 = (bf16[1,256,128]{2,1,0:T(8,128)(2,1)S(1)}, bf16[1,256,128]{2,1,0:T(8,128)(2,1)S(1)}, u32[]{:S(2)}, u32[]{:S(2)}) collective-permute-start(bf16[1,256,128]{2,1,0:T(8,128)(2,1)S(1)} %bitcast.8), channel_id=1, source_target_pairs={{0,8},{2,10},{4,12},{6,14},{8,0},{10,2},{12,4},{14,6},{16,24},{18,... | collective-permute-start | bytes 196616 | tf_op jit(solution)/shard_map/ppermute | solution.py:243
  5.9 2.6 %collective-permute-start.2 = (bf16[1,256,128]{2,1,0:T(8,128)(2,1)S(1)}, bf16[1,256,128]{2,1,0:T(8,128)(2,1)S(1)}, u32[]{:S(2)}, u32[]{:S(2)}) collective-permute-start(bf16[1,256,128]{2,1,0:T(8,128)(2,1)S(1)} %bitcast.9), channel_id=1, source_target_pairs={{0,16},{2,18},{4,20},{6,22},{8,24},{10,26},{12,28},{14,30},{16,0},... | collective-permute-start | bytes 196616 | tf_op jit(solution)/shard_map/ppermute | solution.py:243
  8.5 0.0 collective-permute-start.3
  8.5 0.0 collective-permute-done.1
  8.5 5.0 %collective-permute-done.2 = bf16[1,256,128]{2,1,0:T(8,128)(2,1)S(1)} collective-permute-done((bf16[1,256,128]{2,1,0:T(8,128)(2,1)S(1)}, bf16[1,256,128]{2,1,0:T(8,128)(2,1)S(1)}, u32[]{:S(2)}, u32[]{:S(2)}) %collective-permute-start.2) | collective-permute-done | bytes 65568 | tf_op jit(solution)/shard_map/ppermute | solution.py:243
  13.5 1.1 %collective-permute-done.3 = bf16[1,256,128]{2,1,0:T(8,128)(2,1)S(1)} collective-permute-done((bf16[1,256,128]{2,1,0:T(8,128)(2,1)S(1)}, bf16[1,256,128]{2,1,0:T(8,128)(2,1)S(1)}, u32[]{:S(2)}, u32[]{:S(2)}) %collective-permute-start.3) | collective-permute-done | bytes 65568 | tf_op jit(solution)/shard_map/ppermute | solution.py:243
  14.6 1.6 %collective-permute-start.6 = (bf16[4,256,128]{2,1,0:T(8,128)(2,1)S(1)}, bf16[4,256,128]{2,1,0:T(8,128)(2,1)S(1)}, u32[]{:S(2)}, u32[]{:S(2)}) collective-permute-start(bf16[4,256,128]{2,1,0:T(8,128)(2,1)S(1)} %pad_maximum_fusion.refs_2_), channel_id=1, source_target_pairs={{0,4},{2,6},{4,0},{6,2},{8,12},{10,14},{12,8},{14,10},{16,20},{18,... | collective-permute-start | bytes 786440 | tf_op jit(solution)/shard_map/ppermute | solution.py:243
  16.2 1.5 %collective-permute-start.5 = (bf16[4,256,128]{2,1,0:T(8,128)(2,1)S(1)}, bf16[4,256,128]{2,1,0:T(8,128)(2,1)S(1)}, u32[]{:S(2)}, u32[]{:S(2)}) collective-permute-start(bf16[4,256,128]{2,1,0:T(8,128)(2,1)S(1)} %pad_maximum_fusion.refs_2_), channel_id=1, source_target_pairs={{0,2},{2,0},{4,6},{6,4},{8,10},{10,8},{12,14},{14,12},{16,18},{18,... | collective-permute-start | bytes 786440 | tf_op jit(solution)/shard_map/ppermute | solution.py:243
  17.7 0.5 collective-permute-start.4
  18.2 0.0 collective-permute-done.refs_1_.refs_2_
  18.2 0.1 add_reduce_fusion
  18.3 5.2 %score.4.refs_4_ = f32[4,8,128]{2,1,0:T(8,128)S(1)} custom-call(s32[2]{0:T(128)S(1)} %and_select_fusion.counts_ref, bf16[74,64,128]{2,1,0:T(8,128)(2,1)S(1)} %prep.1.refs_0_.refs_1_, bf16[74,64,128]{2,1,0:T(8,128)(2,1)S(1)} %collective-permute-done.refs_1_.refs_2_, bf16[4,256,128]{2,1,0:T(8,128)(2,1)S(1)} %pad_maximum_fusion.refs_2_), custom_call_target="tpu_custom_call" | custom-call | flops 4966055936 | bytes 2424832 | tf_op jit(solution)/shard_map/score/pallas_call | solution.py:199
  23.6 0.0 collective-permute-done.6.refs_2_
  23.6 5.2 %score.6.refs_6_ = f32[4,8,128]{2,1,0:T(8,128)S(1)} custom-call(s32[2]{0:T(128)S(1)} %and_select_fusion.counts_ref, bf16[74,64,128]{2,1,0:T(8,128)(2,1)S(1)} %prep.1.refs_0_.refs_1_, bf16[74,64,128]{2,1,0:T(8,128)(2,1)S(1)} %collective-permute-done.refs_1_.refs_2_, bf16[4,256,128]{2,1,0:T(8,128)(2,1)S(1)} %collective-permute-done.6.refs_2_), custom_call_target="tpu_custom_call" | custom-call | flops 4966055936 | bytes 2424832 | tf_op jit(solution)/shard_map/score/pallas_call | solution.py:199
  28.8 0.0 collective-permute-done.5.refs_2_
  28.8 5.3 %score.5.refs_5_ = f32[4,8,128]{2,1,0:T(8,128)S(1)} custom-call(s32[2]{0:T(128)S(1)} %and_select_fusion.counts_ref, bf16[74,64,128]{2,1,0:T(8,128)(2,1)S(1)} %prep.1.refs_0_.refs_1_, bf16[74,64,128]{2,1,0:T(8,128)(2,1)S(1)} %collective-permute-done.refs_1_.refs_2_, bf16[4,256,128]{2,1,0:T(8,128)(2,1)S(1)} %collective-permute-done.5.refs_2_), custom_call_target="tpu_custom_call" | custom-call | flops 4966055936 | bytes 2424832 | tf_op jit(solution)/shard_map/score/pallas_call | solution.py:199
  34.1 0.0 copy-start.3
  34.1 0.0 copy-start.1
  34.1 0.0 collective-permute-done.4.refs_3_
  34.1 5.9 %score.7 = f32[16,8,128]{2,1,0:T(8,128)} custom-call(s32[2]{0:T(128)S(1)} %and_select_fusion.counts_ref, s32[4,4]{1,0:T(4,128)S(1)} %xor_xor_fusion.refs_0_, bf16[74,64,128]{2,1,0:T(8,128)(2,1)S(1)} %prep.1.refs_0_.refs_1_, bf16[74,64,128]{2,1,0:T(8,128)(2,1)S(1)} %collective-permute-done.refs_1_.refs_2_, ...), custom_call_target="tpu_custom_call" | custom-call | flops 4966055936 | bytes 2424832 | tf_op jit(solution)/shard_map/score/pallas_call | solution.py:199
  40.0 6.6 %all-to-all-start = ((f32[16,8,128]{2,1,0:T(8,128)}), f32[16,8,128]{2,1,0:T(8,128)S(1)}, u32[]{:S(2)}, u32[]{:S(2)}) async-start(f32[16,8,128]{2,1,0:T(8,128)} %score.7), calls=%async_computation | async-start | bytes 131072 | tf_op jit(solution)/shard_map/all_to_all | solution.py:261
  46.6 0.0 copy-done.3
  46.6 7.5 %all-to-all-done.table_ref = f32[16,8,128]{2,1,0:T(8,128)S(1)} async-done(((f32[16,8,128]{2,1,0:T(8,128)}), f32[16,8,128]{2,1,0:T(8,128)S(1)}, u32[]{:S(2)}, u32[]{:S(2)}) %all-to-all-start) | async-done | bytes 65568 | tf_op jit(solution)/shard_map/all_to_all | solution.py:261
  54.1 0.0 copy-done.1
  54.1 0.7 %pick.1 = f32[8,256]{1,0:T(8,128)} custom-call(s32[1]{0:T(128)} %bitcast.core_ref, f32[16,8,128]{2,1,0:T(8,128)S(1)} %all-to-all-done.table_ref, s32[8,256]{1,0:T(8,128)S(1)} %bitcast.7, s32[8,256]{1,0:T(8,128)S(1)} %copy-done.1), custom_call_target="tpu_custom_call" | custom-call | tf_op jit(solution)/shard_map/pick/pallas_call | solution.py:262
  (7 shorter events, 0.1 us)
Async XLA Ops:
  0.7 1.3 %copy-start = (bf16[64,70,128]{2,0,1:T(8,128)(2,1)S(1)}, bf16[64,70,128]{2,0,1:T(8,128)(2,1)}, u32[]{:S(2)}) copy-start(bf16[64,70,128]{2,0,1:T(8,128)(2,1)} %param.8) | copy-start | bytes 3440644
  2.0 1.1 %copy-start.2 = (bf16[8,32,128]{2,1,0:T(8,128)(2,1)S(1)}, bf16[8,32,128]{2,1,0:T(8,128)(2,1)}, u32[]{:S(2)}) copy-start(bf16[8,32,128]{2,1,0:T(8,128)(2,1)} %param.5) | copy-start | bytes 196612
  2.6 15.6 %collective-permute-start = (bf16[74,64,128]{2,1,0:T(8,128)(2,1)S(1)}, bf16[74,64,128]{2,1,0:T(8,128)(2,1)S(1)}, u32[]{:S(2)}, u32[]{:S(2)}) collective-permute-start(bf16[74,64,128]{2,1,0:T(8,128)(2,1)S(1)} %prep.1.refs_0_.refs_1_), channel_id=1, source_target_pairs={{0,1},{1,0},{2,3},{3,2},{4,5},{5,4},{6,7},{7,6},{8,9},{9,8},{10,11... | collective-permute-start | bytes 3637256 | tf_op jit(solution)/shard_map/ppermute | solution.py:255
  3.1 5.4 %collective-permute-start.1 = (bf16[1,256,128]{2,1,0:T(8,128)(2,1)S(1)}, bf16[1,256,128]{2,1,0:T(8,128)(2,1)S(1)}, u32[]{:S(2)}, u32[]{:S(2)}) collective-permute-start(bf16[1,256,128]{2,1,0:T(8,128)(2,1)S(1)} %bitcast.8), channel_id=1, source_target_pairs={{0,8},{2,10},{4,12},{6,14},{8,0},{10,2},{12,4},{14,6},{16,24},{18,... | collective-permute-start | bytes 196616 | tf_op jit(solution)/shard_map/ppermute | solution.py:243
  5.9 7.6 %collective-permute-start.2 = (bf16[1,256,128]{2,1,0:T(8,128)(2,1)S(1)}, bf16[1,256,128]{2,1,0:T(8,128)(2,1)S(1)}, u32[]{:S(2)}, u32[]{:S(2)}) collective-permute-start(bf16[1,256,128]{2,1,0:T(8,128)(2,1)S(1)} %bitcast.9), channel_id=1, source_target_pairs={{0,16},{2,18},{4,20},{6,22},{8,24},{10,26},{12,28},{14,30},{16,0},... | collective-permute-start | bytes 196616 | tf_op jit(solution)/shard_map/ppermute | solution.py:243
  8.5 6.1 %collective-permute-start.3 = (bf16[1,256,128]{2,1,0:T(8,128)(2,1)S(1)}, bf16[1,256,128]{2,1,0:T(8,128)(2,1)S(1)}, u32[]{:S(2)}, u32[]{:S(2)}) collective-permute-start(bf16[1,256,128]{2,1,0:T(8,128)(2,1)S(1)} %bitcast.10), channel_id=1, source_target_pairs={{0,24},{2,26},{4,28},{6,30},{8,16},{10,18},{12,20},{14,22},{16,8},... | collective-permute-start | bytes 196616 | tf_op jit(solution)/shard_map/ppermute | solution.py:243
  14.6 9.0 %collective-permute-start.6 = (bf16[4,256,128]{2,1,0:T(8,128)(2,1)S(1)}, bf16[4,256,128]{2,1,0:T(8,128)(2,1)S(1)}, u32[]{:S(2)}, u32[]{:S(2)}) collective-permute-start(bf16[4,256,128]{2,1,0:T(8,128)(2,1)S(1)} %pad_maximum_fusion.refs_2_), channel_id=1, source_target_pairs={{0,4},{2,6},{4,0},{6,2},{8,12},{10,14},{12,8},{14,10},{16,20},{18,... | collective-permute-start | bytes 786440 | tf_op jit(solution)/shard_map/ppermute | solution.py:243
  16.2 12.6 %collective-permute-start.5 = (bf16[4,256,128]{2,1,0:T(8,128)(2,1)S(1)}, bf16[4,256,128]{2,1,0:T(8,128)(2,1)S(1)}, u32[]{:S(2)}, u32[]{:S(2)}) collective-permute-start(bf16[4,256,128]{2,1,0:T(8,128)(2,1)S(1)} %pad_maximum_fusion.refs_2_), channel_id=1, source_target_pairs={{0,2},{2,0},{4,6},{6,4},{8,10},{10,8},{12,14},{14,12},{16,18},{18,... | collective-permute-start | bytes 786440 | tf_op jit(solution)/shard_map/ppermute | solution.py:243
  17.7 16.4 %collective-permute-start.4 = (bf16[4,256,128]{2,1,0:T(8,128)(2,1)S(1)}, bf16[4,256,128]{2,1,0:T(8,128)(2,1)S(1)}, u32[]{:S(2)}, u32[]{:S(2)}) collective-permute-start(bf16[4,256,128]{2,1,0:T(8,128)(2,1)S(1)} %pad_maximum_fusion.refs_2_), channel_id=1, source_target_pairs={{0,6},{2,4},{4,2},{6,0},{8,14},{10,12},{12,10},{14,8},{16,22},{18,... | collective-permute-start | bytes 786440 | tf_op jit(solution)/shard_map/ppermute | solution.py:243
  34.1 12.5 %copy-start.3 = (s32[8,256,1]{1,2,0:T(1,128)S(1)}, s32[8,256,1]{1,2,0:T(1,128)}, u32[]{:S(2)}) copy-start(s32[8,256,1]{1,2,0:T(1,128)} %param.6) | copy-start | bytes 24580
  34.1 20.0 %copy-start.1 = (s32[8,256]{1,0:T(8,128)S(1)}, s32[8,256]{1,0:T(8,128)}, u32[]{:S(2)}) copy-start(s32[8,256]{1,0:T(8,128)} %local_ref.1) | copy-start | bytes 24580
  40.0 14.1 %all-to-all-start = ((f32[16,8,128]{2,1,0:T(8,128)}), f32[16,8,128]{2,1,0:T(8,128)S(1)}, u32[]{:S(2)}, u32[]{:S(2)}) async-start(f32[16,8,128]{2,1,0:T(8,128)} %score.7), calls=%async_computation | async-start | bytes 131072 | tf_op jit(solution)/shard_map/all_to_all | solution.py:261

commit v3 on v2

--- a/solution.py
+++ b/solution.py
@@ -14,15 +14,22 @@
 GROUPS = 2
 CHUNK = 8
 LANES = 128
+ROWS = 128
 LOWEST = -1e30
 
 
-def prep_kernel(lengths_ref, passages_ref, out_ref):
+def prep_kernel(counts_ref, store_ref, out_ref, lengths_ref, passages_ref, arrived):
+    load_lengths = pltpu.make_async_copy(counts_ref, lengths_ref, arrived.at[0])
+    load_store = pltpu.make_async_copy(store_ref, passages_ref, arrived.at[1])
+    load_lengths.start()
+    load_store.start()
+    load_lengths.wait()
     slots, store, dim = passages_ref.shape
     padded = out_ref.shape[0] - 2
     per_core = store // GROUPS
     shape = (store, 2 * store)
-    along = jnp.broadcast_to(lengths_ref[...], shape)
+    lengths = lengths_ref[...]
+    along = jnp.broadcast_to(jnp.concatenate([lengths, lengths], axis=1), shape)
     row = lax.broadcasted_iota(jnp.int32, shape, 0)
     lane = lax.broadcasted_iota(jnp.int32, shape, 1)
     lane = jnp.where(lane >= store, lane - store, lane)
@@ -37,6 +44,7 @@
     target = rank + jnp.where(lane >= store, store, 0)
     order = (target == row).astype(jnp.float32).astype(passages_ref.dtype)
 
+    load_store.wait()
     first = None
     for t in range(0, slots, 2):
         pair = passages_ref[t : t + 2].reshape(2 * store, dim)
@@ -58,11 +66,22 @@
     return pl.pallas_call(
         prep_kernel,
         out_shape=jax.ShapeDtypeStruct((padded + 2, store, dim), passages.dtype),
-        in_specs=[VMEM, VMEM],
+        in_specs=[pl.BlockSpec(memory_space=pl.ANY)] * 2,
         out_specs=VMEM,
+        scratch_shapes=[
+            pltpu.VMEM((1, store), jnp.int32),
+            pltpu.VMEM((slots, store, dim), passages.dtype),
+            pltpu.SemaphoreType.DMA((2,)),
+        ],
         compiler_params=pltpu.CompilerParams(vmem_limit_bytes=12 << 20),
+        cost_estimate=pl.CostEstimate(
+            flops=64 * passages.size * store, bytes_accessed=4 * passages.size, transcendentals=0
+        ),
         name="prep",
-    )(jnp.tile(lengths, 2).reshape(1, 2 * store), passages.transpose(1, 0, 2))
+    )(
+        pltpu.with_memory_space_constraint(lengths.reshape(1, store), pltpu.HBM),
+        pltpu.with_memory_space_constraint(passages.transpose(1, 0, 2), pltpu.HBM),
+    )
 
 
 def chunk_counts(own, sib):
@@ -119,98 +138,110 @@
         pop(0, step)
         return 0
 
+    def finish(part):
+        _, at = where_of(last)
+        fresh = [pltpu.matmul_pop(unit) for unit in units[part]]
+        for start in range(0, half, ROWS):
+            take = slice(start, start + ROWS)
+            best = jnp.maximum(fresh[0][take], fresh[1][take])
+            best = jnp.maximum(jnp.where(at == 0, LOWEST, acc[part][GROUPS - 1, take]), best)
+            first = acc[part][0, take]
+            first = jnp.maximum(first[:, :LANES], first[:, LANES:])
+            second = jnp.maximum(best[:, :LANES], best[:, LANES:])
+            lane = lax.broadcasted_iota(jnp.int32, first.shape, 1) < width
+            turned = pltpu.roll(jnp.where(lane, second, first), width, 1)
+            best = jnp.maximum(jnp.where(lane, first, second), turned)
+            partial = best.reshape(ROWS // TOKENS, TOKENS // 8, 8, LANES).sum(axis=1)
+            spot = start * 8 // TOKENS
+            sums[part, spot : spot + ROWS * 8 // TOKENS] = partial.reshape(-1, LANES)
+        total = sums[part, pl.ds(0, half // TOKENS, stride=8), :]
+        for k in range(1, 8):
+            total = total + sums[part, pl.ds(k, half // TOKENS, stride=8), :]
+        write(part, total)
+
     lax.fori_loop(1, last, body, 0)
     stream(0, True)
     pop(1, last - 1)
     stream(1, False)
-    pop(0, last)
-    pop(1, last)
-
-    for part in range(2):
-        lane = lax.broadcasted_iota(jnp.int32, (half, LANES), 1) < width
-        first, second = [
-            jnp.maximum(acc[part][g, :, :LANES], acc[part][g, :, LANES:]) for g in range(GROUPS)
-        ]
-        turned = pltpu.roll(jnp.where(lane, second, first), width, 1)
-        best = jnp.maximum(jnp.where(lane, first, second), turned)
-        partial = best.reshape(half // TOKENS, TOKENS // 8, 8, LANES).sum(axis=1)
-        sums[part, :] = partial.reshape(half * 8 // TOKENS, LANES)
-        total = sums[part, pl.ds(0, half // TOKENS, stride=8), :]
-        for k in range(1, 8):
-            total = total + sums[part, pl.ds(k, half // TOKENS, stride=8), :]
-        write(part, total)
-
-
-def score_kernel(pieces, counts_ref, *refs):
-    if pieces:
+    finish(0)
+    finish(1)
+
+
+def score_kernel(first, earlier, counts_ref, *refs):
+    if earlier:
         ids_ref, *refs = refs
     own_ref, sib_ref, blocks_ref, *refs = refs
-    earlier, (out_ref, acc_0, acc_1, sums) = refs[:pieces], refs[pieces:]
+    pieces, (out_ref, acc_0, acc_1, sums, scores) = refs[:earlier], refs[earlier:]
     blocks, rows, dim = blocks_ref.shape
-    step = min(blocks, BLOCKS)
+    step = min(blocks - first, BLOCKS)
+    local = rows // TOKENS
+    half = step * rows // 2
     planes, store, _ = own_ref.shape
     per_core = store // GROUPS
-    for k, ref in enumerate(earlier):
-        for block in range(blocks):
-            out_ref[ids_ref[k, block]] = ref[block]
+    flat_ref = blocks_ref.reshape(blocks * rows, dim)
+    at = 0
+    for piece in pieces:
+        for block in range(piece.shape[0]):
+            out_ref[ids_ref[at]] = piece[block]
+            at += 1
 
     lane = lax.broadcasted_iota(jnp.int32, (16, LANES), 1)
     position = jnp.where(
         lane < store,
         own_ref[planes - 1, :16].astype(jnp.float32),
         sib_ref[planes - 1, :16].astype(jnp.float32) + per_core,
-    ).astype(jnp.int32)[:8]
+    ).astype(jnp.int32)[:1]
 
     def run(*units):
         def chunk(start):
             def read_rows(part):
-                return blocks_ref[pl.ds(start + part * (step // 2), step // 2)].reshape(-1, dim)
+                return flat_ref[pl.ds((first + start) * rows + part * half, half)]
 
             def write(part, total):
-                count = rows // TOKENS
-                for k in range(step // 2):
-                    block = start + part * (step // 2) + k
-                    picked = jnp.take_along_axis(
-                        total[k * count : (k + 1) * count], position, axis=1
-                    )
-                    out_ref[ids_ref[pieces, block] if pieces else block] = picked
+                count = half // TOKENS
+                index = jnp.broadcast_to(position, (count, LANES))
+                scores[part * count : (part + 1) * count] = jnp.take_along_axis(
+                    total, index, axis=1
+                )
 
             score_block(
                 own_ref, sib_ref, read_rows, (acc_0, acc_1), sums,
                 ((units[0], units[1]), (units[2], units[3])), [counts_ref[0], counts_ref[1]], write,
             )
-
-        if blocks == step:
+            for block in range(step):
+                spot = ids_ref[at + start + block] if earlier else start + block
+                out_ref[spot] = scores[block * local : (block + 1) * local]
+
+        if blocks - first == step:
             chunk(0)
         else:
-            pl.loop(0, blocks, step=step)(chunk)
-
-    half = step // 2 * rows
+            pl.loop(0, blocks - first, step=step)(chunk)
+
     pl.run_scoped(run, *[pltpu.ACC(unit)((half, 2 * LANES), jnp.float32) for unit in (0, 1, 0, 1)])
 
 
-def score(counts, own, sib, blocks, ids=None, earlier=()):
-    count = blocks.shape[0]
+def score(counts, own, sib, blocks, first=0, ids=None, earlier=()):
+    count = blocks.shape[0] - first
     step = min(count, BLOCKS)
-    half = step // 2 * blocks.shape[1]
+    half = step * blocks.shape[1] // 2
     local = blocks.shape[1] // TOKENS
     scalars = [counts] if ids is None else [counts, ids]
     operands = [own, sib, blocks, *earlier]
+    total = count + sum(piece.shape[0] for piece in earlier)
     return pl.pallas_call(
-        functools.partial(score_kernel, len(earlier)),
-        out_shape=jax.ShapeDtypeStruct(
-            (count * (1 + len(earlier)), local, 2 * own.shape[1]), jnp.float32
-        ),
+        functools.partial(score_kernel, first, len(earlier)),
+        out_shape=jax.ShapeDtypeStruct((total, local, 2 * own.shape[1]), jnp.float32),
         in_specs=[SMEM] * len(scalars) + [VMEM] * len(operands),
         out_specs=VMEM,
         scratch_shapes=[
             pltpu.VMEM((GROUPS, half, 2 * LANES), jnp.float32),
             pltpu.VMEM((GROUPS, half, 2 * LANES), jnp.float32),
             pltpu.VMEM((2, half * 8 // TOKENS, LANES), jnp.float32),
+            pltpu.VMEM((step * local, LANES), jnp.float32),
         ],
         compiler_params=pltpu.CompilerParams(vmem_limit_bytes=12 << 20),
         cost_estimate=pl.CostEstimate(
-            flops=8 * blocks.size * own.shape[0] * own.shape[1],
+            flops=8 * count * blocks[0].size * own.shape[0] * own.shape[1],
             bytes_accessed=4 * own.size,
             transcendentals=0,
         ),
@@ -242,22 +273,24 @@
     def swap(a, bits):
         return lax.ppermute(a, "psg", [(i, i ^ bits) for i in range(chips)])
 
+    own = prep(passages, lengths)
     rows = queries.reshape(1, local * qlen, dim)
     if chips == 16:
         others = [swap(rows, z) for z in (4, 8, 12)]
+        own, *others = lax.optimization_barrier((own, *others))
         column = jnp.concatenate([rows] + others, axis=0)
     else:
         column, bit = rows, 4
         while bit < chips:
             column = jnp.concatenate([column, swap(column, bit)], axis=0)
             bit *= 2
-    own = prep(passages, lengths)
     sib = lax.ppermute(own, "qry", [(0, 1), (1, 0)])
     counts = chunk_counts(own, sib)
     ids = (jnp.arange(0, chips, 4)[None, :] ^ jnp.arange(4)[:, None]).astype(jnp.int32) ^ me
     beside = [column] + [swap(column, k) for k in (1, 2, 3)]
-    pieces = [score(counts, own, sib, beside[k]) for k in range(3)]
-    table = score(counts, own, sib, beside[3], ids, pieces)
+    pieces = [score(counts, own, sib, column)]
+    pieces += [score(counts, own, sib, beside[k]) for k in (1, 2)]
+    table = score(counts, own, sib, beside[3], ids=ids.reshape(-1), earlier=pieces)
     returned = lax.all_to_all(table, "psg", split_axis=0, concat_axis=0, tiled=True)
     return pl.pallas_call(
         pick_kernel,

time: 55.1 us -> 50.1 us (0.909)
  starting transfers between devices: 16 us -> 14 us
  local copies, waits for them, and re-layouts: 2.07 us -> 0.16 us
  waiting for transfers between devices: 13.6 us -> 12.1 us
    all_to_all x1, starting transfers between devices: 6.58 us -> 4.82 us  [body(): lax.all_to_all(table, 'psg', split_axis=0, concat_axis=0, tiled=True)]
    ppermute x6, waiting for transfers between devices: 6.08 us -> 4.57 us  [swap(): return lax.ppermute(a, 'psg', [(i, i ^ bits) for i in range(chips)])]
    unnamed x9 -> x7, local copies, waits for them, and re-layouts: 1.27 us -> 0.01 us
    pallas_call x1, Pallas kernels: 0.57 us -> 1.78 us  [prep(): pl.pallas_call(prep_kernel, out_shape=jax.ShapeDtypeStruct((padded + 2, s...]
    pallas_call x4, Pallas kernels: 21.7 us -> 20.8 us  [score(): pl.pallas_call(functools.partial(score_kernel, first, len(earlier)), out_...]
    another operation x2 -> x0, local copies, waits for them, and re-layouts: 0.74 us -> none  [prep(): jnp.tile(lengths, 2).reshape(1, 2 * store)]
  transfers between devices with their start and end apart: 8 -> 8, of which waited for: 3 -> 4; matrix products, arithmetic and copies ran while one was open for 0% -> 1% of each run, Pallas kernels for 29% -> 34%
where the time goes in v3:
time: 50.1 us; the launch traced here: 49.8 us
  Pallas kernels  23.3 us (47%)
  starting transfers between devices  14 us (28%)
  waiting for transfers between devices  12.1 us (24%)
    pallas_call x4, Pallas kernels, score(): pl.pallas_call(functools.partial(score_kernel, first, len(earlier)), out_...  20.8 us
    ppermute x6, starting transfers between devices, swap(): return lax.ppermute(a, 'psg', [(i, i ^ bits) for i in range(chips)])  9.17 us
    all_to_all x1, waiting for transfers between devices, body(): lax.all_to_all(table, 'psg', split_axis=0, concat_axis=0, tiled=True)  7.51 us
    all_to_all x1, starting transfers between devices, body(): lax.all_to_all(table, 'psg', split_axis=0, concat_axis=0, tiled=True)  4.82 us
    ppermute x6, waiting for transfers between devices, swap(): return lax.ppermute(a, 'psg', [(i, i ^ bits) for i in range(chips)])  4.57 us
    pallas_call x1, Pallas kernels, prep(): pl.pallas_call(prep_kernel, out_shape=jax.ShapeDtypeStruct((padded + 2, s...  1.78 us
  transfers between devices with their start and end apart: 8, of which 4 were waited for; matrix products, arithmetic and copies ran while one was open for 1% of the time, Pallas kernels for 34%

profile of v3, /device:TPU:0, one launch (start us, length us, event | category | flops | bytes accessed | tf_op | source)
XLA Modules:
  0.0 49.8 jit_solution(11207051615424526212)
XLA Ops:
  0.0 3.0 %collective-permute-start = (bf16[1,256,128]{2,1,0:T(8,128)(2,1)}, bf16[1,256,128]{2,1,0:T(8,128)(2,1)S(1)}, u32[]{:S(2)}, u32[]{:S(2)}) collective-permute-start(bf16[1,256,128]{2,1,0:T(8,128)(2,1)} %bitcast.8), channel_id=1, source_target_pairs={{0,8},{2,10},{4,12},{6,14},{8,0},{10,2},{12,4},{14,6},{16,24},{18,... | collective-permute-start | bytes 196616 | tf_op jit(solution)/shard_map/ppermute | solution.py:274
  3.0 2.6 %collective-permute-start.1 = (bf16[1,256,128]{2,1,0:T(8,128)(2,1)}, bf16[1,256,128]{2,1,0:T(8,128)(2,1)S(1)}, u32[]{:S(2)}, u32[]{:S(2)}) collective-permute-start(bf16[1,256,128]{2,1,0:T(8,128)(2,1)} %bitcast.9), channel_id=1, source_target_pairs={{0,16},{2,18},{4,20},{6,22},{8,24},{10,26},{12,28},{14,30},{16,0},... | collective-permute-start | bytes 196616 | tf_op jit(solution)/shard_map/ppermute | solution.py:274
  5.6 0.0 collective-permute-start.2
  5.6 0.0 copy-start.1
  5.6 1.8 %prep.1.refs_0_.refs_1_ = bf16[74,64,128]{2,1,0:T(8,128)(2,1)S(1)} custom-call(s32[1,64]{1,0:T(1,128)} %bitcast.13, bf16[70,64,128]{2,1,0:T(8,128)(2,1)} %bitcast.12), custom_call_target="tpu_custom_call" | custom-call | flops 2348810240 | bytes 2293760 | tf_op jit(solution)/shard_map/prep/pallas_call | solution.py:66
  7.4 0.0 collective-permute-done
  7.4 3.1 %collective-permute-done.1 = bf16[1,256,128]{2,1,0:T(8,128)(2,1)S(1)} collective-permute-done((bf16[1,256,128]{2,1,0:T(8,128)(2,1)}, bf16[1,256,128]{2,1,0:T(8,128)(2,1)S(1)}, u32[]{:S(2)}, u32[]{:S(2)}) %collective-permute-start.1) | collective-permute-done | bytes 65568 | tf_op jit(solution)/shard_map/ppermute | solution.py:274
  10.5 1.4 %collective-permute-done.2 = bf16[1,256,128]{2,1,0:T(8,128)(2,1)S(1)} collective-permute-done((bf16[1,256,128]{2,1,0:T(8,128)(2,1)}, bf16[1,256,128]{2,1,0:T(8,128)(2,1)S(1)}, u32[]{:S(2)}, u32[]{:S(2)}) %collective-permute-start.2) | collective-permute-done | bytes 65568 | tf_op jit(solution)/shard_map/ppermute | solution.py:274
  11.9 0.0 collective-permute-start.3
  11.9 0.1 xor.30.refs_0_
  12.0 0.0 copy-done.1
  12.1 1.6 %collective-permute-start.6 = (bf16[4,256,128]{2,1,0:T(8,128)(2,1)S(1)}, bf16[4,256,128]{2,1,0:T(8,128)(2,1)S(1)}, u32[]{:S(2)}, u32[]{:S(2)}) collective-permute-start(bf16[4,256,128]{2,1,0:T(8,128)(2,1)S(1)} %pad_maximum_fusion.refs_2_), channel_id=1, source_target_pairs={{0,4},{2,6},{4,0},{6,2},{8,12},{10,14},{12,8},{14,10},{16,20},{18,... | collective-permute-start | bytes 786440 | tf_op jit(solution)/shard_map/ppermute | solution.py:274
  13.7 1.5 %collective-permute-start.5 = (bf16[4,256,128]{2,1,0:T(8,128)(2,1)S(1)}, bf16[4,256,128]{2,1,0:T(8,128)(2,1)S(1)}, u32[]{:S(2)}, u32[]{:S(2)}) collective-permute-start(bf16[4,256,128]{2,1,0:T(8,128)(2,1)S(1)} %pad_maximum_fusion.refs_2_), channel_id=1, source_target_pairs={{0,2},{2,0},{4,6},{6,4},{8,10},{10,8},{12,14},{14,12},{16,18},{18,... | collective-permute-start | bytes 786440 | tf_op jit(solution)/shard_map/ppermute | solution.py:274
  15.2 0.5 collective-permute-start.4
  15.6 0.0 collective-permute-done.3.refs_1_.refs_2_
  15.7 0.1 add_reduce_fusion
  15.8 5.0 %score.4.refs_4_ = f32[4,8,128]{2,1,0:T(8,128)S(1)} custom-call(s32[2]{0:T(128)S(1)} %and_select_fusion.counts_ref, bf16[74,64,128]{2,1,0:T(8,128)(2,1)S(1)} %prep.1.refs_0_.refs_1_, bf16[74,64,128]{2,1,0:T(8,128)(2,1)S(1)} %collective-permute-done.3.refs_1_.refs_2_, bf16[4,256,128]{2,1,0:T(8,128)(2,1)S(1)} %pad_maximum_fusion.refs_2_), custom_call_target="tpu_custom_call" | custom-call | flops 4966055936 | bytes 2424832 | tf_op jit(solution)/shard_map/score/pallas_call | solution.py:231
  20.8 0.1 collective-permute-done.6.refs_2_
  20.9 5.0 %score.6.refs_6_ = f32[4,8,128]{2,1,0:T(8,128)S(1)} custom-call(s32[2]{0:T(128)S(1)} %and_select_fusion.counts_ref, bf16[74,64,128]{2,1,0:T(8,128)(2,1)S(1)} %prep.1.refs_0_.refs_1_, bf16[74,64,128]{2,1,0:T(8,128)(2,1)S(1)} %collective-permute-done.3.refs_1_.refs_2_, bf16[4,256,128]{2,1,0:T(8,128)(2,1)S(1)} %collective-permute-done.6.refs_2_), custom_call_target="tpu_custom_call" | custom-call | flops 4966055936 | bytes 2424832 | tf_op jit(solution)/shard_map/score/pallas_call | solution.py:231
  25.9 0.0 collective-permute-done.5.refs_2_
  25.9 5.1 %score.5.refs_5_ = f32[4,8,128]{2,1,0:T(8,128)S(1)} custom-call(s32[2]{0:T(128)S(1)} %and_select_fusion.counts_ref, bf16[74,64,128]{2,1,0:T(8,128)(2,1)S(1)} %prep.1.refs_0_.refs_1_, bf16[74,64,128]{2,1,0:T(8,128)(2,1)S(1)} %collective-permute-done.3.refs_1_.refs_2_, bf16[4,256,128]{2,1,0:T(8,128)(2,1)S(1)} %collective-permute-done.5.refs_2_), custom_call_target="tpu_custom_call" | custom-call | flops 4966055936 | bytes 2424832 | tf_op jit(solution)/shard_map/score/pallas_call | solution.py:231
  31.0 0.0 copy-start.2
  31.0 0.0 copy-start
  31.0 0.0 collective-permute-done.4.refs_3_
  31.0 5.7 %score.7 = f32[16,8,128]{2,1,0:T(8,128)} custom-call(s32[2]{0:T(128)S(1)} %and_select_fusion.counts_ref, s32[16]{0:T(128)S(1)} %xor.30.refs_0_, bf16[74,64,128]{2,1,0:T(8,128)(2,1)S(1)} %prep.1.refs_0_.refs_1_, bf16[74,64,128]{2,1,0:T(8,128)(2,1)S(1)} %collective-permute-done.3.refs_1_.refs_2_, bf16[4,256,128]{2,1,0:T(8,128)(2,1)S(1)} %collective-permute-done.4.refs_3_, ...), custom_call_target="tpu_custom_call" | custom-call | flops 4966055936 | bytes 2424832 | tf_op jit(solution)/shard_map/score/pallas_call | solution.py:231
  36.7 4.8 %all-to-all-start = ((f32[16,8,128]{2,1,0:T(8,128)}), f32[16,8,128]{2,1,0:T(8,128)S(1)}, u32[]{:S(2)}, u32[]{:S(2)}) async-start(f32[16,8,128]{2,1,0:T(8,128)} %score.7), calls=%async_computation | async-start | bytes 131072 | tf_op jit(solution)/shard_map/all_to_all | solution.py:294
  41.5 0.0 copy-done.2
  41.5 7.5 %all-to-all-done.table_ref = f32[16,8,128]{2,1,0:T(8,128)S(1)} async-done(((f32[16,8,128]{2,1,0:T(8,128)}), f32[16,8,128]{2,1,0:T(8,128)S(1)}, u32[]{:S(2)}, u32[]{:S(2)}) %all-to-all-start) | async-done | bytes 65568 | tf_op jit(solution)/shard_map/all_to_all | solution.py:294
  49.0 0.0 copy-done
  49.0 0.7 %pick.1 = f32[8,256]{1,0:T(8,128)} custom-call(s32[1]{0:T(128)} %bitcast.core_ref, f32[16,8,128]{2,1,0:T(8,128)S(1)} %all-to-all-done.table_ref, s32[8,256]{1,0:T(8,128)S(1)} %bitcast.7, s32[8,256]{1,0:T(8,128)S(1)} %copy-done), custom_call_target="tpu_custom_call" | custom-call | tf_op jit(solution)/shard_map/pick/pallas_call | solution.py:295
  (7 shorter events, 0.1 us)
Async XLA Ops:
  0.0 7.4 %collective-permute-start = (bf16[1,256,128]{2,1,0:T(8,128)(2,1)}, bf16[1,256,128]{2,1,0:T(8,128)(2,1)S(1)}, u32[]{:S(2)}, u32[]{:S(2)}) collective-permute-start(bf16[1,256,128]{2,1,0:T(8,128)(2,1)} %bitcast.8), channel_id=1, source_target_pairs={{0,8},{2,10},{4,12},{6,14},{8,0},{10,2},{12,4},{14,6},{16,24},{18,... | collective-permute-start | bytes 196616 | tf_op jit(solution)/shard_map/ppermute | solution.py:274
  3.0 7.5 %collective-permute-start.1 = (bf16[1,256,128]{2,1,0:T(8,128)(2,1)}, bf16[1,256,128]{2,1,0:T(8,128)(2,1)S(1)}, u32[]{:S(2)}, u32[]{:S(2)}) collective-permute-start(bf16[1,256,128]{2,1,0:T(8,128)(2,1)} %bitcast.9), channel_id=1, source_target_pairs={{0,16},{2,18},{4,20},{6,22},{8,24},{10,26},{12,28},{14,30},{16,0},... | collective-permute-start | bytes 196616 | tf_op jit(solution)/shard_map/ppermute | solution.py:274
  5.6 6.3 %collective-permute-start.2 = (bf16[1,256,128]{2,1,0:T(8,128)(2,1)}, bf16[1,256,128]{2,1,0:T(8,128)(2,1)S(1)}, u32[]{:S(2)}, u32[]{:S(2)}) collective-permute-start(bf16[1,256,128]{2,1,0:T(8,128)(2,1)} %bitcast.10), channel_id=1, source_target_pairs={{0,24},{2,26},{4,28},{6,30},{8,16},{10,18},{12,20},{14,22},{16,8},... | collective-permute-start | bytes 196616 | tf_op jit(solution)/shard_map/ppermute | solution.py:274
  5.6 6.4 %copy-start.1 = (bf16[8,32,128]{2,1,0:T(8,128)(2,1)S(1)}, bf16[8,32,128]{2,1,0:T(8,128)(2,1)}, u32[]{:S(2)}) copy-start(bf16[8,32,128]{2,1,0:T(8,128)(2,1)} %param.5) | copy-start | bytes 196612
  11.9 3.7 %collective-permute-start.3 = (bf16[74,64,128]{2,1,0:T(8,128)(2,1)S(1)}, bf16[74,64,128]{2,1,0:T(8,128)(2,1)S(1)}, u32[]{:S(2)}, u32[]{:S(2)}) collective-permute-start(bf16[74,64,128]{2,1,0:T(8,128)(2,1)S(1)} %prep.1.refs_0_.refs_1_), channel_id=1, source_target_pairs={{0,1},{1,0},{2,3},{3,2},{4,5},{5,4},{6,7},{7,6},{8,9},{9,8},{10,11... | collective-permute-start | bytes 3637256 | tf_op jit(solution)/shard_map/ppermute | solution.py:287
  12.1 8.8 %collective-permute-start.6 = (bf16[4,256,128]{2,1,0:T(8,128)(2,1)S(1)}, bf16[4,256,128]{2,1,0:T(8,128)(2,1)S(1)}, u32[]{:S(2)}, u32[]{:S(2)}) collective-permute-start(bf16[4,256,128]{2,1,0:T(8,128)(2,1)S(1)} %pad_maximum_fusion.refs_2_), channel_id=1, source_target_pairs={{0,4},{2,6},{4,0},{6,2},{8,12},{10,14},{12,8},{14,10},{16,20},{18,... | collective-permute-start | bytes 786440 | tf_op jit(solution)/shard_map/ppermute | solution.py:274
  13.7 12.3 %collective-permute-start.5 = (bf16[4,256,128]{2,1,0:T(8,128)(2,1)S(1)}, bf16[4,256,128]{2,1,0:T(8,128)(2,1)S(1)}, u32[]{:S(2)}, u32[]{:S(2)}) collective-permute-start(bf16[4,256,128]{2,1,0:T(8,128)(2,1)S(1)} %pad_maximum_fusion.refs_2_), channel_id=1, source_target_pairs={{0,2},{2,0},{4,6},{6,4},{8,10},{10,8},{12,14},{14,12},{16,18},{18,... | collective-permute-start | bytes 786440 | tf_op jit(solution)/shard_map/ppermute | solution.py:274
  15.2 15.8 %collective-permute-start.4 = (bf16[4,256,128]{2,1,0:T(8,128)(2,1)S(1)}, bf16[4,256,128]{2,1,0:T(8,128)(2,1)S(1)}, u32[]{:S(2)}, u32[]{:S(2)}) collective-permute-start(bf16[4,256,128]{2,1,0:T(8,128)(2,1)S(1)} %pad_maximum_fusion.refs_2_), channel_id=1, source_target_pairs={{0,6},{2,4},{4,2},{6,0},{8,14},{10,12},{12,10},{14,8},{16,22},{18,... | collective-permute-start | bytes 786440 | tf_op jit(solution)/shard_map/ppermute | solution.py:274
  31.0 10.5 %copy-start.2 = (s32[8,256,1]{1,2,0:T(1,128)S(1)}, s32[8,256,1]{1,2,0:T(1,128)}, u32[]{:S(2)}) copy-start(s32[8,256,1]{1,2,0:T(1,128)} %param.6) | copy-start | bytes 24580
  31.0 18.1 %copy-start = (s32[8,256]{1,0:T(8,128)S(1)}, s32[8,256]{1,0:T(8,128)}, u32[]{:S(2)}) copy-start(s32[8,256]{1,0:T(8,128)} %local_ref.1) | copy-start | bytes 24580
  36.7 12.4 %all-to-all-start = ((f32[16,8,128]{2,1,0:T(8,128)}), f32[16,8,128]{2,1,0:T(8,128)S(1)}, u32[]{:S(2)}, u32[]{:S(2)}) async-start(f32[16,8,128]{2,1,0:T(8,128)} %score.7), calls=%async_computation | async-start | bytes 131072 | tf_op jit(solution)/shard_map/all_to_all | solution.py:294

commit v4 on v3

--- a/solution.py
+++ b/solution.py
@@ -115,7 +115,7 @@
 
     def stream(part, load):
         rows = read_rows(part)
-        rows = jnp.concatenate([rows, rows], axis=1)
+        rows = jnp.concatenate([rows, jnp.zeros_like(rows)], axis=1)
         for unit in range(2):
             pltpu.matmul_acc_lhs(units[part][unit], rows, 0 if load else None)
 
@@ -255,7 +255,7 @@
     for half in range(shard_ref.shape[1] // LANES):
         lanes = slice(half * LANES, half * LANES + LANES)
         shard = shard_ref[:, lanes]
-        chip = shard // 2
+        chip = chips - 1 - shard // 2
         lane = ((shard % 2) ^ core_ref[0]) * store + local_ref[:, lanes]
         total = jnp.zeros(lane.shape, jnp.float32)
         for k in range(chips):
@@ -290,8 +290,12 @@
     beside = [column] + [swap(column, k) for k in (1, 2, 3)]
     pieces = [score(counts, own, sib, column)]
     pieces += [score(counts, own, sib, beside[k]) for k in (1, 2)]
-    table = score(counts, own, sib, beside[3], ids=ids.reshape(-1), earlier=pieces)
-    returned = lax.all_to_all(table, "psg", split_axis=0, concat_axis=0, tiled=True)
+    ids = chips - 1 - ids.reshape(-1)
+    table = score(counts, own, sib, beside[3], ids=ids, earlier=pieces)
+    returned = lax.all_to_all(
+        table, "psg", split_axis=0, concat_axis=0, tiled=True,
+        axis_index_groups=[list(reversed(range(chips)))],
+    )
     return pl.pallas_call(
         pick_kernel,
         out_shape=jax.ShapeDtypeStruct(cand_local.shape, jnp.float32),

time: 50.1 us -> 47.4 us (0.946)
  waiting for transfers between devices: 12.1 us -> 7.79 us
  starting transfers between devices: 14 us -> 17 us
  Pallas kernels: 23.3 us -> 22.1 us
    all_to_all x1, waiting for transfers between devices: 7.51 us -> 2.94 us  [body(): lax.all_to_all(table, 'psg', split_axis=0, concat_axis=0, tiled=True, axi...]
    all_to_all x1, starting transfers between devices: 4.82 us -> 7.82 us  [body(): lax.all_to_all(table, 'psg', split_axis=0, concat_axis=0, tiled=True, axi...]
    pallas_call x4, Pallas kernels: 20.8 us -> 19.6 us  [score(): pl.pallas_call(functools.partial(score_kernel, first, len(earlier)), out_...]
where the time goes in v4:
time: 47.4 us; the launch traced here: 47.2 us
  Pallas kernels  22.1 us (47%)
  starting transfers between devices  17 us (36%)
  waiting for transfers between devices  7.79 us (16%)
    pallas_call x4, Pallas kernels, score(): pl.pallas_call(functools.partial(score_kernel, first, len(earlier)), out_...  19.6 us
    ppermute x6, starting transfers between devices, swap(): return lax.ppermute(a, 'psg', [(i, i ^ bits) for i in range(chips)])  9.17 us
    all_to_all x1, starting transfers between devices, body(): lax.all_to_all(table, 'psg', split_axis=0, concat_axis=0, tiled=True, axi...  7.82 us
    ppermute x6, waiting for transfers between devices, swap(): return lax.ppermute(a, 'psg', [(i, i ^ bits) for i in range(chips)])  4.85 us
    all_to_all x1, waiting for transfers between devices, body(): lax.all_to_all(table, 'psg', split_axis=0, concat_axis=0, tiled=True, axi...  2.94 us
    pallas_call x1, Pallas kernels, prep(): pl.pallas_call(prep_kernel, out_shape=jax.ShapeDtypeStruct((padded + 2, s...  1.78 us
  transfers between devices with their start and end apart: 8, of which 4 were waited for; matrix products, arithmetic and copies ran while one was open for 1% of the time, Pallas kernels for 34%

profile of v4, /device:TPU:0, one launch (start us, length us, event | category | flops | bytes accessed | tf_op | source)
XLA Modules:
  0.0 47.2 jit_solution(11820822741878105174)
XLA Ops:
  0.0 3.0 %collective-permute-start = (bf16[1,256,128]{2,1,0:T(8,128)(2,1)}, bf16[1,256,128]{2,1,0:T(8,128)(2,1)S(1)}, u32[]{:S(2)}, u32[]{:S(2)}) collective-permute-start(bf16[1,256,128]{2,1,0:T(8,128)(2,1)} %bitcast.8), channel_id=1, source_target_pairs={{0,8},{2,10},{4,12},{6,14},{8,0},{10,2},{12,4},{14,6},{16,24},{18,... | collective-permute-start | bytes 196616 | tf_op jit(solution)/shard_map/ppermute | solution.py:274
  3.0 2.6 %collective-permute-start.1 = (bf16[1,256,128]{2,1,0:T(8,128)(2,1)}, bf16[1,256,128]{2,1,0:T(8,128)(2,1)S(1)}, u32[]{:S(2)}, u32[]{:S(2)}) collective-permute-start(bf16[1,256,128]{2,1,0:T(8,128)(2,1)} %bitcast.9), channel_id=1, source_target_pairs={{0,16},{2,18},{4,20},{6,22},{8,24},{10,26},{12,28},{14,30},{16,0},... | collective-permute-start | bytes 196616 | tf_op jit(solution)/shard_map/ppermute | solution.py:274
  5.6 0.0 collective-permute-start.2
  5.6 0.0 copy-start.1
  5.6 1.8 %prep.1.refs_0_.refs_1_ = bf16[74,64,128]{2,1,0:T(8,128)(2,1)S(1)} custom-call(s32[1,64]{1,0:T(1,128)} %bitcast.13, bf16[70,64,128]{2,1,0:T(8,128)(2,1)} %bitcast.12), custom_call_target="tpu_custom_call" | custom-call | flops 2348810240 | bytes 2293760 | tf_op jit(solution)/shard_map/prep/pallas_call | solution.py:66
  7.4 0.0 collective-permute-done
  7.4 3.1 %collective-permute-done.1 = bf16[1,256,128]{2,1,0:T(8,128)(2,1)S(1)} collective-permute-done((bf16[1,256,128]{2,1,0:T(8,128)(2,1)}, bf16[1,256,128]{2,1,0:T(8,128)(2,1)S(1)}, u32[]{:S(2)}, u32[]{:S(2)}) %collective-permute-start.1) | collective-permute-done | bytes 65568 | tf_op jit(solution)/shard_map/ppermute | solution.py:274
  10.5 1.4 %collective-permute-done.2 = bf16[1,256,128]{2,1,0:T(8,128)(2,1)S(1)} collective-permute-done((bf16[1,256,128]{2,1,0:T(8,128)(2,1)}, bf16[1,256,128]{2,1,0:T(8,128)(2,1)S(1)}, u32[]{:S(2)}, u32[]{:S(2)}) %collective-permute-start.2) | collective-permute-done | bytes 65568 | tf_op jit(solution)/shard_map/ppermute | solution.py:274
  11.9 0.0 collective-permute-start.3
  11.9 0.1 sub.24.refs_0_
  12.1 0.0 copy-done.1
  12.1 1.6 %collective-permute-start.6 = (bf16[4,256,128]{2,1,0:T(8,128)(2,1)S(1)}, bf16[4,256,128]{2,1,0:T(8,128)(2,1)S(1)}, u32[]{:S(2)}, u32[]{:S(2)}) collective-permute-start(bf16[4,256,128]{2,1,0:T(8,128)(2,1)S(1)} %pad_maximum_fusion.refs_2_), channel_id=1, source_target_pairs={{0,4},{2,6},{4,0},{6,2},{8,12},{10,14},{12,8},{14,10},{16,20},{18,... | collective-permute-start | bytes 786440 | tf_op jit(solution)/shard_map/ppermute | solution.py:274
  13.7 1.5 %collective-permute-start.5 = (bf16[4,256,128]{2,1,0:T(8,128)(2,1)S(1)}, bf16[4,256,128]{2,1,0:T(8,128)(2,1)S(1)}, u32[]{:S(2)}, u32[]{:S(2)}) collective-permute-start(bf16[4,256,128]{2,1,0:T(8,128)(2,1)S(1)} %pad_maximum_fusion.refs_2_), channel_id=1, source_target_pairs={{0,2},{2,0},{4,6},{6,4},{8,10},{10,8},{12,14},{14,12},{16,18},{18,... | collective-permute-start | bytes 786440 | tf_op jit(solution)/shard_map/ppermute | solution.py:274
  15.2 0.5 %collective-permute-start.4 = (bf16[4,256,128]{2,1,0:T(8,128)(2,1)S(1)}, bf16[4,256,128]{2,1,0:T(8,128)(2,1)S(1)}, u32[]{:S(2)}, u32[]{:S(2)}) collective-permute-start(bf16[4,256,128]{2,1,0:T(8,128)(2,1)S(1)} %pad_maximum_fusion.refs_2_), channel_id=1, source_target_pairs={{0,6},{2,4},{4,2},{6,0},{8,14},{10,12},{12,10},{14,8},{16,22},{18,... | collective-permute-start | bytes 786440 | tf_op jit(solution)/shard_map/ppermute | solution.py:274
  15.6 0.0 collective-permute-done.3.refs_1_.refs_2_
  15.7 0.1 add_reduce_fusion
  15.8 4.7 %score.4.refs_4_ = f32[4,8,128]{2,1,0:T(8,128)S(1)} custom-call(s32[2]{0:T(128)S(1)} %and_select_fusion.counts_ref, bf16[74,64,128]{2,1,0:T(8,128)(2,1)S(1)} %prep.1.refs_0_.refs_1_, bf16[74,64,128]{2,1,0:T(8,128)(2,1)S(1)} %collective-permute-done.3.refs_1_.refs_2_, bf16[4,256,128]{2,1,0:T(8,128)(2,1)S(1)} %pad_maximum_fusion.refs_2_), custom_call_target="tpu_custom_call" | custom-call | flops 4966055936 | bytes 2424832 | tf_op jit(solution)/shard_map/score/pallas_call | solution.py:231
  20.5 0.3 collective-permute-done.6.refs_2_
  20.9 4.7 %score.6.refs_6_ = f32[4,8,128]{2,1,0:T(8,128)S(1)} custom-call(s32[2]{0:T(128)S(1)} %and_select_fusion.counts_ref, bf16[74,64,128]{2,1,0:T(8,128)(2,1)S(1)} %prep.1.refs_0_.refs_1_, bf16[74,64,128]{2,1,0:T(8,128)(2,1)S(1)} %collective-permute-done.3.refs_1_.refs_2_, bf16[4,256,128]{2,1,0:T(8,128)(2,1)S(1)} %collective-permute-done.6.refs_2_), custom_call_target="tpu_custom_call" | custom-call | flops 4966055936 | bytes 2424832 | tf_op jit(solution)/shard_map/score/pallas_call | solution.py:231
  25.6 0.0 collective-permute-done.5.refs_2_
  25.6 4.7 %score.5.refs_5_ = f32[4,8,128]{2,1,0:T(8,128)S(1)} custom-call(s32[2]{0:T(128)S(1)} %and_select_fusion.counts_ref, bf16[74,64,128]{2,1,0:T(8,128)(2,1)S(1)} %prep.1.refs_0_.refs_1_, bf16[74,64,128]{2,1,0:T(8,128)(2,1)S(1)} %collective-permute-done.3.refs_1_.refs_2_, bf16[4,256,128]{2,1,0:T(8,128)(2,1)S(1)} %collective-permute-done.5.refs_2_), custom_call_target="tpu_custom_call" | custom-call | flops 4966055936 | bytes 2424832 | tf_op jit(solution)/shard_map/score/pallas_call | solution.py:231
  30.4 0.0 copy-start.2
  30.4 0.0 copy-start
  30.4 0.0 collective-permute-done.4.refs_3_
  30.4 5.4 %score.7 = f32[16,8,128]{2,1,0:T(8,128)} custom-call(s32[2]{0:T(128)S(1)} %and_select_fusion.counts_ref, s32[16]{0:T(128)S(1)} %sub.24.refs_0_, bf16[74,64,128]{2,1,0:T(8,128)(2,1)S(1)} %prep.1.refs_0_.refs_1_, bf16[74,64,128]{2,1,0:T(8,128)(2,1)S(1)} %collective-permute-done.3.refs_1_.refs_2_, bf16[4,256,128]{2,1,0:T(8,128)(2,1)S(1)} %collective-permute-done.4.refs_3_, ...), custom_call_target="tpu_custom_call" | custom-call | flops 4966055936 | bytes 2424832 | tf_op jit(solution)/shard_map/score/pallas_call | solution.py:231
  35.7 7.8 %all-to-all-start = ((f32[16,8,128]{2,1,0:T(8,128)}), f32[16,8,128]{2,1,0:T(8,128)S(1)}, u32[]{:S(2)}, u32[]{:S(2)}) async-start(f32[16,8,128]{2,1,0:T(8,128)} %score.7), calls=%async_computation | async-start | bytes 131072 | tf_op jit(solution)/shard_map/all_to_all | solution.py:295
  43.6 0.0 copy-done.2
  43.6 2.9 %all-to-all-done.table_ref = f32[16,8,128]{2,1,0:T(8,128)S(1)} async-done(((f32[16,8,128]{2,1,0:T(8,128)}), f32[16,8,128]{2,1,0:T(8,128)S(1)}, u32[]{:S(2)}, u32[]{:S(2)}) %all-to-all-start) | async-done | bytes 65568 | tf_op jit(solution)/shard_map/all_to_all | solution.py:295
  46.5 0.0 copy-done
  46.5 0.7 %pick.1 = f32[8,256]{1,0:T(8,128)} custom-call(s32[1]{0:T(128)} %bitcast.core_ref, f32[16,8,128]{2,1,0:T(8,128)S(1)} %all-to-all-done.table_ref, s32[8,256]{1,0:T(8,128)S(1)} %bitcast.7, s32[8,256]{1,0:T(8,128)S(1)} %copy-done), custom_call_target="tpu_custom_call" | custom-call | tf_op jit(solution)/shard_map/pick/pallas_call | solution.py:299
  (7 shorter events, 0.1 us)
Async XLA Ops:
  0.0 7.4 %collective-permute-start = (bf16[1,256,128]{2,1,0:T(8,128)(2,1)}, bf16[1,256,128]{2,1,0:T(8,128)(2,1)S(1)}, u32[]{:S(2)}, u32[]{:S(2)}) collective-permute-start(bf16[1,256,128]{2,1,0:T(8,128)(2,1)} %bitcast.8), channel_id=1, source_target_pairs={{0,8},{2,10},{4,12},{6,14},{8,0},{10,2},{12,4},{14,6},{16,24},{18,... | collective-permute-start | bytes 196616 | tf_op jit(solution)/shard_map/ppermute | solution.py:274
  3.0 7.5 %collective-permute-start.1 = (bf16[1,256,128]{2,1,0:T(8,128)(2,1)}, bf16[1,256,128]{2,1,0:T(8,128)(2,1)S(1)}, u32[]{:S(2)}, u32[]{:S(2)}) collective-permute-start(bf16[1,256,128]{2,1,0:T(8,128)(2,1)} %bitcast.9), channel_id=1, source_target_pairs={{0,16},{2,18},{4,20},{6,22},{8,24},{10,26},{12,28},{14,30},{16,0},... | collective-permute-start | bytes 196616 | tf_op jit(solution)/shard_map/ppermute | solution.py:274
  5.6 6.3 %collective-permute-start.2 = (bf16[1,256,128]{2,1,0:T(8,128)(2,1)}, bf16[1,256,128]{2,1,0:T(8,128)(2,1)S(1)}, u32[]{:S(2)}, u32[]{:S(2)}) collective-permute-start(bf16[1,256,128]{2,1,0:T(8,128)(2,1)} %bitcast.10), channel_id=1, source_target_pairs={{0,24},{2,26},{4,28},{6,30},{8,16},{10,18},{12,20},{14,22},{16,8},... | collective-permute-start | bytes 196616 | tf_op jit(solution)/shard_map/ppermute | solution.py:274
  5.6 6.4 %copy-start.1 = (bf16[8,32,128]{2,1,0:T(8,128)(2,1)S(1)}, bf16[8,32,128]{2,1,0:T(8,128)(2,1)}, u32[]{:S(2)}) copy-start(bf16[8,32,128]{2,1,0:T(8,128)(2,1)} %param.5) | copy-start | bytes 196612
  11.9 3.7 %collective-permute-start.3 = (bf16[74,64,128]{2,1,0:T(8,128)(2,1)S(1)}, bf16[74,64,128]{2,1,0:T(8,128)(2,1)S(1)}, u32[]{:S(2)}, u32[]{:S(2)}) collective-permute-start(bf16[74,64,128]{2,1,0:T(8,128)(2,1)S(1)} %prep.1.refs_0_.refs_1_), channel_id=1, source_target_pairs={{0,1},{1,0},{2,3},{3,2},{4,5},{5,4},{6,7},{7,6},{8,9},{9,8},{10,11... | collective-permute-start | bytes 3637256 | tf_op jit(solution)/shard_map/ppermute | solution.py:287
  12.1 8.8 %collective-permute-start.6 = (bf16[4,256,128]{2,1,0:T(8,128)(2,1)S(1)}, bf16[4,256,128]{2,1,0:T(8,128)(2,1)S(1)}, u32[]{:S(2)}, u32[]{:S(2)}) collective-permute-start(bf16[4,256,128]{2,1,0:T(8,128)(2,1)S(1)} %pad_maximum_fusion.refs_2_), channel_id=1, source_target_pairs={{0,4},{2,6},{4,0},{6,2},{8,12},{10,14},{12,8},{14,10},{16,20},{18,... | collective-permute-start | bytes 786440 | tf_op jit(solution)/shard_map/ppermute | solution.py:274
  13.7 11.9 %collective-permute-start.5 = (bf16[4,256,128]{2,1,0:T(8,128)(2,1)S(1)}, bf16[4,256,128]{2,1,0:T(8,128)(2,1)S(1)}, u32[]{:S(2)}, u32[]{:S(2)}) collective-permute-start(bf16[4,256,128]{2,1,0:T(8,128)(2,1)S(1)} %pad_maximum_fusion.refs_2_), channel_id=1, source_target_pairs={{0,2},{2,0},{4,6},{6,4},{8,10},{10,8},{12,14},{14,12},{16,18},{18,... | collective-permute-start | bytes 786440 | tf_op jit(solution)/shard_map/ppermute | solution.py:274
  15.2 15.2 %collective-permute-start.4 = (bf16[4,256,128]{2,1,0:T(8,128)(2,1)S(1)}, bf16[4,256,128]{2,1,0:T(8,128)(2,1)S(1)}, u32[]{:S(2)}, u32[]{:S(2)}) collective-permute-start(bf16[4,256,128]{2,1,0:T(8,128)(2,1)S(1)} %pad_maximum_fusion.refs_2_), channel_id=1, source_target_pairs={{0,6},{2,4},{4,2},{6,0},{8,14},{10,12},{12,10},{14,8},{16,22},{18,... | collective-permute-start | bytes 786440 | tf_op jit(solution)/shard_map/ppermute | solution.py:274
  30.4 13.2 %copy-start.2 = (s32[8,256,1]{1,2,0:T(1,128)S(1)}, s32[8,256,1]{1,2,0:T(1,128)}, u32[]{:S(2)}) copy-start(s32[8,256,1]{1,2,0:T(1,128)} %param.6) | copy-start | bytes 24580
  30.4 16.2 %copy-start = (s32[8,256]{1,0:T(8,128)S(1)}, s32[8,256]{1,0:T(8,128)}, u32[]{:S(2)}) copy-start(s32[8,256]{1,0:T(8,128)} %local_ref.1) | copy-start | bytes 24580
  35.7 10.8 %all-to-all-start = ((f32[16,8,128]{2,1,0:T(8,128)}), f32[16,8,128]{2,1,0:T(8,128)S(1)}, u32[]{:S(2)}, u32[]{:S(2)}) async-start(f32[16,8,128]{2,1,0:T(8,128)} %score.7), calls=%async_computation | async-start | bytes 131072 | tf_op jit(solution)/shard_map/all_to_all | solution.py:295

commit v5 on v4

--- a/solution.py
+++ b/solution.py
@@ -87,24 +87,26 @@
 def chunk_counts(own, sib):
     per_core = own.shape[1] // GROUPS
     longest = [plane[-2, ::per_core, 0].astype(jnp.int32) for plane in (own, sib)]
-    return (jnp.maximum(*longest) + CHUNK - 1) // CHUNK
-
-
-def score_block(own_ref, sib_ref, read_rows, acc, sums, units, counts, write):
+    return jnp.maximum((jnp.maximum(*longest) + CHUNK - 1) // CHUNK, 2)
+
+
+def score_block(own_ref, sib_ref, read_rows, acc, sums, units, read_counts, write):
     half = acc[0].shape[1]
     per_core = own_ref.shape[1] // GROUPS
     width = 2 * per_core
     per_tile = 2 * LANES // width
-    last = counts[0] + counts[1] - 1
     zeros = jnp.zeros((2 * LANES, LANES), own_ref.dtype)
 
     def where_of(step):
+        if isinstance(step, int):
+            return 0, step
         group = (step >= counts[0]).astype(jnp.int32)
         return group, step - group * counts[0]
 
     def push(step):
         group, at = where_of(step)
-        lanes = pl.ds(pl.multiple_of(group * per_core, per_core), per_core)
+        lanes = group * per_core
+        lanes = pl.ds(lanes if isinstance(group, int) else pl.multiple_of(lanes, per_core), per_core)
         for unit in range(2):
             parts = []
             for k in range(per_tile):
@@ -122,13 +124,23 @@
     def pop(part, step):
         group, at = where_of(step)
         best = jnp.maximum(pltpu.matmul_pop(units[part][0]), pltpu.matmul_pop(units[part][1]))
-        acc[part][group] = jnp.maximum(jnp.where(at == 0, LOWEST, acc[part][group]), best)
+        if isinstance(step, int):
+            acc[part][group] = best if at == 0 else jnp.maximum(acc[part][group], best)
+        else:
+            acc[part][group] = jnp.maximum(jnp.where(at == 0, LOWEST, acc[part][group]), best)
 
     push(0)
     stream(0, True)
     push(1)
     pop(0, 0)
     stream(1, False)
+    pop(1, 0)
+    counts = read_counts()
+    last = counts[0] + counts[1] - 1
+    stream(0, True)
+    push(jnp.minimum(last, 2))
+    stream(1, False)
+    pop(0, 1)
 
     def body(step, _):
         stream(0, True)
@@ -159,7 +171,7 @@
             total = total + sums[part, pl.ds(k, half // TOKENS, stride=8), :]
         write(part, total)
 
-    lax.fori_loop(1, last, body, 0)
+    lax.fori_loop(2, last, body, 0)
     stream(0, True)
     pop(1, last - 1)
     stream(1, False)
@@ -171,7 +183,13 @@
     if earlier:
         ids_ref, *refs = refs
     own_ref, sib_ref, blocks_ref, *refs = refs
-    pieces, (out_ref, acc_0, acc_1, sums, scores) = refs[:earlier], refs[earlier:]
+    pieces, refs = refs[:earlier], refs[earlier:]
+    out_ref, acc_0, acc_1, sums, scores, counts_here, ids_here, arrived = refs
+    load_counts = pltpu.make_async_copy(counts_ref, counts_here, arrived.at[0])
+    load_counts.start()
+    if earlier:
+        load_ids = pltpu.make_async_copy(ids_ref, ids_here, arrived.at[1])
+        load_ids.start()
     blocks, rows, dim = blocks_ref.shape
     step = min(blocks - first, BLOCKS)
     local = rows // TOKENS
@@ -179,11 +197,23 @@
     planes, store, _ = own_ref.shape
     per_core = store // GROUPS
     flat_ref = blocks_ref.reshape(blocks * rows, dim)
-    at = 0
-    for piece in pieces:
-        for block in range(piece.shape[0]):
-            out_ref[ids_ref[at]] = piece[block]
-            at += 1
+    at = sum(piece.shape[0] for piece in pieces)
+    waited, placed = [], []
+
+    def receive():
+        if placed:
+            return
+        placed.append(load_ids.wait())
+        spot = 0
+        for piece in pieces:
+            for block in range(piece.shape[0]):
+                out_ref[ids_here[spot]] = piece[block]
+                spot += 1
+
+    def read_counts():
+        if not waited:
+            waited.append(load_counts.wait())
+        return [counts_here[g] for g in range(GROUPS)]
 
     lane = lax.broadcasted_iota(jnp.int32, (16, LANES), 1)
     position = jnp.where(
@@ -206,15 +236,20 @@
 
             score_block(
                 own_ref, sib_ref, read_rows, (acc_0, acc_1), sums,
-                ((units[0], units[1]), (units[2], units[3])), [counts_ref[0], counts_ref[1]], write,
+                ((units[0], units[1]), (units[2], units[3])), read_counts, write,
             )
+            if earlier:
+                receive()
             for block in range(step):
-                spot = ids_ref[at + start + block] if earlier else start + block
+                spot = ids_here[at + start + block] if earlier else start + block
                 out_ref[spot] = scores[block * local : (block + 1) * local]
 
         if blocks - first == step:
             chunk(0)
         else:
+            read_counts()
+            if earlier:
+                receive()
             pl.loop(0, blocks - first, step=step)(chunk)
 
     pl.run_scoped(run, *[pltpu.ACC(unit)((half, 2 * LANES), jnp.float32) for unit in (0, 1, 0, 1)])
@@ -231,13 +266,16 @@
     return pl.pallas_call(
         functools.partial(score_kernel, first, len(earlier)),
         out_shape=jax.ShapeDtypeStruct((total, local, 2 * own.shape[1]), jnp.float32),
-        in_specs=[SMEM] * len(scalars) + [VMEM] * len(operands),
+        in_specs=[pl.BlockSpec(memory_space=pl.ANY)] * len(scalars) + [VMEM] * len(operands),
         out_specs=VMEM,
         scratch_shapes=[
             pltpu.VMEM((GROUPS, half, 2 * LANES), jnp.float32),
             pltpu.VMEM((GROUPS, half, 2 * LANES), jnp.float32),
             pltpu.VMEM((2, half * 8 // TOKENS, LANES), jnp.float32),
             pltpu.VMEM((step * local, LANES), jnp.float32),
+            pltpu.SMEM(counts.shape, jnp.int32),
+            pltpu.SMEM((total,), jnp.int32),
+            pltpu.SemaphoreType.DMA((2,)),
         ],
         compiler_params=pltpu.CompilerParams(vmem_limit_bytes=12 << 20),
         cost_estimate=pl.CostEstimate(

time: 47.4 us -> 46.2 us (0.975)
  starting transfers between devices: 17 us -> 16.2 us
    all_to_all x1, starting transfers between devices: 7.82 us -> 7.02 us  [body(): lax.all_to_all(table, 'psg', split_axis=0, concat_axis=0, tiled=True, axi...]
where the time goes in v5:
time: 46.2 us; the launch traced here: 46.3 us
  Pallas kernels  21.9 us (47%)
  starting transfers between devices  16.2 us (35%)
  waiting for transfers between devices  7.78 us (17%)
    pallas_call x4, Pallas kernels, score(): pl.pallas_call(functools.partial(score_kernel, first, len(earlier)), out_...  19.4 us
    ppermute x6, starting transfers between devices, swap(): return lax.ppermute(a, 'psg', [(i, i ^ bits) for i in range(chips)])  9.17 us
    all_to_all x1, starting transfers between devices, body(): lax.all_to_all(table, 'psg', split_axis=0, concat_axis=0, tiled=True, axi...  7.02 us
    ppermute x6, waiting for transfers between devices, swap(): return lax.ppermute(a, 'psg', [(i, i ^ bits) for i in range(chips)])  4.89 us
    all_to_all x1, waiting for transfers between devices, body(): lax.all_to_all(table, 'psg', split_axis=0, concat_axis=0, tiled=True, axi...  2.88 us
    pallas_call x1, Pallas kernels, prep(): pl.pallas_call(prep_kernel, out_shape=jax.ShapeDtypeStruct((padded + 2, s...  1.78 us
  transfers between devices with their start and end apart: 8, of which 4 were waited for; matrix products, arithmetic and copies ran while one was open for 1% of the time, Pallas kernels for 34%

profile of v5, /device:TPU:0, one launch (start us, length us, event | category | flops | bytes accessed | tf_op | source)
XLA Modules:
  0.0 46.3 jit_solution(322219437491215243)
XLA Ops:
  0.0 3.0 %collective-permute-start = (bf16[1,256,128]{2,1,0:T(8,128)(2,1)}, bf16[1,256,128]{2,1,0:T(8,128)(2,1)S(1)}, u32[]{:S(2)}, u32[]{:S(2)}) collective-permute-start(bf16[1,256,128]{2,1,0:T(8,128)(2,1)} %bitcast.8), channel_id=1, source_target_pairs={{0,8},{2,10},{4,12},{6,14},{8,0},{10,2},{12,4},{14,6},{16,24},{18,... | collective-permute-start | bytes 196616 | tf_op jit(solution)/shard_map/ppermute | solution.py:312
  3.0 2.6 %collective-permute-start.1 = (bf16[1,256,128]{2,1,0:T(8,128)(2,1)}, bf16[1,256,128]{2,1,0:T(8,128)(2,1)S(1)}, u32[]{:S(2)}, u32[]{:S(2)}) collective-permute-start(bf16[1,256,128]{2,1,0:T(8,128)(2,1)} %bitcast.9), channel_id=1, source_target_pairs={{0,16},{2,18},{4,20},{6,22},{8,24},{10,26},{12,28},{14,30},{16,0},... | collective-permute-start | bytes 196616 | tf_op jit(solution)/shard_map/ppermute | solution.py:312
  5.6 0.0 collective-permute-start.2
  5.6 0.0 copy-start.1
  5.6 1.8 %prep.1.refs_0_.refs_1_ = bf16[74,64,128]{2,1,0:T(8,128)(2,1)S(1)} custom-call(s32[1,64]{1,0:T(1,128)} %bitcast.13, bf16[70,64,128]{2,1,0:T(8,128)(2,1)} %bitcast.12), custom_call_target="tpu_custom_call" | custom-call | flops 2348810240 | bytes 2293760 | tf_op jit(solution)/shard_map/prep/pallas_call | solution.py:66
  7.4 0.0 collective-permute-done
  7.4 3.1 %collective-permute-done.1 = bf16[1,256,128]{2,1,0:T(8,128)(2,1)S(1)} collective-permute-done((bf16[1,256,128]{2,1,0:T(8,128)(2,1)}, bf16[1,256,128]{2,1,0:T(8,128)(2,1)S(1)}, u32[]{:S(2)}, u32[]{:S(2)}) %collective-permute-start.1) | collective-permute-done | bytes 65568 | tf_op jit(solution)/shard_map/ppermute | solution.py:312
  10.5 1.4 %collective-permute-done.2 = bf16[1,256,128]{2,1,0:T(8,128)(2,1)S(1)} collective-permute-done((bf16[1,256,128]{2,1,0:T(8,128)(2,1)}, bf16[1,256,128]{2,1,0:T(8,128)(2,1)S(1)}, u32[]{:S(2)}, u32[]{:S(2)}) %collective-permute-start.2) | collective-permute-done | bytes 65568 | tf_op jit(solution)/shard_map/ppermute | solution.py:312
  11.9 0.0 collective-permute-start.3
  11.9 0.1 sub.24.refs_0_
  12.1 0.0 copy-done.1
  12.1 1.6 %collective-permute-start.6 = (bf16[4,256,128]{2,1,0:T(8,128)(2,1)S(1)}, bf16[4,256,128]{2,1,0:T(8,128)(2,1)S(1)}, u32[]{:S(2)}, u32[]{:S(2)}) collective-permute-start(bf16[4,256,128]{2,1,0:T(8,128)(2,1)S(1)} %pad_maximum_fusion.refs_2_), channel_id=1, source_target_pairs={{0,4},{2,6},{4,0},{6,2},{8,12},{10,14},{12,8},{14,10},{16,20},{18,... | collective-permute-start | bytes 786440 | tf_op jit(solution)/shard_map/ppermute | solution.py:312
  13.7 1.5 %collective-permute-start.5 = (bf16[4,256,128]{2,1,0:T(8,128)(2,1)S(1)}, bf16[4,256,128]{2,1,0:T(8,128)(2,1)S(1)}, u32[]{:S(2)}, u32[]{:S(2)}) collective-permute-start(bf16[4,256,128]{2,1,0:T(8,128)(2,1)S(1)} %pad_maximum_fusion.refs_2_), channel_id=1, source_target_pairs={{0,2},{2,0},{4,6},{6,4},{8,10},{10,8},{12,14},{14,12},{16,18},{18,... | collective-permute-start | bytes 786440 | tf_op jit(solution)/shard_map/ppermute | solution.py:312
  15.2 0.5 %collective-permute-start.4 = (bf16[4,256,128]{2,1,0:T(8,128)(2,1)S(1)}, bf16[4,256,128]{2,1,0:T(8,128)(2,1)S(1)}, u32[]{:S(2)}, u32[]{:S(2)}) collective-permute-start(bf16[4,256,128]{2,1,0:T(8,128)(2,1)S(1)} %pad_maximum_fusion.refs_2_), channel_id=1, source_target_pairs={{0,6},{2,4},{4,2},{6,0},{8,14},{10,12},{12,10},{14,8},{16,22},{18,... | collective-permute-start | bytes 786440 | tf_op jit(solution)/shard_map/ppermute | solution.py:312
  15.6 0.0 collective-permute-done.3.refs_1_.refs_2_
  15.7 0.1 add_reduce_fusion
  15.8 4.7 %score.4.refs_4_ = f32[4,8,128]{2,1,0:T(8,128)S(1)} custom-call(s32[2]{0:T(128)S(1)} %fusion.counts_ref, bf16[74,64,128]{2,1,0:T(8,128)(2,1)S(1)} %prep.1.refs_0_.refs_1_, bf16[74,64,128]{2,1,0:T(8,128)(2,1)S(1)} %collective-permute-done.3.refs_1_.refs_2_, bf16[4,256,128]{2,1,0:T(8,128)(2,1)S(1)} %pad_maximum_fusion.refs_2_), custom_call_target="tpu_custom_call" | custom-call | flops 4966055936 | bytes 2424832 | tf_op jit(solution)/shard_map/score/pallas_call | solution.py:266
  20.5 0.4 collective-permute-done.6.refs_2_
  20.9 4.7 %score.6.refs_6_ = f32[4,8,128]{2,1,0:T(8,128)S(1)} custom-call(s32[2]{0:T(128)S(1)} %fusion.counts_ref, bf16[74,64,128]{2,1,0:T(8,128)(2,1)S(1)} %prep.1.refs_0_.refs_1_, bf16[74,64,128]{2,1,0:T(8,128)(2,1)S(1)} %collective-permute-done.3.refs_1_.refs_2_, bf16[4,256,128]{2,1,0:T(8,128)(2,1)S(1)} %collective-permute-done.6.refs_2_), custom_call_target="tpu_custom_call" | custom-call | flops 4966055936 | bytes 2424832 | tf_op jit(solution)/shard_map/score/pallas_call | solution.py:266
  25.6 0.0 collective-permute-done.5.refs_2_
  25.6 4.7 %score.5.refs_5_ = f32[4,8,128]{2,1,0:T(8,128)S(1)} custom-call(s32[2]{0:T(128)S(1)} %fusion.counts_ref, bf16[74,64,128]{2,1,0:T(8,128)(2,1)S(1)} %prep.1.refs_0_.refs_1_, bf16[74,64,128]{2,1,0:T(8,128)(2,1)S(1)} %collective-permute-done.3.refs_1_.refs_2_, bf16[4,256,128]{2,1,0:T(8,128)(2,1)S(1)} %collective-permute-done.5.refs_2_), custom_call_target="tpu_custom_call" | custom-call | flops 4966055936 | bytes 2424832 | tf_op jit(solution)/shard_map/score/pallas_call | solution.py:266
  30.3 0.0 copy-start.2
  30.3 0.0 copy-start
  30.3 0.0 collective-permute-done.4.refs_3_
  30.3 5.4 %score.7 = f32[16,8,128]{2,1,0:T(8,128)} custom-call(s32[2]{0:T(128)S(1)} %fusion.counts_ref, s32[16]{0:T(128)S(1)} %sub.24.refs_0_, bf16[74,64,128]{2,1,0:T(8,128)(2,1)S(1)} %prep.1.refs_0_.refs_1_, bf16[74,64,128]{2,1,0:T(8,128)(2,1)S(1)} %collective-permute-done.3.refs_1_.refs_2_, bf16[4,256,128]{2,1,0:T(8,128)(2,1)S(1)} %collective-permute-done.4.refs_3_, ...), custom_call_target="tpu_custom_call" | custom-call | flops 4966055936 | bytes 2424832 | tf_op jit(solution)/shard_map/score/pallas_call | solution.py:266
  35.7 7.0 %all-to-all-start = ((f32[16,8,128]{2,1,0:T(8,128)}), f32[16,8,128]{2,1,0:T(8,128)S(1)}, u32[]{:S(2)}, u32[]{:S(2)}) async-start(f32[16,8,128]{2,1,0:T(8,128)} %score.7), calls=%async_computation | async-start | bytes 131072 | tf_op jit(solution)/shard_map/all_to_all | solution.py:333
  42.7 0.0 copy-done.2
  42.7 2.9 %all-to-all-done.table_ref = f32[16,8,128]{2,1,0:T(8,128)S(1)} async-done(((f32[16,8,128]{2,1,0:T(8,128)}), f32[16,8,128]{2,1,0:T(8,128)S(1)}, u32[]{:S(2)}, u32[]{:S(2)}) %all-to-all-start) | async-done | bytes 65568 | tf_op jit(solution)/shard_map/all_to_all | solution.py:333
  45.6 0.0 copy-done
  45.6 0.7 %pick.1 = f32[8,256]{1,0:T(8,128)} custom-call(s32[1]{0:T(128)} %bitcast.core_ref, f32[16,8,128]{2,1,0:T(8,128)S(1)} %all-to-all-done.table_ref, s32[8,256]{1,0:T(8,128)S(1)} %bitcast.7, s32[8,256]{1,0:T(8,128)S(1)} %copy-done), custom_call_target="tpu_custom_call" | custom-call | tf_op jit(solution)/shard_map/pick/pallas_call | solution.py:337
  (7 shorter events, 0.1 us)
Async XLA Ops:
  0.0 7.4 %collective-permute-start = (bf16[1,256,128]{2,1,0:T(8,128)(2,1)}, bf16[1,256,128]{2,1,0:T(8,128)(2,1)S(1)}, u32[]{:S(2)}, u32[]{:S(2)}) collective-permute-start(bf16[1,256,128]{2,1,0:T(8,128)(2,1)} %bitcast.8), channel_id=1, source_target_pairs={{0,8},{2,10},{4,12},{6,14},{8,0},{10,2},{12,4},{14,6},{16,24},{18,... | collective-permute-start | bytes 196616 | tf_op jit(solution)/shard_map/ppermute | solution.py:312
  3.0 7.5 %collective-permute-start.1 = (bf16[1,256,128]{2,1,0:T(8,128)(2,1)}, bf16[1,256,128]{2,1,0:T(8,128)(2,1)S(1)}, u32[]{:S(2)}, u32[]{:S(2)}) collective-permute-start(bf16[1,256,128]{2,1,0:T(8,128)(2,1)} %bitcast.9), channel_id=1, source_target_pairs={{0,16},{2,18},{4,20},{6,22},{8,24},{10,26},{12,28},{14,30},{16,0},... | collective-permute-start | bytes 196616 | tf_op jit(solution)/shard_map/ppermute | solution.py:312
  5.6 6.3 %collective-permute-start.2 = (bf16[1,256,128]{2,1,0:T(8,128)(2,1)}, bf16[1,256,128]{2,1,0:T(8,128)(2,1)S(1)}, u32[]{:S(2)}, u32[]{:S(2)}) collective-permute-start(bf16[1,256,128]{2,1,0:T(8,128)(2,1)} %bitcast.10), channel_id=1, source_target_pairs={{0,24},{2,26},{4,28},{6,30},{8,16},{10,18},{12,20},{14,22},{16,8},... | collective-permute-start | bytes 196616 | tf_op jit(solution)/shard_map/ppermute | solution.py:312
  5.6 6.4 %copy-start.1 = (bf16[8,32,128]{2,1,0:T(8,128)(2,1)S(1)}, bf16[8,32,128]{2,1,0:T(8,128)(2,1)}, u32[]{:S(2)}) copy-start(bf16[8,32,128]{2,1,0:T(8,128)(2,1)} %param.5) | copy-start | bytes 196612
  11.9 3.7 %collective-permute-start.3 = (bf16[74,64,128]{2,1,0:T(8,128)(2,1)S(1)}, bf16[74,64,128]{2,1,0:T(8,128)(2,1)S(1)}, u32[]{:S(2)}, u32[]{:S(2)}) collective-permute-start(bf16[74,64,128]{2,1,0:T(8,128)(2,1)S(1)} %prep.1.refs_0_.refs_1_), channel_id=1, source_target_pairs={{0,1},{1,0},{2,3},{3,2},{4,5},{5,4},{6,7},{7,6},{8,9},{9,8},{10,11... | collective-permute-start | bytes 3637256 | tf_op jit(solution)/shard_map/ppermute | solution.py:325
  12.1 8.8 %collective-permute-start.6 = (bf16[4,256,128]{2,1,0:T(8,128)(2,1)S(1)}, bf16[4,256,128]{2,1,0:T(8,128)(2,1)S(1)}, u32[]{:S(2)}, u32[]{:S(2)}) collective-permute-start(bf16[4,256,128]{2,1,0:T(8,128)(2,1)S(1)} %pad_maximum_fusion.refs_2_), channel_id=1, source_target_pairs={{0,4},{2,6},{4,0},{6,2},{8,12},{10,14},{12,8},{14,10},{16,20},{18,... | collective-permute-start | bytes 786440 | tf_op jit(solution)/shard_map/ppermute | solution.py:312
  13.7 11.9 %collective-permute-start.5 = (bf16[4,256,128]{2,1,0:T(8,128)(2,1)S(1)}, bf16[4,256,128]{2,1,0:T(8,128)(2,1)S(1)}, u32[]{:S(2)}, u32[]{:S(2)}) collective-permute-start(bf16[4,256,128]{2,1,0:T(8,128)(2,1)S(1)} %pad_maximum_fusion.refs_2_), channel_id=1, source_target_pairs={{0,2},{2,0},{4,6},{6,4},{8,10},{10,8},{12,14},{14,12},{16,18},{18,... | collective-permute-start | bytes 786440 | tf_op jit(solution)/shard_map/ppermute | solution.py:312
  15.2 15.1 %collective-permute-start.4 = (bf16[4,256,128]{2,1,0:T(8,128)(2,1)S(1)}, bf16[4,256,128]{2,1,0:T(8,128)(2,1)S(1)}, u32[]{:S(2)}, u32[]{:S(2)}) collective-permute-start(bf16[4,256,128]{2,1,0:T(8,128)(2,1)S(1)} %pad_maximum_fusion.refs_2_), channel_id=1, source_target_pairs={{0,6},{2,4},{4,2},{6,0},{8,14},{10,12},{12,10},{14,8},{16,22},{18,... | collective-permute-start | bytes 786440 | tf_op jit(solution)/shard_map/ppermute | solution.py:312
  30.3 12.4 %copy-start.2 = (s32[8,256,1]{1,2,0:T(1,128)S(1)}, s32[8,256,1]{1,2,0:T(1,128)}, u32[]{:S(2)}) copy-start(s32[8,256,1]{1,2,0:T(1,128)} %param.6) | copy-start | bytes 24580
  30.3 15.3 %copy-start = (s32[8,256]{1,0:T(8,128)S(1)}, s32[8,256]{1,0:T(8,128)}, u32[]{:S(2)}) copy-start(s32[8,256]{1,0:T(8,128)} %local_ref.1) | copy-start | bytes 24580
  35.7 9.9 %all-to-all-start = ((f32[16,8,128]{2,1,0:T(8,128)}), f32[16,8,128]{2,1,0:T(8,128)S(1)}, u32[]{:S(2)}, u32[]{:S(2)}) async-start(f32[16,8,128]{2,1,0:T(8,128)} %score.7), calls=%async_computation | async-start | bytes 131072 | tf_op jit(solution)/shard_map/all_to_all | solution.py:333

commit v6 on v5

--- a/solution.py
+++ b/solution.py
@@ -11,7 +11,7 @@
 SMEM = pl.BlockSpec(memory_space=pltpu.SMEM)
 TOKENS = 32
 BLOCKS = 4
-GROUPS = 2
+GROUPS = 3
 CHUNK = 8
 LANES = 128
 ROWS = 128
@@ -25,8 +25,7 @@
     load_store.start()
     load_lengths.wait()
     slots, store, dim = passages_ref.shape
-    padded = out_ref.shape[0] - 2
-    per_core = store // GROUPS
+    quarter = store // 4
     shape = (store, 2 * store)
     lengths = lengths_ref[...]
     along = jnp.broadcast_to(jnp.concatenate([lengths, lengths], axis=1), shape)
@@ -52,20 +51,19 @@
         first = moved[0] if first is None else first
         for k in range(2):
             out_ref[t + k] = jnp.where(t + k < sorted_lengths, moved[k], first).astype(out_ref.dtype)
-    for t in range(slots, padded):
-        out_ref[t] = first.astype(out_ref.dtype)
-    place = rank + jnp.where(rank >= per_core, per_core, 0)
+    place = rank // quarter
+    place = jnp.where(place == 0, 3, jnp.where(place == 1, 1, jnp.where(place == 2, 0, 2)))
+    place = place * 2 * quarter + rank % quarter
     for k, value in enumerate((sorted_lengths, place)):
         value = jnp.broadcast_to(value, (store, dim)).astype(jnp.float32)
-        out_ref[padded + k] = value.astype(out_ref.dtype)
+        out_ref[slots + k] = value.astype(out_ref.dtype)
 
 
 def prep(passages, lengths):
     store, slots, dim = passages.shape
-    padded = -(-slots // CHUNK) * CHUNK
     return pl.pallas_call(
         prep_kernel,
-        out_shape=jax.ShapeDtypeStruct((padded + 2, store, dim), passages.dtype),
+        out_shape=jax.ShapeDtypeStruct((slots + 2, store, dim), passages.dtype),
         in_specs=[pl.BlockSpec(memory_space=pl.ANY)] * 2,
         out_specs=VMEM,
         scratch_shapes=[
@@ -73,7 +71,7 @@
             pltpu.VMEM((slots, store, dim), passages.dtype),
             pltpu.SemaphoreType.DMA((2,)),
         ],
-        compiler_params=pltpu.CompilerParams(vmem_limit_bytes=12 << 20),
+        compiler_params=pltpu.CompilerParams(vmem_limit_bytes=4 << 20),
         cost_estimate=pl.CostEstimate(
             flops=64 * passages.size * store, bytes_accessed=4 * passages.size, transcendentals=0
         ),
@@ -85,32 +83,41 @@
 
 
 def chunk_counts(own, sib):
-    per_core = own.shape[1] // GROUPS
-    longest = [plane[-2, ::per_core, 0].astype(jnp.int32) for plane in (own, sib)]
-    return jnp.maximum((jnp.maximum(*longest) + CHUNK - 1) // CHUNK, 2)
+    quarter = own.shape[1] // 4
+    longest = [plane[-2, ::quarter, 0].astype(jnp.int32) for plane in (own, sib)]
+    at_once = CHUNK * (1 + jnp.arange(4, dtype=jnp.int32) // 2)
+    counts = (jnp.maximum(*longest) + at_once - 1) // at_once
+    return jnp.maximum(counts, 2)
 
 
 def score_block(own_ref, sib_ref, read_rows, acc, sums, units, read_counts, write):
     half = acc[0].shape[1]
-    per_core = own_ref.shape[1] // GROUPS
-    width = 2 * per_core
-    per_tile = 2 * LANES // width
+    slots = own_ref.shape[0] - 2
+    quarter = own_ref.shape[1] // 4
+    width = 2 * quarter
     zeros = jnp.zeros((2 * LANES, LANES), own_ref.dtype)
 
     def where_of(step):
         if isinstance(step, int):
             return 0, step
-        group = (step >= counts[0]).astype(jnp.int32)
-        return group, step - group * counts[0]
+        third, fourth = counts[0], counts[0] + counts[2]
+        group = (step >= third).astype(jnp.int32) + (step >= fourth).astype(jnp.int32)
+        start = jnp.where(step >= fourth, fourth, jnp.where(step >= third, third, 0))
+        return group, step - start
 
     def push(step):
         group, at = where_of(step)
-        lanes = group * per_core
-        lanes = pl.ds(lanes if isinstance(group, int) else pl.multiple_of(lanes, per_core), per_core)
         for unit in range(2):
             parts = []
-            for k in range(per_tile):
-                slot = at * CHUNK + unit * per_tile + k
+            for k in range(CHUNK):
+                token, place = k // 2, (k + k // 2) % 2 * quarter
+                slot = at * CHUNK + unit * CHUNK // 2 + token
+                if not isinstance(step, int):
+                    short = at * 2 * CHUNK + unit * CHUNK + k
+                    slot = jnp.minimum(jnp.where(group == 0, slot, short), slots - 1)
+                    place = jnp.where(group == 0, place, (group + 1) * quarter)
+                    place = pl.multiple_of(place, quarter)
+                lanes = pl.ds(place, quarter)
                 parts += [own_ref[slot, lanes, :], sib_ref[slot, lanes, :]]
             tile = jnp.concatenate([jnp.concatenate(parts, axis=0), zeros], axis=1)
             pltpu.matmul_push_rhs(tile, 0, unit, transpose=True)
@@ -136,7 +143,7 @@
     stream(1, False)
     pop(1, 0)
     counts = read_counts()
-    last = counts[0] + counts[1] - 1
+    last = counts[0] + counts[2] + counts[3] - 1
     stream(0, True)
     push(jnp.minimum(last, 2))
     stream(1, False)
@@ -151,18 +158,23 @@
         return 0
 
     def finish(part):
-        _, at = where_of(last)
         fresh = [pltpu.matmul_pop(unit) for unit in units[part]]
         for start in range(0, half, ROWS):
-            take = slice(start, start + ROWS)
-            best = jnp.maximum(fresh[0][take], fresh[1][take])
-            best = jnp.maximum(jnp.where(at == 0, LOWEST, acc[part][GROUPS - 1, take]), best)
-            first = acc[part][0, take]
-            first = jnp.maximum(first[:, :LANES], first[:, LANES:])
-            second = jnp.maximum(best[:, :LANES], best[:, LANES:])
-            lane = lax.broadcasted_iota(jnp.int32, first.shape, 1) < width
-            turned = pltpu.roll(jnp.where(lane, second, first), width, 1)
-            best = jnp.maximum(jnp.where(lane, first, second), turned)
+            rows = slice(start, start + ROWS)
+            found = [acc[part][g, rows] for g in range(GROUPS)]
+            found[-1] = jnp.maximum(found[-1], jnp.maximum(fresh[0][rows], fresh[1][rows]))
+            long, third, fourth = [jnp.maximum(x[:, :LANES], x[:, LANES:]) for x in found]
+            lane = lax.broadcasted_iota(jnp.int32, long.shape, 1)
+            low = lane < 2 * width
+            even = lane // width % 2 == 0
+            short = jnp.maximum(
+                jnp.where(low, third, fourth),
+                pltpu.roll(jnp.where(low, fourth, third), 2 * width, 1),
+            )
+            best = jnp.maximum(
+                jnp.where(even, short, long),
+                pltpu.roll(jnp.where(even, long, short), LANES - width, 1),
+            )
             partial = best.reshape(ROWS // TOKENS, TOKENS // 8, 8, LANES).sum(axis=1)
             spot = start * 8 // TOKENS
             sums[part, spot : spot + ROWS * 8 // TOKENS] = partial.reshape(-1, LANES)
@@ -195,7 +207,7 @@
     local = rows // TOKENS
     half = step * rows // 2
     planes, store, _ = own_ref.shape
-    per_core = store // GROUPS
+    quarter = store // 4
     flat_ref = blocks_ref.reshape(blocks * rows, dim)
     at = sum(piece.shape[0] for piece in pieces)
     waited, placed = [], []
@@ -213,13 +225,13 @@
     def read_counts():
         if not waited:
             waited.append(load_counts.wait())
-        return [counts_here[g] for g in range(GROUPS)]
+        return [counts_here[g] for g in range(4)]
 
     lane = lax.broadcasted_iota(jnp.int32, (16, LANES), 1)
     position = jnp.where(
         lane < store,
         own_ref[planes - 1, :16].astype(jnp.float32),
-        sib_ref[planes - 1, :16].astype(jnp.float32) + per_core,
+        sib_ref[planes - 1, :16].astype(jnp.float32) + quarter,
     ).astype(jnp.int32)[:1]
 
     def run(*units):
@@ -263,6 +275,8 @@
     scalars = [counts] if ids is None else [counts, ids]
     operands = [own, sib, blocks, *earlier]
     total = count + sum(piece.shape[0] for piece in earlier)
+    held = sum(x.size * x.dtype.itemsize for x in operands) + total * local * LANES * 4
+    held += 2 * GROUPS * half * 2 * LANES * 4
     return pl.pallas_call(
         functools.partial(score_kernel, first, len(earlier)),
         out_shape=jax.ShapeDtypeStruct((total, local, 2 * own.shape[1]), jnp.float32),
@@ -277,7 +291,7 @@
             pltpu.SMEM((total,), jnp.int32),
             pltpu.SemaphoreType.DMA((2,)),
         ],
-        compiler_params=pltpu.CompilerParams(vmem_limit_bytes=12 << 20),
+        compiler_params=pltpu.CompilerParams(vmem_limit_bytes=held + (1 << 20)),
         cost_estimate=pl.CostEstimate(
             flops=8 * count * blocks[0].size * own.shape[0] * own.shape[1],
             bytes_accessed=4 * own.size,

time: 46.2 us -> 46.1 us (level)
  Pallas kernels: 21.9 us -> 21.3 us
    pallas_call x4, Pallas kernels: 19.4 us -> 18.8 us  [score(): pl.pallas_call(functools.partial(score_kernel, first, len(earlier)), out_...]
  transfers between devices with their start and end apart: 8 -> 8, of which waited for: 4 -> 4; matrix products, arithmetic and copies ran while one was open for 1% -> 1% of each run, Pallas kernels for 34% -> 33%
where the time goes in v6:
time: 46.1 us; the launch traced here: 45.9 us
  Pallas kernels  21.3 us (46%)
  starting transfers between devices  16.2 us (35%)
  waiting for transfers between devices  7.89 us (17%)
    pallas_call x4, Pallas kernels, score(): pl.pallas_call(functools.partial(score_kernel, first, len(earlier)), out_...  18.8 us
    ppermute x6, starting transfers between devices, swap(): return lax.ppermute(a, 'psg', [(i, i ^ bits) for i in range(chips)])  9.17 us
    all_to_all x1, starting transfers between devices, body(): lax.all_to_all(table, 'psg', split_axis=0, concat_axis=0, tiled=True, axi...  7.01 us
    ppermute x6, waiting for transfers between devices, swap(): return lax.ppermute(a, 'psg', [(i, i ^ bits) for i in range(chips)])  4.95 us
    all_to_all x1, waiting for transfers between devices, body(): lax.all_to_all(table, 'psg', split_axis=0, concat_axis=0, tiled=True, axi...  2.94 us
    pallas_call x1, Pallas kernels, prep(): pl.pallas_call(prep_kernel, out_shape=jax.ShapeDtypeStruct((slots + 2, st...  1.78 us
  transfers between devices with their start and end apart: 8, of which 4 were waited for; matrix products, arithmetic and copies ran while one was open for 1% of the time, Pallas kernels for 33%

profile of v6, /device:TPU:0, one launch (start us, length us, event | category | flops | bytes accessed | tf_op | source)
XLA Modules:
  0.0 45.9 jit_solution(3186944961758808698)
XLA Ops:
  0.0 3.0 %collective-permute-start = (bf16[1,256,128]{2,1,0:T(8,128)(2,1)}, bf16[1,256,128]{2,1,0:T(8,128)(2,1)S(1)}, u32[]{:S(2)}, u32[]{:S(2)}) collective-permute-start(bf16[1,256,128]{2,1,0:T(8,128)(2,1)} %bitcast.8), channel_id=1, source_target_pairs={{0,8},{2,10},{4,12},{6,14},{8,0},{10,2},{12,4},{14,6},{16,24},{18,... | collective-permute-start | bytes 196616 | tf_op jit(solution)/shard_map/ppermute | solution.py:326
  3.0 2.6 %collective-permute-start.1 = (bf16[1,256,128]{2,1,0:T(8,128)(2,1)}, bf16[1,256,128]{2,1,0:T(8,128)(2,1)S(1)}, u32[]{:S(2)}, u32[]{:S(2)}) collective-permute-start(bf16[1,256,128]{2,1,0:T(8,128)(2,1)} %bitcast.9), channel_id=1, source_target_pairs={{0,16},{2,18},{4,20},{6,22},{8,24},{10,26},{12,28},{14,30},{16,0},... | collective-permute-start | bytes 196616 | tf_op jit(solution)/shard_map/ppermute | solution.py:326
  5.6 0.0 collective-permute-start.2
  5.6 0.0 copy-start.1
  5.6 1.8 %prep.1.refs_0_.refs_1_ = bf16[72,64,128]{2,1,0:T(8,128)(2,1)S(1)} custom-call(s32[1,64]{1,0:T(1,128)} %bitcast.13, bf16[70,64,128]{2,1,0:T(8,128)(2,1)} %bitcast.12), custom_call_target="tpu_custom_call" | custom-call | flops 2348810240 | bytes 2293760 | tf_op jit(solution)/shard_map/prep/pallas_call | solution.py:64
  7.4 0.0 collective-permute-done
  7.4 3.1 %collective-permute-done.1 = bf16[1,256,128]{2,1,0:T(8,128)(2,1)S(1)} collective-permute-done((bf16[1,256,128]{2,1,0:T(8,128)(2,1)}, bf16[1,256,128]{2,1,0:T(8,128)(2,1)S(1)}, u32[]{:S(2)}, u32[]{:S(2)}) %collective-permute-start.1) | collective-permute-done | bytes 65568 | tf_op jit(solution)/shard_map/ppermute | solution.py:326
  10.5 1.4 %collective-permute-done.2 = bf16[1,256,128]{2,1,0:T(8,128)(2,1)S(1)} collective-permute-done((bf16[1,256,128]{2,1,0:T(8,128)(2,1)}, bf16[1,256,128]{2,1,0:T(8,128)(2,1)S(1)}, u32[]{:S(2)}, u32[]{:S(2)}) %collective-permute-start.2) | collective-permute-done | bytes 65568 | tf_op jit(solution)/shard_map/ppermute | solution.py:326
  11.9 0.0 collective-permute-start.3
  11.9 0.1 sub.26.refs_0_
  12.1 0.0 copy-done.1
  12.1 1.6 %collective-permute-start.6 = (bf16[4,256,128]{2,1,0:T(8,128)(2,1)S(1)}, bf16[4,256,128]{2,1,0:T(8,128)(2,1)S(1)}, u32[]{:S(2)}, u32[]{:S(2)}) collective-permute-start(bf16[4,256,128]{2,1,0:T(8,128)(2,1)S(1)} %pad_maximum_fusion.refs_2_), channel_id=1, source_target_pairs={{0,4},{2,6},{4,0},{6,2},{8,12},{10,14},{12,8},{14,10},{16,20},{18,... | collective-permute-start | bytes 786440 | tf_op jit(solution)/shard_map/ppermute | solution.py:326
  13.7 1.5 %collective-permute-start.5 = (bf16[4,256,128]{2,1,0:T(8,128)(2,1)S(1)}, bf16[4,256,128]{2,1,0:T(8,128)(2,1)S(1)}, u32[]{:S(2)}, u32[]{:S(2)}) collective-permute-start(bf16[4,256,128]{2,1,0:T(8,128)(2,1)S(1)} %pad_maximum_fusion.refs_2_), channel_id=1, source_target_pairs={{0,2},{2,0},{4,6},{6,4},{8,10},{10,8},{12,14},{14,12},{16,18},{18,... | collective-permute-start | bytes 786440 | tf_op jit(solution)/shard_map/ppermute | solution.py:326
  15.2 0.5 %collective-permute-start.4 = (bf16[4,256,128]{2,1,0:T(8,128)(2,1)S(1)}, bf16[4,256,128]{2,1,0:T(8,128)(2,1)S(1)}, u32[]{:S(2)}, u32[]{:S(2)}) collective-permute-start(bf16[4,256,128]{2,1,0:T(8,128)(2,1)S(1)} %pad_maximum_fusion.refs_2_), channel_id=1, source_target_pairs={{0,6},{2,4},{4,2},{6,0},{8,14},{10,12},{12,10},{14,8},{16,22},{18,... | collective-permute-start | bytes 786440 | tf_op jit(solution)/shard_map/ppermute | solution.py:326
  15.6 0.0 collective-permute-done.3.refs_1_.refs_2_
  15.7 0.1 maximum_reduce_fusion
  15.8 0.1 fusion.2.counts_ref
  15.9 4.5 %score.4.refs_4_ = f32[4,8,128]{2,1,0:T(8,128)S(1)} custom-call(s32[4]{0:T(128)S(1)} %fusion.2.counts_ref, bf16[72,64,128]{2,1,0:T(8,128)(2,1)S(1)} %prep.1.refs_0_.refs_1_, bf16[72,64,128]{2,1,0:T(8,128)(2,1)S(1)} %collective-permute-done.3.refs_1_.refs_2_, bf16[4,256,128]{2,1,0:T(8,128)(2,1)S(1)} %pad_maximum_fusion.refs_2_), custom_call_target="tpu_custom_call" | custom-call | flops 4831838208 | bytes 2359296 | tf_op jit(solution)/shard_map/score/pallas_call | solution.py:280
  20.4 0.4 collective-permute-done.6.refs_2_
  20.9 4.5 %score.6.refs_6_ = f32[4,8,128]{2,1,0:T(8,128)S(1)} custom-call(s32[4]{0:T(128)S(1)} %fusion.2.counts_ref, bf16[72,64,128]{2,1,0:T(8,128)(2,1)S(1)} %prep.1.refs_0_.refs_1_, bf16[72,64,128]{2,1,0:T(8,128)(2,1)S(1)} %collective-permute-done.3.refs_1_.refs_2_, bf16[4,256,128]{2,1,0:T(8,128)(2,1)S(1)} %collective-permute-done.6.refs_2_), custom_call_target="tpu_custom_call" | custom-call | flops 4831838208 | bytes 2359296 | tf_op jit(solution)/shard_map/score/pallas_call | solution.py:280
  25.4 0.0 collective-permute-done.5.refs_2_
  25.4 4.5 %score.5.refs_5_ = f32[4,8,128]{2,1,0:T(8,128)S(1)} custom-call(s32[4]{0:T(128)S(1)} %fusion.2.counts_ref, bf16[72,64,128]{2,1,0:T(8,128)(2,1)S(1)} %prep.1.refs_0_.refs_1_, bf16[72,64,128]{2,1,0:T(8,128)(2,1)S(1)} %collective-permute-done.3.refs_1_.refs_2_, bf16[4,256,128]{2,1,0:T(8,128)(2,1)S(1)} %collective-permute-done.5.refs_2_), custom_call_target="tpu_custom_call" | custom-call | flops 4831838208 | bytes 2359296 | tf_op jit(solution)/shard_map/score/pallas_call | solution.py:280
  30.0 0.0 copy-start.2
  30.0 0.0 copy-start
  30.0 0.0 collective-permute-done.4.refs_3_
  30.0 5.2 %score.7 = f32[16,8,128]{2,1,0:T(8,128)} custom-call(s32[4]{0:T(128)S(1)} %fusion.2.counts_ref, s32[16]{0:T(128)S(1)} %sub.26.refs_0_, bf16[72,64,128]{2,1,0:T(8,128)(2,1)S(1)} %prep.1.refs_0_.refs_1_, bf16[72,64,128]{2,1,0:T(8,128)(2,1)S(1)} %collective-permute-done.3.refs_1_.refs_2_, bf16[4,256,128]{2,1,0:T(8,128)(2,1)S(1)} %collective-permute-done.4.refs_3_, ...), custom_call_target="tpu_custom_call" | custom-call | flops 4831838208 | bytes 2359296 | tf_op jit(solution)/shard_map/score/pallas_call | solution.py:280
  35.2 7.0 %all-to-all-start = ((f32[16,8,128]{2,1,0:T(8,128)}), f32[16,8,128]{2,1,0:T(8,128)S(1)}, u32[]{:S(2)}, u32[]{:S(2)}) async-start(f32[16,8,128]{2,1,0:T(8,128)} %score.7), calls=%async_computation | async-start | bytes 131072 | tf_op jit(solution)/shard_map/all_to_all | solution.py:347
  42.2 0.0 copy-done.2
  42.3 2.9 %all-to-all-done.table_ref = f32[16,8,128]{2,1,0:T(8,128)S(1)} async-done(((f32[16,8,128]{2,1,0:T(8,128)}), f32[16,8,128]{2,1,0:T(8,128)S(1)}, u32[]{:S(2)}, u32[]{:S(2)}) %all-to-all-start) | async-done | bytes 65568 | tf_op jit(solution)/shard_map/all_to_all | solution.py:347
  45.2 0.0 copy-done
  45.2 0.7 %pick.1 = f32[8,256]{1,0:T(8,128)} custom-call(s32[1]{0:T(128)} %bitcast.core_ref, f32[16,8,128]{2,1,0:T(8,128)S(1)} %all-to-all-done.table_ref, s32[8,256]{1,0:T(8,128)S(1)} %bitcast.7, s32[8,256]{1,0:T(8,128)S(1)} %copy-done), custom_call_target="tpu_custom_call" | custom-call | tf_op jit(solution)/shard_map/pick/pallas_call | solution.py:351
  (6 shorter events, 0.1 us)
Async XLA Ops:
  0.0 7.4 %collective-permute-start = (bf16[1,256,128]{2,1,0:T(8,128)(2,1)}, bf16[1,256,128]{2,1,0:T(8,128)(2,1)S(1)}, u32[]{:S(2)}, u32[]{:S(2)}) collective-permute-start(bf16[1,256,128]{2,1,0:T(8,128)(2,1)} %bitcast.8), channel_id=1, source_target_pairs={{0,8},{2,10},{4,12},{6,14},{8,0},{10,2},{12,4},{14,6},{16,24},{18,... | collective-permute-start | bytes 196616 | tf_op jit(solution)/shard_map/ppermute | solution.py:326
  3.0 7.5 %collective-permute-start.1 = (bf16[1,256,128]{2,1,0:T(8,128)(2,1)}, bf16[1,256,128]{2,1,0:T(8,128)(2,1)S(1)}, u32[]{:S(2)}, u32[]{:S(2)}) collective-permute-start(bf16[1,256,128]{2,1,0:T(8,128)(2,1)} %bitcast.9), channel_id=1, source_target_pairs={{0,16},{2,18},{4,20},{6,22},{8,24},{10,26},{12,28},{14,30},{16,0},... | collective-permute-start | bytes 196616 | tf_op jit(solution)/shard_map/ppermute | solution.py:326
  5.6 6.3 %collective-permute-start.2 = (bf16[1,256,128]{2,1,0:T(8,128)(2,1)}, bf16[1,256,128]{2,1,0:T(8,128)(2,1)S(1)}, u32[]{:S(2)}, u32[]{:S(2)}) collective-permute-start(bf16[1,256,128]{2,1,0:T(8,128)(2,1)} %bitcast.10), channel_id=1, source_target_pairs={{0,24},{2,26},{4,28},{6,30},{8,16},{10,18},{12,20},{14,22},{16,8},... | collective-permute-start | bytes 196616 | tf_op jit(solution)/shard_map/ppermute | solution.py:326
  5.6 6.4 %copy-start.1 = (bf16[8,32,128]{2,1,0:T(8,128)(2,1)S(1)}, bf16[8,32,128]{2,1,0:T(8,128)(2,1)}, u32[]{:S(2)}) copy-start(bf16[8,32,128]{2,1,0:T(8,128)(2,1)} %param.5) | copy-start | bytes 196612
  11.9 3.7 %collective-permute-start.3 = (bf16[72,64,128]{2,1,0:T(8,128)(2,1)S(1)}, bf16[72,64,128]{2,1,0:T(8,128)(2,1)S(1)}, u32[]{:S(2)}, u32[]{:S(2)}) collective-permute-start(bf16[72,64,128]{2,1,0:T(8,128)(2,1)S(1)} %prep.1.refs_0_.refs_1_), channel_id=1, source_target_pairs={{0,1},{1,0},{2,3},{3,2},{4,5},{5,4},{6,7},{7,6},{8,9},{9,8},{10,11... | collective-permute-start | bytes 3538952 | tf_op jit(solution)/shard_map/ppermute | solution.py:339
  12.1 8.8 %collective-permute-start.6 = (bf16[4,256,128]{2,1,0:T(8,128)(2,1)S(1)}, bf16[4,256,128]{2,1,0:T(8,128)(2,1)S(1)}, u32[]{:S(2)}, u32[]{:S(2)}) collective-permute-start(bf16[4,256,128]{2,1,0:T(8,128)(2,1)S(1)} %pad_maximum_fusion.refs_2_), channel_id=1, source_target_pairs={{0,4},{2,6},{4,0},{6,2},{8,12},{10,14},{12,8},{14,10},{16,20},{18,... | collective-permute-start | bytes 786440 | tf_op jit(solution)/shard_map/ppermute | solution.py:326
  13.7 11.7 %collective-permute-start.5 = (bf16[4,256,128]{2,1,0:T(8,128)(2,1)S(1)}, bf16[4,256,128]{2,1,0:T(8,128)(2,1)S(1)}, u32[]{:S(2)}, u32[]{:S(2)}) collective-permute-start(bf16[4,256,128]{2,1,0:T(8,128)(2,1)S(1)} %pad_maximum_fusion.refs_2_), channel_id=1, source_target_pairs={{0,2},{2,0},{4,6},{6,4},{8,10},{10,8},{12,14},{14,12},{16,18},{18,... | collective-permute-start | bytes 786440 | tf_op jit(solution)/shard_map/ppermute | solution.py:326
  15.2 14.8 %collective-permute-start.4 = (bf16[4,256,128]{2,1,0:T(8,128)(2,1)S(1)}, bf16[4,256,128]{2,1,0:T(8,128)(2,1)S(1)}, u32[]{:S(2)}, u32[]{:S(2)}) collective-permute-start(bf16[4,256,128]{2,1,0:T(8,128)(2,1)S(1)} %pad_maximum_fusion.refs_2_), channel_id=1, source_target_pairs={{0,6},{2,4},{4,2},{6,0},{8,14},{10,12},{12,10},{14,8},{16,22},{18,... | collective-permute-start | bytes 786440 | tf_op jit(solution)/shard_map/ppermute | solution.py:326
  30.0 12.3 %copy-start.2 = (s32[8,256,1]{1,2,0:T(1,128)S(1)}, s32[8,256,1]{1,2,0:T(1,128)}, u32[]{:S(2)}) copy-start(s32[8,256,1]{1,2,0:T(1,128)} %param.6) | copy-start | bytes 24580
  30.0 15.2 %copy-start = (s32[8,256]{1,0:T(8,128)S(1)}, s32[8,256]{1,0:T(8,128)}, u32[]{:S(2)}) copy-start(s32[8,256]{1,0:T(8,128)} %local_ref.1) | copy-start | bytes 24580
  35.2 10.0 %all-to-all-start = ((f32[16,8,128]{2,1,0:T(8,128)}), f32[16,8,128]{2,1,0:T(8,128)S(1)}, u32[]{:S(2)}, u32[]{:S(2)}) async-start(f32[16,8,128]{2,1,0:T(8,128)} %score.7), calls=%async_computation | async-start | bytes 131072 | tf_op jit(solution)/shard_map/all_to_all | solution.py:347

commit v7 on v6

--- a/solution.py
+++ b/solution.py
@@ -328,7 +328,7 @@
     own = prep(passages, lengths)
     rows = queries.reshape(1, local * qlen, dim)
     if chips == 16:
-        others = [swap(rows, z) for z in (4, 8, 12)]
+        others = [swap(rows, z) for z in (12, 4, 8)]
         own, *others = lax.optimization_barrier((own, *others))
         column = jnp.concatenate([rows] + others, axis=0)
     else:
@@ -338,7 +338,8 @@
             bit *= 2
     sib = lax.ppermute(own, "qry", [(0, 1), (1, 0)])
     counts = chunk_counts(own, sib)
-    ids = (jnp.arange(0, chips, 4)[None, :] ^ jnp.arange(4)[:, None]).astype(jnp.int32) ^ me
+    near = jnp.array([0, 12, 4, 8]) if chips == 16 else jnp.arange(0, chips, 4)
+    ids = (near[None, :] ^ jnp.arange(4)[:, None]).astype(jnp.int32) ^ me
     beside = [column] + [swap(column, k) for k in (1, 2, 3)]
     pieces = [score(counts, own, sib, column)]
     pieces += [score(counts, own, sib, beside[k]) for k in (1, 2)]

time: 46.1 us -> 45.5 us (0.987)
  waiting for transfers between devices: 7.89 us -> 6.82 us
    ppermute x6, waiting for transfers between devices: 4.95 us -> 3.93 us  [swap(): return lax.ppermute(a, 'psg', [(i, i ^ bits) for i in range(chips)])]
  transfers between devices with their start and end apart: 8 -> 8, of which waited for: 4 -> 5; matrix products, arithmetic and copies ran while one was open for 1% -> 1% of each run, Pallas kernels for 33% -> 34%
where the time goes in v7:
time: 45.5 us; the launch traced here: 45.3 us
  Pallas kernels  21.3 us (47%)
  starting transfers between devices  16.6 us (36%)
  waiting for transfers between devices  6.82 us (15%)
    pallas_call x4, Pallas kernels, score(): pl.pallas_call(functools.partial(score_kernel, first, len(earlier)), out_...  18.8 us
    ppermute x6, starting transfers between devices, swap(): return lax.ppermute(a, 'psg', [(i, i ^ bits) for i in range(chips)])  9.17 us
    all_to_all x1, starting transfers between devices, body(): lax.all_to_all(table, 'psg', split_axis=0, concat_axis=0, tiled=True, axi...  7.43 us
    ppermute x6, waiting for transfers between devices, swap(): return lax.ppermute(a, 'psg', [(i, i ^ bits) for i in range(chips)])  3.93 us
    all_to_all x1, waiting for transfers between devices, body(): lax.all_to_all(table, 'psg', split_axis=0, concat_axis=0, tiled=True, axi...  2.88 us
    pallas_call x1, Pallas kernels, prep(): pl.pallas_call(prep_kernel, out_shape=jax.ShapeDtypeStruct((slots + 2, st...  1.78 us
  transfers between devices with their start and end apart: 8, of which 5 were waited for; matrix products, arithmetic and copies ran while one was open for 1% of the time, Pallas kernels for 34%

profile of v7, /device:TPU:0, one launch (start us, length us, event | category | flops | bytes accessed | tf_op | source)
XLA Modules:
  0.0 45.3 jit_solution(10587868817045197793)
XLA Ops:
  0.0 5.0 %collective-permute-start = (bf16[1,256,128]{2,1,0:T(8,128)(2,1)}, bf16[1,256,128]{2,1,0:T(8,128)(2,1)S(1)}, u32[]{:S(2)}, u32[]{:S(2)}) collective-permute-start(bf16[1,256,128]{2,1,0:T(8,128)(2,1)} %bitcast.8), channel_id=1, source_target_pairs={{0,24},{2,26},{4,28},{6,30},{8,16},{10,18},{12,20},{14,22},{16,8},... | collective-permute-start | bytes 196616 | tf_op jit(solution)/shard_map/ppermute | solution.py:326
  5.0 0.0 collective-permute-start.1
  5.1 0.6 %collective-permute-start.2 = (bf16[1,256,128]{2,1,0:T(8,128)(2,1)}, bf16[1,256,128]{2,1,0:T(8,128)(2,1)S(1)}, u32[]{:S(2)}, u32[]{:S(2)}) collective-permute-start(bf16[1,256,128]{2,1,0:T(8,128)(2,1)} %bitcast.10), channel_id=1, source_target_pairs={{0,16},{2,18},{4,20},{6,22},{8,24},{10,26},{12,28},{14,30},{16,0},... | collective-permute-start | bytes 196616 | tf_op jit(solution)/shard_map/ppermute | solution.py:326
  5.6 0.0 copy-start.3
  5.6 0.0 copy-start.1
  5.6 1.8 %prep.1.refs_0_.refs_1_ = bf16[72,64,128]{2,1,0:T(8,128)(2,1)S(1)} custom-call(s32[1,64]{1,0:T(1,128)} %bitcast.13, bf16[70,64,128]{2,1,0:T(8,128)(2,1)} %bitcast.12), custom_call_target="tpu_custom_call" | custom-call | flops 2348810240 | bytes 2293760 | tf_op jit(solution)/shard_map/prep/pallas_call | solution.py:64
  7.4 0.7 %collective-permute-done = bf16[1,256,128]{2,1,0:T(8,128)(2,1)S(1)} collective-permute-done((bf16[1,256,128]{2,1,0:T(8,128)(2,1)}, bf16[1,256,128]{2,1,0:T(8,128)(2,1)S(1)}, u32[]{:S(2)}, u32[]{:S(2)}) %collective-permute-start) | collective-permute-done | bytes 65568 | tf_op jit(solution)/shard_map/ppermute | solution.py:326
  8.2 1.8 %collective-permute-done.1 = bf16[1,256,128]{2,1,0:T(8,128)(2,1)S(1)} collective-permute-done((bf16[1,256,128]{2,1,0:T(8,128)(2,1)}, bf16[1,256,128]{2,1,0:T(8,128)(2,1)S(1)}, u32[]{:S(2)}, u32[]{:S(2)}) %collective-permute-start.1) | collective-permute-done | bytes 65568 | tf_op jit(solution)/shard_map/ppermute | solution.py:326
  9.9 1.0 %collective-permute-done.2 = bf16[1,256,128]{2,1,0:T(8,128)(2,1)S(1)} collective-permute-done((bf16[1,256,128]{2,1,0:T(8,128)(2,1)}, bf16[1,256,128]{2,1,0:T(8,128)(2,1)S(1)}, u32[]{:S(2)}, u32[]{:S(2)}) %collective-permute-start.2) | collective-permute-done | bytes 65568 | tf_op jit(solution)/shard_map/ppermute | solution.py:326
  10.9 0.0 collective-permute-start.3
  10.9 0.0 copy-done.3
  10.9 0.1 sub.26.refs_0_
  11.0 0.0 copy-done.1
  11.1 1.6 %collective-permute-start.6 = (bf16[4,256,128]{2,1,0:T(8,128)(2,1)S(1)}, bf16[4,256,128]{2,1,0:T(8,128)(2,1)S(1)}, u32[]{:S(2)}, u32[]{:S(2)}) collective-permute-start(bf16[4,256,128]{2,1,0:T(8,128)(2,1)S(1)} %pad_maximum_fusion.refs_2_), channel_id=1, source_target_pairs={{0,4},{2,6},{4,0},{6,2},{8,12},{10,14},{12,8},{14,10},{16,20},{18,... | collective-permute-start | bytes 786440 | tf_op jit(solution)/shard_map/ppermute | solution.py:326
  12.7 1.5 %collective-permute-start.5 = (bf16[4,256,128]{2,1,0:T(8,128)(2,1)S(1)}, bf16[4,256,128]{2,1,0:T(8,128)(2,1)S(1)}, u32[]{:S(2)}, u32[]{:S(2)}) collective-permute-start(bf16[4,256,128]{2,1,0:T(8,128)(2,1)S(1)} %pad_maximum_fusion.refs_2_), channel_id=1, source_target_pairs={{0,2},{2,0},{4,6},{6,4},{8,10},{10,8},{12,14},{14,12},{16,18},{18,... | collective-permute-start | bytes 786440 | tf_op jit(solution)/shard_map/ppermute | solution.py:326
  14.1 0.5 %collective-permute-start.4 = (bf16[4,256,128]{2,1,0:T(8,128)(2,1)S(1)}, bf16[4,256,128]{2,1,0:T(8,128)(2,1)S(1)}, u32[]{:S(2)}, u32[]{:S(2)}) collective-permute-start(bf16[4,256,128]{2,1,0:T(8,128)(2,1)S(1)} %pad_maximum_fusion.refs_2_), channel_id=1, source_target_pairs={{0,6},{2,4},{4,2},{6,0},{8,14},{10,12},{12,10},{14,8},{16,22},{18,... | collective-permute-start | bytes 786440 | tf_op jit(solution)/shard_map/ppermute | solution.py:326
  14.6 0.0 collective-permute-done.3.refs_1_.refs_2_
  14.7 0.1 maximum_reduce_fusion
  14.8 0.1 fusion.2.counts_ref
  14.9 4.5 %score.4.refs_4_ = f32[4,8,128]{2,1,0:T(8,128)S(1)} custom-call(s32[4]{0:T(128)S(1)} %fusion.2.counts_ref, bf16[72,64,128]{2,1,0:T(8,128)(2,1)S(1)} %prep.1.refs_0_.refs_1_, bf16[72,64,128]{2,1,0:T(8,128)(2,1)S(1)} %collective-permute-done.3.refs_1_.refs_2_, bf16[4,256,128]{2,1,0:T(8,128)(2,1)S(1)} %pad_maximum_fusion.refs_2_), custom_call_target="tpu_custom_call" | custom-call | flops 4831838208 | bytes 2359296 | tf_op jit(solution)/shard_map/score/pallas_call | solution.py:280
  19.4 0.4 collective-permute-done.6.refs_2_
  19.9 4.5 %score.6.refs_6_ = f32[4,8,128]{2,1,0:T(8,128)S(1)} custom-call(s32[4]{0:T(128)S(1)} %fusion.2.counts_ref, bf16[72,64,128]{2,1,0:T(8,128)(2,1)S(1)} %prep.1.refs_0_.refs_1_, bf16[72,64,128]{2,1,0:T(8,128)(2,1)S(1)} %collective-permute-done.3.refs_1_.refs_2_, bf16[4,256,128]{2,1,0:T(8,128)(2,1)S(1)} %collective-permute-done.6.refs_2_), custom_call_target="tpu_custom_call" | custom-call | flops 4831838208 | bytes 2359296 | tf_op jit(solution)/shard_map/score/pallas_call | solution.py:280
  24.4 0.0 collective-permute-done.5.refs_2_
  24.4 4.5 %score.5.refs_5_ = f32[4,8,128]{2,1,0:T(8,128)S(1)} custom-call(s32[4]{0:T(128)S(1)} %fusion.2.counts_ref, bf16[72,64,128]{2,1,0:T(8,128)(2,1)S(1)} %prep.1.refs_0_.refs_1_, bf16[72,64,128]{2,1,0:T(8,128)(2,1)S(1)} %collective-permute-done.3.refs_1_.refs_2_, bf16[4,256,128]{2,1,0:T(8,128)(2,1)S(1)} %collective-permute-done.5.refs_2_), custom_call_target="tpu_custom_call" | custom-call | flops 4831838208 | bytes 2359296 | tf_op jit(solution)/shard_map/score/pallas_call | solution.py:280
  28.9 0.0 copy-start.2
  28.9 0.0 copy-start
  29.0 0.0 collective-permute-done.4.refs_3_
  29.0 5.2 %score.7 = f32[16,8,128]{2,1,0:T(8,128)} custom-call(s32[4]{0:T(128)S(1)} %fusion.2.counts_ref, s32[16]{0:T(128)S(1)} %sub.26.refs_0_, bf16[72,64,128]{2,1,0:T(8,128)(2,1)S(1)} %prep.1.refs_0_.refs_1_, bf16[72,64,128]{2,1,0:T(8,128)(2,1)S(1)} %collective-permute-done.3.refs_1_.refs_2_, bf16[4,256,128]{2,1,0:T(8,128)(2,1)S(1)} %collective-permute-done.4.refs_3_, ...), custom_call_target="tpu_custom_call" | custom-call | flops 4831838208 | bytes 2359296 | tf_op jit(solution)/shard_map/score/pallas_call | solution.py:280
  34.2 7.4 %all-to-all-start = ((f32[16,8,128]{2,1,0:T(8,128)}), f32[16,8,128]{2,1,0:T(8,128)S(1)}, u32[]{:S(2)}, u32[]{:S(2)}) async-start(f32[16,8,128]{2,1,0:T(8,128)} %score.7), calls=%async_computation | async-start | bytes 131072 | tf_op jit(solution)/shard_map/all_to_all | solution.py:348
  41.6 0.0 copy-done.2
  41.7 2.9 %all-to-all-done.table_ref = f32[16,8,128]{2,1,0:T(8,128)S(1)} async-done(((f32[16,8,128]{2,1,0:T(8,128)}), f32[16,8,128]{2,1,0:T(8,128)S(1)}, u32[]{:S(2)}, u32[]{:S(2)}) %all-to-all-start) | async-done | bytes 65568 | tf_op jit(solution)/shard_map/all_to_all | solution.py:348
  44.5 0.0 copy-done
  44.6 0.7 %pick.1 = f32[8,256]{1,0:T(8,128)} custom-call(s32[1]{0:T(128)} %bitcast.core_ref, f32[16,8,128]{2,1,0:T(8,128)S(1)} %all-to-all-done.table_ref, s32[8,256]{1,0:T(8,128)S(1)} %bitcast.7, s32[8,256]{1,0:T(8,128)S(1)} %copy-done), custom_call_target="tpu_custom_call" | custom-call | tf_op jit(solution)/shard_map/pick/pallas_call | solution.py:352
  (5 shorter events, 0.1 us)
Async XLA Ops:
  0.0 8.2 %collective-permute-start = (bf16[1,256,128]{2,1,0:T(8,128)(2,1)}, bf16[1,256,128]{2,1,0:T(8,128)(2,1)S(1)}, u32[]{:S(2)}, u32[]{:S(2)}) collective-permute-start(bf16[1,256,128]{2,1,0:T(8,128)(2,1)} %bitcast.8), channel_id=1, source_target_pairs={{0,24},{2,26},{4,28},{6,30},{8,16},{10,18},{12,20},{14,22},{16,8},... | collective-permute-start | bytes 196616 | tf_op jit(solution)/shard_map/ppermute | solution.py:326
  5.0 4.9 %collective-permute-start.1 = (bf16[1,256,128]{2,1,0:T(8,128)(2,1)}, bf16[1,256,128]{2,1,0:T(8,128)(2,1)S(1)}, u32[]{:S(2)}, u32[]{:S(2)}) collective-permute-start(bf16[1,256,128]{2,1,0:T(8,128)(2,1)} %bitcast.9), channel_id=1, source_target_pairs={{0,8},{2,10},{4,12},{6,14},{8,0},{10,2},{12,4},{14,6},{16,24},{18,... | collective-permute-start | bytes 196616 | tf_op jit(solution)/shard_map/ppermute | solution.py:326
  5.1 5.8 %collective-permute-start.2 = (bf16[1,256,128]{2,1,0:T(8,128)(2,1)}, bf16[1,256,128]{2,1,0:T(8,128)(2,1)S(1)}, u32[]{:S(2)}, u32[]{:S(2)}) collective-permute-start(bf16[1,256,128]{2,1,0:T(8,128)(2,1)} %bitcast.10), channel_id=1, source_target_pairs={{0,16},{2,18},{4,20},{6,22},{8,24},{10,26},{12,28},{14,30},{16,0},... | collective-permute-start | bytes 196616 | tf_op jit(solution)/shard_map/ppermute | solution.py:326
  5.6 5.3 %copy-start.3 = (s32[4]{0:T(128)S(1)}, s32[4]{0:T(128)}, u32[]{:S(2)}) copy-start(s32[4]{0:T(128)} %constant.39.clone) | copy-start | bytes 52
  5.6 5.4 %copy-start.1 = (bf16[8,32,128]{2,1,0:T(8,128)(2,1)S(1)}, bf16[8,32,128]{2,1,0:T(8,128)(2,1)}, u32[]{:S(2)}) copy-start(bf16[8,32,128]{2,1,0:T(8,128)(2,1)} %param.6) | copy-start | bytes 196612
  10.9 3.7 %collective-permute-start.3 = (bf16[72,64,128]{2,1,0:T(8,128)(2,1)S(1)}, bf16[72,64,128]{2,1,0:T(8,128)(2,1)S(1)}, u32[]{:S(2)}, u32[]{:S(2)}) collective-permute-start(bf16[72,64,128]{2,1,0:T(8,128)(2,1)S(1)} %prep.1.refs_0_.refs_1_), channel_id=1, source_target_pairs={{0,1},{1,0},{2,3},{3,2},{4,5},{5,4},{6,7},{7,6},{8,9},{9,8},{10,11... | collective-permute-start | bytes 3538952 | tf_op jit(solution)/shard_map/ppermute | solution.py:339
  11.1 8.8 %collective-permute-start.6 = (bf16[4,256,128]{2,1,0:T(8,128)(2,1)S(1)}, bf16[4,256,128]{2,1,0:T(8,128)(2,1)S(1)}, u32[]{:S(2)}, u32[]{:S(2)}) collective-permute-start(bf16[4,256,128]{2,1,0:T(8,128)(2,1)S(1)} %pad_maximum_fusion.refs_2_), channel_id=1, source_target_pairs={{0,4},{2,6},{4,0},{6,2},{8,12},{10,14},{12,8},{14,10},{16,20},{18,... | collective-permute-start | bytes 786440 | tf_op jit(solution)/shard_map/ppermute | solution.py:326
  12.7 11.7 %collective-permute-start.5 = (bf16[4,256,128]{2,1,0:T(8,128)(2,1)S(1)}, bf16[4,256,128]{2,1,0:T(8,128)(2,1)S(1)}, u32[]{:S(2)}, u32[]{:S(2)}) collective-permute-start(bf16[4,256,128]{2,1,0:T(8,128)(2,1)S(1)} %pad_maximum_fusion.refs_2_), channel_id=1, source_target_pairs={{0,2},{2,0},{4,6},{6,4},{8,10},{10,8},{12,14},{14,12},{16,18},{18,... | collective-permute-start | bytes 786440 | tf_op jit(solution)/shard_map/ppermute | solution.py:326
  14.1 14.8 %collective-permute-start.4 = (bf16[4,256,128]{2,1,0:T(8,128)(2,1)S(1)}, bf16[4,256,128]{2,1,0:T(8,128)(2,1)S(1)}, u32[]{:S(2)}, u32[]{:S(2)}) collective-permute-start(bf16[4,256,128]{2,1,0:T(8,128)(2,1)S(1)} %pad_maximum_fusion.refs_2_), channel_id=1, source_target_pairs={{0,6},{2,4},{4,2},{6,0},{8,14},{10,12},{12,10},{14,8},{16,22},{18,... | collective-permute-start | bytes 786440 | tf_op jit(solution)/shard_map/ppermute | solution.py:326
  28.9 12.7 %copy-start.2 = (s32[8,256,1]{1,2,0:T(1,128)S(1)}, s32[8,256,1]{1,2,0:T(1,128)}, u32[]{:S(2)}) copy-start(s32[8,256,1]{1,2,0:T(1,128)} %param.7) | copy-start | bytes 24580
  28.9 15.6 %copy-start = (s32[8,256]{1,0:T(8,128)S(1)}, s32[8,256]{1,0:T(8,128)}, u32[]{:S(2)}) copy-start(s32[8,256]{1,0:T(8,128)} %local_ref.1) | copy-start | bytes 24580
  34.2 10.3 %all-to-all-start = ((f32[16,8,128]{2,1,0:T(8,128)}), f32[16,8,128]{2,1,0:T(8,128)S(1)}, u32[]{:S(2)}, u32[]{:S(2)}) async-start(f32[16,8,128]{2,1,0:T(8,128)} %score.7), calls=%async_computation | async-start | bytes 131072 | tf_op jit(solution)/shard_map/all_to_all | solution.py:348

commit v8 on v7

--- a/solution.py
+++ b/solution.py
@@ -85,8 +85,8 @@
 def chunk_counts(own, sib):
     quarter = own.shape[1] // 4
     longest = [plane[-2, ::quarter, 0].astype(jnp.int32) for plane in (own, sib)]
-    at_once = CHUNK * (1 + jnp.arange(4, dtype=jnp.int32) // 2)
-    counts = (jnp.maximum(*longest) + at_once - 1) // at_once
+    halves = 2 - (jnp.arange(4, dtype=jnp.int32) >> 1)
+    counts = (jnp.maximum(*longest) * halves + 2 * CHUNK - 1) // (2 * CHUNK)
     return jnp.maximum(counts, 2)
 
 

time: 45.5 us -> 46.1 us (1.013)
  starting transfers between devices: 16.6 us -> 17.5 us
    all_to_all x1, starting transfers between devices: 7.43 us -> 8.28 us  [body(): lax.all_to_all(table, 'psg', split_axis=0, concat_axis=0, tiled=True, axi...]
  transfers between devices with their start and end apart: 8 -> 8, of which waited for: 5 -> 5; matrix products, arithmetic and copies ran while one was open for 1% -> 1% of each run, Pallas kernels for 34% -> 33%
where the time goes in v8:
time: 46.1 us
  Pallas kernels  21.3 us (46%)
  starting transfers between devices  17.5 us (38%)
  waiting for transfers between devices  6.95 us (15%)
    pallas_call x4, Pallas kernels, score(): pl.pallas_call(functools.partial(score_kernel, first, len(earlier)), out_...  18.8 us
    ppermute x6, starting transfers between devices, swap(): return lax.ppermute(a, 'psg', [(i, i ^ bits) for i in range(chips)])  9.17 us
    all_to_all x1, starting transfers between devices, body(): lax.all_to_all(table, 'psg', split_axis=0, concat_axis=0, tiled=True, axi...  8.28 us
    ppermute x6, waiting for transfers between devices, swap(): return lax.ppermute(a, 'psg', [(i, i ^ bits) for i in range(chips)])  4.06 us
    all_to_all x1, waiting for transfers between devices, body(): lax.all_to_all(table, 'psg', split_axis=0, concat_axis=0, tiled=True, axi...  2.88 us
    pallas_call x1, Pallas kernels, prep(): pl.pallas_call(prep_kernel, out_shape=jax.ShapeDtypeStruct((slots + 2, st...  1.78 us
  transfers between devices with their start and end apart: 8, of which 5 were waited for; matrix products, arithmetic and copies ran while one was open for 1% of the time, Pallas kernels for 33%

profile of v8, /device:TPU:0, one launch (start us, length us, event | category | flops | bytes accessed | tf_op | source)
XLA Modules:
  0.0 46.1 jit_solution(15162000728015400587)
XLA Ops:
  0.0 5.0 %collective-permute-start = (bf16[1,256,128]{2,1,0:T(8,128)(2,1)}, bf16[1,256,128]{2,1,0:T(8,128)(2,1)S(1)}, u32[]{:S(2)}, u32[]{:S(2)}) collective-permute-start(bf16[1,256,128]{2,1,0:T(8,128)(2,1)} %bitcast.8), channel_id=1, source_target_pairs={{0,24},{2,26},{4,28},{6,30},{8,16},{10,18},{12,20},{14,22},{16,8},... | collective-permute-start | bytes 196616 | tf_op jit(solution)/shard_map/ppermute | solution.py:326
  5.0 0.0 collective-permute-start.1
  5.1 0.6 %collective-permute-start.2 = (bf16[1,256,128]{2,1,0:T(8,128)(2,1)}, bf16[1,256,128]{2,1,0:T(8,128)(2,1)S(1)}, u32[]{:S(2)}, u32[]{:S(2)}) collective-permute-start(bf16[1,256,128]{2,1,0:T(8,128)(2,1)} %bitcast.10), channel_id=1, source_target_pairs={{0,16},{2,18},{4,20},{6,22},{8,24},{10,26},{12,28},{14,30},{16,0},... | collective-permute-start | bytes 196616 | tf_op jit(solution)/shard_map/ppermute | solution.py:326
  5.6 0.0 copy-start.3
  5.6 0.0 copy-start.1
  5.6 1.8 %prep.1.refs_0_.refs_1_ = bf16[72,64,128]{2,1,0:T(8,128)(2,1)S(1)} custom-call(s32[1,64]{1,0:T(1,128)} %bitcast.13, bf16[70,64,128]{2,1,0:T(8,128)(2,1)} %bitcast.12), custom_call_target="tpu_custom_call" | custom-call | flops 2348810240 | bytes 2293760 | tf_op jit(solution)/shard_map/prep/pallas_call | solution.py:64
  7.4 0.7 %collective-permute-done = bf16[1,256,128]{2,1,0:T(8,128)(2,1)S(1)} collective-permute-done((bf16[1,256,128]{2,1,0:T(8,128)(2,1)}, bf16[1,256,128]{2,1,0:T(8,128)(2,1)S(1)}, u32[]{:S(2)}, u32[]{:S(2)}) %collective-permute-start) | collective-permute-done | bytes 65568 | tf_op jit(solution)/shard_map/ppermute | solution.py:326
  8.2 1.8 %collective-permute-done.1 = bf16[1,256,128]{2,1,0:T(8,128)(2,1)S(1)} collective-permute-done((bf16[1,256,128]{2,1,0:T(8,128)(2,1)}, bf16[1,256,128]{2,1,0:T(8,128)(2,1)S(1)}, u32[]{:S(2)}, u32[]{:S(2)}) %collective-permute-start.1) | collective-permute-done | bytes 65568 | tf_op jit(solution)/shard_map/ppermute | solution.py:326
  9.9 1.0 %collective-permute-done.2 = bf16[1,256,128]{2,1,0:T(8,128)(2,1)S(1)} collective-permute-done((bf16[1,256,128]{2,1,0:T(8,128)(2,1)}, bf16[1,256,128]{2,1,0:T(8,128)(2,1)S(1)}, u32[]{:S(2)}, u32[]{:S(2)}) %collective-permute-start.2) | collective-permute-done | bytes 65568 | tf_op jit(solution)/shard_map/ppermute | solution.py:326
  10.9 0.0 collective-permute-start.3
  10.9 0.0 copy-done.3
  10.9 0.1 sub.22.refs_0_
  11.0 0.0 copy-done.1
  11.1 1.6 %collective-permute-start.6 = (bf16[4,256,128]{2,1,0:T(8,128)(2,1)S(1)}, bf16[4,256,128]{2,1,0:T(8,128)(2,1)S(1)}, u32[]{:S(2)}, u32[]{:S(2)}) collective-permute-start(bf16[4,256,128]{2,1,0:T(8,128)(2,1)S(1)} %pad_maximum_fusion.refs_2_), channel_id=1, source_target_pairs={{0,4},{2,6},{4,0},{6,2},{8,12},{10,14},{12,8},{14,10},{16,20},{18,... | collective-permute-start | bytes 786440 | tf_op jit(solution)/shard_map/ppermute | solution.py:326
  12.7 1.5 %collective-permute-start.5 = (bf16[4,256,128]{2,1,0:T(8,128)(2,1)S(1)}, bf16[4,256,128]{2,1,0:T(8,128)(2,1)S(1)}, u32[]{:S(2)}, u32[]{:S(2)}) collective-permute-start(bf16[4,256,128]{2,1,0:T(8,128)(2,1)S(1)} %pad_maximum_fusion.refs_2_), channel_id=1, source_target_pairs={{0,2},{2,0},{4,6},{6,4},{8,10},{10,8},{12,14},{14,12},{16,18},{18,... | collective-permute-start | bytes 786440 | tf_op jit(solution)/shard_map/ppermute | solution.py:326
  14.1 0.5 %collective-permute-start.4 = (bf16[4,256,128]{2,1,0:T(8,128)(2,1)S(1)}, bf16[4,256,128]{2,1,0:T(8,128)(2,1)S(1)}, u32[]{:S(2)}, u32[]{:S(2)}) collective-permute-start(bf16[4,256,128]{2,1,0:T(8,128)(2,1)S(1)} %pad_maximum_fusion.refs_2_), channel_id=1, source_target_pairs={{0,6},{2,4},{4,2},{6,0},{8,14},{10,12},{12,10},{14,8},{16,22},{18,... | collective-permute-start | bytes 786440 | tf_op jit(solution)/shard_map/ppermute | solution.py:326
  14.6 0.0 collective-permute-done.3.refs_1_.refs_2_
  14.7 0.1 maximum_reduce_fusion
  14.8 4.5 %score.4.refs_4_ = f32[4,8,128]{2,1,0:T(8,128)S(1)} custom-call(s32[4]{0:T(128)S(1)} %fusion.counts_ref, bf16[72,64,128]{2,1,0:T(8,128)(2,1)S(1)} %prep.1.refs_0_.refs_1_, bf16[72,64,128]{2,1,0:T(8,128)(2,1)S(1)} %collective-permute-done.3.refs_1_.refs_2_, bf16[4,256,128]{2,1,0:T(8,128)(2,1)S(1)} %pad_maximum_fusion.refs_2_), custom_call_target="tpu_custom_call" | custom-call | flops 4831838208 | bytes 2359296 | tf_op jit(solution)/shard_map/score/pallas_call | solution.py:280
  19.3 0.6 %collective-permute-done.6.refs_2_ = bf16[4,256,128]{2,1,0:T(8,128)(2,1)S(1)} collective-permute-done((bf16[4,256,128]{2,1,0:T(8,128)(2,1)S(1)}, bf16[4,256,128]{2,1,0:T(8,128)(2,1)S(1)}, u32[]{:S(2)}, u32[]{:S(2)}) %collective-permute-start.6) | collective-permute-done | bytes 262176 | tf_op jit(solution)/shard_map/ppermute | solution.py:326
  19.9 4.5 %score.6.refs_6_ = f32[4,8,128]{2,1,0:T(8,128)S(1)} custom-call(s32[4]{0:T(128)S(1)} %fusion.counts_ref, bf16[72,64,128]{2,1,0:T(8,128)(2,1)S(1)} %prep.1.refs_0_.refs_1_, bf16[72,64,128]{2,1,0:T(8,128)(2,1)S(1)} %collective-permute-done.3.refs_1_.refs_2_, bf16[4,256,128]{2,1,0:T(8,128)(2,1)S(1)} %collective-permute-done.6.refs_2_), custom_call_target="tpu_custom_call" | custom-call | flops 4831838208 | bytes 2359296 | tf_op jit(solution)/shard_map/score/pallas_call | solution.py:280
  24.4 0.0 collective-permute-done.5.refs_2_
  24.4 4.5 %score.5.refs_5_ = f32[4,8,128]{2,1,0:T(8,128)S(1)} custom-call(s32[4]{0:T(128)S(1)} %fusion.counts_ref, bf16[72,64,128]{2,1,0:T(8,128)(2,1)S(1)} %prep.1.refs_0_.refs_1_, bf16[72,64,128]{2,1,0:T(8,128)(2,1)S(1)} %collective-permute-done.3.refs_1_.refs_2_, bf16[4,256,128]{2,1,0:T(8,128)(2,1)S(1)} %collective-permute-done.5.refs_2_), custom_call_target="tpu_custom_call" | custom-call | flops 4831838208 | bytes 2359296 | tf_op jit(solution)/shard_map/score/pallas_call | solution.py:280
  28.9 0.0 copy-start.2
  28.9 0.0 copy-start
  29.0 0.0 collective-permute-done.4.refs_3_
  29.0 5.2 %score.7 = f32[16,8,128]{2,1,0:T(8,128)} custom-call(s32[4]{0:T(128)S(1)} %fusion.counts_ref, s32[16]{0:T(128)S(1)} %sub.22.refs_0_, bf16[72,64,128]{2,1,0:T(8,128)(2,1)S(1)} %prep.1.refs_0_.refs_1_, bf16[72,64,128]{2,1,0:T(8,128)(2,1)S(1)} %collective-permute-done.3.refs_1_.refs_2_, bf16[4,256,128]{2,1,0:T(8,128)(2,1)S(1)} %collective-permute-done.4.refs_3_, ...), custom_call_target="tpu_custom_call" | custom-call | flops 4831838208 | bytes 2359296 | tf_op jit(solution)/shard_map/score/pallas_call | solution.py:280
  34.2 8.3 %all-to-all-start = ((f32[16,8,128]{2,1,0:T(8,128)}), f32[16,8,128]{2,1,0:T(8,128)S(1)}, u32[]{:S(2)}, u32[]{:S(2)}) async-start(f32[16,8,128]{2,1,0:T(8,128)} %score.7), calls=%async_computation | async-start | bytes 131072 | tf_op jit(solution)/shard_map/all_to_all | solution.py:348
  42.5 0.0 copy-done.2
  42.5 2.9 %all-to-all-done.table_ref = f32[16,8,128]{2,1,0:T(8,128)S(1)} async-done(((f32[16,8,128]{2,1,0:T(8,128)}), f32[16,8,128]{2,1,0:T(8,128)S(1)}, u32[]{:S(2)}, u32[]{:S(2)}) %all-to-all-start) | async-done | bytes 65568 | tf_op jit(solution)/shard_map/all_to_all | solution.py:348
  45.4 0.0 copy-done
  45.4 0.7 %pick.1 = f32[8,256]{1,0:T(8,128)} custom-call(s32[1]{0:T(128)} %bitcast.core_ref, f32[16,8,128]{2,1,0:T(8,128)S(1)} %all-to-all-done.table_ref, s32[8,256]{1,0:T(8,128)S(1)} %bitcast.7, s32[8,256]{1,0:T(8,128)S(1)} %copy-done), custom_call_target="tpu_custom_call" | custom-call | tf_op jit(solution)/shard_map/pick/pallas_call | solution.py:352
  (6 shorter events, 0.1 us)
Async XLA Ops:
  0.0 8.2 %collective-permute-start = (bf16[1,256,128]{2,1,0:T(8,128)(2,1)}, bf16[1,256,128]{2,1,0:T(8,128)(2,1)S(1)}, u32[]{:S(2)}, u32[]{:S(2)}) collective-permute-start(bf16[1,256,128]{2,1,0:T(8,128)(2,1)} %bitcast.8), channel_id=1, source_target_pairs={{0,24},{2,26},{4,28},{6,30},{8,16},{10,18},{12,20},{14,22},{16,8},... | collective-permute-start | bytes 196616 | tf_op jit(solution)/shard_map/ppermute | solution.py:326
  5.0 4.9 %collective-permute-start.1 = (bf16[1,256,128]{2,1,0:T(8,128)(2,1)}, bf16[1,256,128]{2,1,0:T(8,128)(2,1)S(1)}, u32[]{:S(2)}, u32[]{:S(2)}) collective-permute-start(bf16[1,256,128]{2,1,0:T(8,128)(2,1)} %bitcast.9), channel_id=1, source_target_pairs={{0,8},{2,10},{4,12},{6,14},{8,0},{10,2},{12,4},{14,6},{16,24},{18,... | collective-permute-start | bytes 196616 | tf_op jit(solution)/shard_map/ppermute | solution.py:326
  5.1 5.8 %collective-permute-start.2 = (bf16[1,256,128]{2,1,0:T(8,128)(2,1)}, bf16[1,256,128]{2,1,0:T(8,128)(2,1)S(1)}, u32[]{:S(2)}, u32[]{:S(2)}) collective-permute-start(bf16[1,256,128]{2,1,0:T(8,128)(2,1)} %bitcast.10), channel_id=1, source_target_pairs={{0,16},{2,18},{4,20},{6,22},{8,24},{10,26},{12,28},{14,30},{16,0},... | collective-permute-start | bytes 196616 | tf_op jit(solution)/shard_map/ppermute | solution.py:326
  5.6 5.3 %copy-start.3 = (s32[4]{0:T(128)S(1)}, s32[4]{0:T(128)}, u32[]{:S(2)}) copy-start(s32[4]{0:T(128)} %constant.33.clone) | copy-start | bytes 52
  5.6 5.4 %copy-start.1 = (bf16[8,32,128]{2,1,0:T(8,128)(2,1)S(1)}, bf16[8,32,128]{2,1,0:T(8,128)(2,1)}, u32[]{:S(2)}) copy-start(bf16[8,32,128]{2,1,0:T(8,128)(2,1)} %param.6) | copy-start | bytes 196612
  10.9 3.7 %collective-permute-start.3 = (bf16[72,64,128]{2,1,0:T(8,128)(2,1)S(1)}, bf16[72,64,128]{2,1,0:T(8,128)(2,1)S(1)}, u32[]{:S(2)}, u32[]{:S(2)}) collective-permute-start(bf16[72,64,128]{2,1,0:T(8,128)(2,1)S(1)} %prep.1.refs_0_.refs_1_), channel_id=1, source_target_pairs={{0,1},{1,0},{2,3},{3,2},{4,5},{5,4},{6,7},{7,6},{8,9},{9,8},{10,11... | collective-permute-start | bytes 3538952 | tf_op jit(solution)/shard_map/ppermute | solution.py:339
  11.1 8.8 %collective-permute-start.6 = (bf16[4,256,128]{2,1,0:T(8,128)(2,1)S(1)}, bf16[4,256,128]{2,1,0:T(8,128)(2,1)S(1)}, u32[]{:S(2)}, u32[]{:S(2)}) collective-permute-start(bf16[4,256,128]{2,1,0:T(8,128)(2,1)S(1)} %pad_maximum_fusion.refs_2_), channel_id=1, source_target_pairs={{0,4},{2,6},{4,0},{6,2},{8,12},{10,14},{12,8},{14,10},{16,20},{18,... | collective-permute-start | bytes 786440 | tf_op jit(solution)/shard_map/ppermute | solution.py:326
  12.7 11.7 %collective-permute-start.5 = (bf16[4,256,128]{2,1,0:T(8,128)(2,1)S(1)}, bf16[4,256,128]{2,1,0:T(8,128)(2,1)S(1)}, u32[]{:S(2)}, u32[]{:S(2)}) collective-permute-start(bf16[4,256,128]{2,1,0:T(8,128)(2,1)S(1)} %pad_maximum_fusion.refs_2_), channel_id=1, source_target_pairs={{0,2},{2,0},{4,6},{6,4},{8,10},{10,8},{12,14},{14,12},{16,18},{18,... | collective-permute-start | bytes 786440 | tf_op jit(solution)/shard_map/ppermute | solution.py:326
  14.1 14.8 %collective-permute-start.4 = (bf16[4,256,128]{2,1,0:T(8,128)(2,1)S(1)}, bf16[4,256,128]{2,1,0:T(8,128)(2,1)S(1)}, u32[]{:S(2)}, u32[]{:S(2)}) collective-permute-start(bf16[4,256,128]{2,1,0:T(8,128)(2,1)S(1)} %pad_maximum_fusion.refs_2_), channel_id=1, source_target_pairs={{0,6},{2,4},{4,2},{6,0},{8,14},{10,12},{12,10},{14,8},{16,22},{18,... | collective-permute-start | bytes 786440 | tf_op jit(solution)/shard_map/ppermute | solution.py:326
  28.9 13.6 %copy-start.2 = (s32[8,256,1]{1,2,0:T(1,128)S(1)}, s32[8,256,1]{1,2,0:T(1,128)}, u32[]{:S(2)}) copy-start(s32[8,256,1]{1,2,0:T(1,128)} %param.7) | copy-start | bytes 24580
  28.9 16.5 %copy-start = (s32[8,256]{1,0:T(8,128)S(1)}, s32[8,256]{1,0:T(8,128)}, u32[]{:S(2)}) copy-start(s32[8,256]{1,0:T(8,128)} %local_ref.1) | copy-start | bytes 24580
  34.2 11.2 %all-to-all-start = ((f32[16,8,128]{2,1,0:T(8,128)}), f32[16,8,128]{2,1,0:T(8,128)S(1)}, u32[]{:S(2)}, u32[]{:S(2)}) async-start(f32[16,8,128]{2,1,0:T(8,128)} %score.7), calls=%async_computation | async-start | bytes 131072 | tf_op jit(solution)/shard_map/all_to_all | solution.py:348

commit v9 on v8

--- a/solution.py
+++ b/solution.py
@@ -191,17 +191,12 @@
     finish(1)
 
 
-def score_kernel(first, earlier, counts_ref, *refs):
-    if earlier:
-        ids_ref, *refs = refs
+def score_kernel(first, earlier, rows_of, counts_ref, *refs):
     own_ref, sib_ref, blocks_ref, *refs = refs
     pieces, refs = refs[:earlier], refs[earlier:]
-    out_ref, acc_0, acc_1, sums, scores, counts_here, ids_here, arrived = refs
+    out_ref, acc_0, acc_1, sums, scores, counts_here, arrived = refs
     load_counts = pltpu.make_async_copy(counts_ref, counts_here, arrived.at[0])
     load_counts.start()
-    if earlier:
-        load_ids = pltpu.make_async_copy(ids_ref, ids_here, arrived.at[1])
-        load_ids.start()
     blocks, rows, dim = blocks_ref.shape
     step = min(blocks - first, BLOCKS)
     local = rows // TOKENS
@@ -212,14 +207,17 @@
     at = sum(piece.shape[0] for piece in pieces)
     waited, placed = [], []
 
+    def row_of(spot):
+        return rows_of(lax.axis_index("psg"), spot)
+
     def receive():
         if placed:
             return
-        placed.append(load_ids.wait())
+        placed.append(True)
         spot = 0
         for piece in pieces:
             for block in range(piece.shape[0]):
-                out_ref[ids_here[spot]] = piece[block]
+                out_ref[row_of(spot)] = piece[block]
                 spot += 1
 
     def read_counts():
@@ -253,7 +251,7 @@
             if earlier:
                 receive()
             for block in range(step):
-                spot = ids_here[at + start + block] if earlier else start + block
+                spot = row_of(at + start + block) if earlier else start + block
                 out_ref[spot] = scores[block * local : (block + 1) * local]
 
         if blocks - first == step:
@@ -267,18 +265,18 @@
     pl.run_scoped(run, *[pltpu.ACC(unit)((half, 2 * LANES), jnp.float32) for unit in (0, 1, 0, 1)])
 
 
-def score(counts, own, sib, blocks, first=0, ids=None, earlier=()):
+def score(counts, own, sib, blocks, first=0, rows_of=None, earlier=()):
     count = blocks.shape[0] - first
     step = min(count, BLOCKS)
     half = step * blocks.shape[1] // 2
     local = blocks.shape[1] // TOKENS
-    scalars = [counts] if ids is None else [counts, ids]
+    scalars = [counts]
     operands = [own, sib, blocks, *earlier]
     total = count + sum(piece.shape[0] for piece in earlier)
     held = sum(x.size * x.dtype.itemsize for x in operands) + total * local * LANES * 4
     held += 2 * GROUPS * half * 2 * LANES * 4
     return pl.pallas_call(
-        functools.partial(score_kernel, first, len(earlier)),
+        functools.partial(score_kernel, first, len(earlier), rows_of),
         out_shape=jax.ShapeDtypeStruct((total, local, 2 * own.shape[1]), jnp.float32),
         in_specs=[pl.BlockSpec(memory_space=pl.ANY)] * len(scalars) + [VMEM] * len(operands),
         out_specs=VMEM,
@@ -288,8 +286,7 @@
             pltpu.VMEM((2, half * 8 // TOKENS, LANES), jnp.float32),
             pltpu.VMEM((step * local, LANES), jnp.float32),
             pltpu.SMEM(counts.shape, jnp.int32),
-            pltpu.SMEM((total,), jnp.int32),
-            pltpu.SemaphoreType.DMA((2,)),
+            pltpu.SemaphoreType.DMA((1,)),
         ],
         compiler_params=pltpu.CompilerParams(vmem_limit_bytes=held + (1 << 20)),
         cost_estimate=pl.CostEstimate(
@@ -317,7 +314,6 @@
 
 
 def body(queries, cand_shard, cand_local, passages, lengths):
-    me = lax.axis_index("psg").astype(jnp.int32)
     core = lax.axis_index("qry").reshape(1).astype(jnp.int32)
     chips = lax.axis_size("psg")
     local, qlen, dim = queries.shape
@@ -338,13 +334,17 @@
             bit *= 2
     sib = lax.ppermute(own, "qry", [(0, 1), (1, 0)])
     counts = chunk_counts(own, sib)
-    near = jnp.array([0, 12, 4, 8]) if chips == 16 else jnp.arange(0, chips, 4)
-    ids = (near[None, :] ^ jnp.arange(4)[:, None]).astype(jnp.int32) ^ me
+    near = [0, 12, 4, 8] if chips == 16 else list(range(0, chips, 4))
+
+    def rows_of(chip, spot):
+        if isinstance(spot, int):
+            return chips - 1 - (chip ^ (near[spot % len(near)] ^ (spot // len(near))))
+        return chips - 1 - (chip ^ (spot % len(near) * 4) ^ (spot // len(near)))
+
     beside = [column] + [swap(column, k) for k in (1, 2, 3)]
     pieces = [score(counts, own, sib, column)]
     pieces += [score(counts, own, sib, beside[k]) for k in (1, 2)]
-    ids = chips - 1 - ids.reshape(-1)
-    table = score(counts, own, sib, beside[3], ids=ids, earlier=pieces)
+    table = score(counts, own, sib, beside[3], rows_of=rows_of, earlier=pieces)
     returned = lax.all_to_all(
         table, "psg", split_axis=0, concat_axis=0, tiled=True,
         axis_index_groups=[list(reversed(range(chips)))],

time: 46.1 us -> 45.4 us (0.985)
  starting transfers between devices: 17.5 us -> 16.6 us
    all_to_all x1, starting transfers between devices: 8.28 us -> 7.42 us  [body(): lax.all_to_all(table, 'psg', split_axis=0, concat_axis=0, tiled=True, axi...]
  transfers between devices with their start and end apart: 8 -> 8, of which waited for: 5 -> 5; matrix products, arithmetic and copies ran while one was open for 1% -> 1% of each run, Pallas kernels for 33% -> 34%
where the time goes in v9:
time: 45.4 us; the launch traced here: 45.2 us
  Pallas kernels  21.3 us (47%)
  starting transfers between devices  16.6 us (37%)
  waiting for transfers between devices  6.95 us (15%)
    pallas_call x4, Pallas kernels, score(): pl.pallas_call(functools.partial(score_kernel, first, len(earlier), rows_...  18.8 us
    ppermute x6, starting transfers between devices, swap(): return lax.ppermute(a, 'psg', [(i, i ^ bits) for i in range(chips)])  9.17 us
    all_to_all x1, starting transfers between devices, body(): lax.all_to_all(table, 'psg', split_axis=0, concat_axis=0, tiled=True, axi...  7.42 us
    ppermute x6, waiting for transfers between devices, swap(): return lax.ppermute(a, 'psg', [(i, i ^ bits) for i in range(chips)])  4.06 us
    all_to_all x1, waiting for transfers between devices, body(): lax.all_to_all(table, 'psg', split_axis=0, concat_axis=0, tiled=True, axi...  2.88 us
    pallas_call x1, Pallas kernels, prep(): pl.pallas_call(prep_kernel, out_shape=jax.ShapeDtypeStruct((slots + 2, st...  1.78 us
  transfers between devices with their start and end apart: 8, of which 5 were waited for; matrix products, arithmetic and copies ran while one was open for 1% of the time, Pallas kernels for 34%

profile of v9, /device:TPU:0, one launch (start us, length us, event | category | flops | bytes accessed | tf_op | source)
XLA Modules:
  0.0 45.2 jit_solution(3610545283075056205)
XLA Ops:
  0.0 5.0 %collective-permute-start = (bf16[1,256,128]{2,1,0:T(8,128)(2,1)}, bf16[1,256,128]{2,1,0:T(8,128)(2,1)S(1)}, u32[]{:S(2)}, u32[]{:S(2)}) collective-permute-start(bf16[1,256,128]{2,1,0:T(8,128)(2,1)} %bitcast.8), channel_id=1, source_target_pairs={{0,24},{2,26},{4,28},{6,30},{8,16},{10,18},{12,20},{14,22},{16,8},... | collective-permute-start | bytes 196616 | tf_op jit(solution)/shard_map/ppermute | solution.py:322
  5.0 0.0 collective-permute-start.1
  5.1 0.6 %collective-permute-start.2 = (bf16[1,256,128]{2,1,0:T(8,128)(2,1)}, bf16[1,256,128]{2,1,0:T(8,128)(2,1)S(1)}, u32[]{:S(2)}, u32[]{:S(2)}) collective-permute-start(bf16[1,256,128]{2,1,0:T(8,128)(2,1)} %bitcast.10), channel_id=1, source_target_pairs={{0,16},{2,18},{4,20},{6,22},{8,24},{10,26},{12,28},{14,30},{16,0},... | collective-permute-start | bytes 196616 | tf_op jit(solution)/shard_map/ppermute | solution.py:322
  5.6 0.0 copy-start.1
  5.6 1.8 %prep.1.refs_0_ = bf16[72,64,128]{2,1,0:T(8,128)(2,1)S(1)} custom-call(s32[1,64]{1,0:T(1,128)} %bitcast.13, bf16[70,64,128]{2,1,0:T(8,128)(2,1)} %bitcast.12), custom_call_target="tpu_custom_call" | custom-call | flops 2348810240 | bytes 2293760 | tf_op jit(solution)/shard_map/prep/pallas_call | solution.py:64
  7.4 0.7 %collective-permute-done = bf16[1,256,128]{2,1,0:T(8,128)(2,1)S(1)} collective-permute-done((bf16[1,256,128]{2,1,0:T(8,128)(2,1)}, bf16[1,256,128]{2,1,0:T(8,128)(2,1)S(1)}, u32[]{:S(2)}, u32[]{:S(2)}) %collective-permute-start) | collective-permute-done | bytes 65568 | tf_op jit(solution)/shard_map/ppermute | solution.py:322
  8.2 1.8 %collective-permute-done.1 = bf16[1,256,128]{2,1,0:T(8,128)(2,1)S(1)} collective-permute-done((bf16[1,256,128]{2,1,0:T(8,128)(2,1)}, bf16[1,256,128]{2,1,0:T(8,128)(2,1)S(1)}, u32[]{:S(2)}, u32[]{:S(2)}) %collective-permute-start.1) | collective-permute-done | bytes 65568 | tf_op jit(solution)/shard_map/ppermute | solution.py:322
  9.9 1.0 %collective-permute-done.2 = bf16[1,256,128]{2,1,0:T(8,128)(2,1)S(1)} collective-permute-done((bf16[1,256,128]{2,1,0:T(8,128)(2,1)}, bf16[1,256,128]{2,1,0:T(8,128)(2,1)S(1)}, u32[]{:S(2)}, u32[]{:S(2)}) %collective-permute-start.2) | collective-permute-done | bytes 65568 | tf_op jit(solution)/shard_map/ppermute | solution.py:322
  10.9 0.0 collective-permute-start.3
  10.9 0.0 copy-done.1
  11.0 1.6 %collective-permute-start.6 = (bf16[4,256,128]{2,1,0:T(8,128)(2,1)S(1)}, bf16[4,256,128]{2,1,0:T(8,128)(2,1)S(1)}, u32[]{:S(2)}, u32[]{:S(2)}) collective-permute-start(bf16[4,256,128]{2,1,0:T(8,128)(2,1)S(1)} %pad_maximum_fusion.refs_2_), channel_id=1, source_target_pairs={{0,4},{2,6},{4,0},{6,2},{8,12},{10,14},{12,8},{14,10},{16,20},{18,... | collective-permute-start | bytes 786440 | tf_op jit(solution)/shard_map/ppermute | solution.py:322
  12.6 1.5 %collective-permute-start.5 = (bf16[4,256,128]{2,1,0:T(8,128)(2,1)S(1)}, bf16[4,256,128]{2,1,0:T(8,128)(2,1)S(1)}, u32[]{:S(2)}, u32[]{:S(2)}) collective-permute-start(bf16[4,256,128]{2,1,0:T(8,128)(2,1)S(1)} %pad_maximum_fusion.refs_2_), channel_id=1, source_target_pairs={{0,2},{2,0},{4,6},{6,4},{8,10},{10,8},{12,14},{14,12},{16,18},{18,... | collective-permute-start | bytes 786440 | tf_op jit(solution)/shard_map/ppermute | solution.py:322
  14.0 0.5 %collective-permute-start.4 = (bf16[4,256,128]{2,1,0:T(8,128)(2,1)S(1)}, bf16[4,256,128]{2,1,0:T(8,128)(2,1)S(1)}, u32[]{:S(2)}, u32[]{:S(2)}) collective-permute-start(bf16[4,256,128]{2,1,0:T(8,128)(2,1)S(1)} %pad_maximum_fusion.refs_2_), channel_id=1, source_target_pairs={{0,6},{2,4},{4,2},{6,0},{8,14},{10,12},{12,10},{14,8},{16,22},{18,... | collective-permute-start | bytes 786440 | tf_op jit(solution)/shard_map/ppermute | solution.py:322
  14.5 0.0 collective-permute-done.3.refs_1_
  14.6 0.1 maximum_reduce_fusion
  14.7 4.5 %score.4.refs_3_ = f32[4,8,128]{2,1,0:T(8,128)S(1)} custom-call(s32[4]{0:T(128)S(1)} %fusion.counts_ref, bf16[72,64,128]{2,1,0:T(8,128)(2,1)S(1)} %prep.1.refs_0_, bf16[72,64,128]{2,1,0:T(8,128)(2,1)S(1)} %collective-permute-done.3.refs_1_, bf16[4,256,128]{2,1,0:T(8,128)(2,1)S(1)} %pad_maximum_fusion.refs_2_), custom_call_target="tpu_custom_call" | custom-call | flops 4831838208 | bytes 2359296 | tf_op jit(solution)/shard_map/score/pallas_call | solution.py:278
  19.2 0.6 %collective-permute-done.6.refs_2_ = bf16[4,256,128]{2,1,0:T(8,128)(2,1)S(1)} collective-permute-done((bf16[4,256,128]{2,1,0:T(8,128)(2,1)S(1)}, bf16[4,256,128]{2,1,0:T(8,128)(2,1)S(1)}, u32[]{:S(2)}, u32[]{:S(2)}) %collective-permute-start.6) | collective-permute-done | bytes 262176 | tf_op jit(solution)/shard_map/ppermute | solution.py:322
  19.8 4.6 %score.6.refs_5_ = f32[4,8,128]{2,1,0:T(8,128)S(1)} custom-call(s32[4]{0:T(128)S(1)} %fusion.counts_ref, bf16[72,64,128]{2,1,0:T(8,128)(2,1)S(1)} %prep.1.refs_0_, bf16[72,64,128]{2,1,0:T(8,128)(2,1)S(1)} %collective-permute-done.3.refs_1_, bf16[4,256,128]{2,1,0:T(8,128)(2,1)S(1)} %collective-permute-done.6.refs_2_), custom_call_target="tpu_custom_call" | custom-call | flops 4831838208 | bytes 2359296 | tf_op jit(solution)/shard_map/score/pallas_call | solution.py:278
  24.3 0.0 collective-permute-done.5.refs_2_
  24.3 4.6 %score.5.refs_4_ = f32[4,8,128]{2,1,0:T(8,128)S(1)} custom-call(s32[4]{0:T(128)S(1)} %fusion.counts_ref, bf16[72,64,128]{2,1,0:T(8,128)(2,1)S(1)} %prep.1.refs_0_, bf16[72,64,128]{2,1,0:T(8,128)(2,1)S(1)} %collective-permute-done.3.refs_1_, bf16[4,256,128]{2,1,0:T(8,128)(2,1)S(1)} %collective-permute-done.5.refs_2_), custom_call_target="tpu_custom_call" | custom-call | flops 4831838208 | bytes 2359296 | tf_op jit(solution)/shard_map/score/pallas_call | solution.py:278
  28.9 0.0 copy-start.2
  28.9 0.0 copy-start
  28.9 0.0 collective-permute-done.4.refs_2_
  28.9 5.2 %score.7 = f32[16,8,128]{2,1,0:T(8,128)} custom-call(s32[4]{0:T(128)S(1)} %fusion.counts_ref, bf16[72,64,128]{2,1,0:T(8,128)(2,1)S(1)} %prep.1.refs_0_, bf16[72,64,128]{2,1,0:T(8,128)(2,1)S(1)} %collective-permute-done.3.refs_1_, bf16[4,256,128]{2,1,0:T(8,128)(2,1)S(1)} %collective-permute-done.4.refs_2_, f32[4,8,128]{2,1,0:T(8,128)S(1)} %score.4.refs_3_, ...), custom_call_target="tpu_custom_call" | custom-call | flops 4831838208 | bytes 2359296 | tf_op jit(solution)/shard_map/score/pallas_call | solution.py:278
  34.2 7.4 %all-to-all-start = ((f32[16,8,128]{2,1,0:T(8,128)}), f32[16,8,128]{2,1,0:T(8,128)S(1)}, u32[]{:S(2)}, u32[]{:S(2)}) async-start(f32[16,8,128]{2,1,0:T(8,128)} %score.7), calls=%async_computation | async-start | bytes 131072 | tf_op jit(solution)/shard_map/all_to_all | solution.py:348
  41.6 0.0 copy-done.2
  41.6 2.9 %all-to-all-done.table_ref = f32[16,8,128]{2,1,0:T(8,128)S(1)} async-done(((f32[16,8,128]{2,1,0:T(8,128)}), f32[16,8,128]{2,1,0:T(8,128)S(1)}, u32[]{:S(2)}, u32[]{:S(2)}) %all-to-all-start) | async-done | bytes 65568 | tf_op jit(solution)/shard_map/all_to_all | solution.py:348
  44.5 0.0 copy-done
  44.5 0.7 %pick.1 = f32[8,256]{1,0:T(8,128)} custom-call(s32[1]{0:T(128)} %bitcast.core_ref, f32[16,8,128]{2,1,0:T(8,128)S(1)} %all-to-all-done.table_ref, s32[8,256]{1,0:T(8,128)S(1)} %bitcast.7, s32[8,256]{1,0:T(8,128)S(1)} %copy-done), custom_call_target="tpu_custom_call" | custom-call | tf_op jit(solution)/shard_map/pick/pallas_call | solution.py:352
  (5 shorter events, 0.1 us)
Async XLA Ops:
  0.0 8.2 %collective-permute-start = (bf16[1,256,128]{2,1,0:T(8,128)(2,1)}, bf16[1,256,128]{2,1,0:T(8,128)(2,1)S(1)}, u32[]{:S(2)}, u32[]{:S(2)}) collective-permute-start(bf16[1,256,128]{2,1,0:T(8,128)(2,1)} %bitcast.8), channel_id=1, source_target_pairs={{0,24},{2,26},{4,28},{6,30},{8,16},{10,18},{12,20},{14,22},{16,8},... | collective-permute-start | bytes 196616 | tf_op jit(solution)/shard_map/ppermute | solution.py:322
  5.0 4.9 %collective-permute-start.1 = (bf16[1,256,128]{2,1,0:T(8,128)(2,1)}, bf16[1,256,128]{2,1,0:T(8,128)(2,1)S(1)}, u32[]{:S(2)}, u32[]{:S(2)}) collective-permute-start(bf16[1,256,128]{2,1,0:T(8,128)(2,1)} %bitcast.9), channel_id=1, source_target_pairs={{0,8},{2,10},{4,12},{6,14},{8,0},{10,2},{12,4},{14,6},{16,24},{18,... | collective-permute-start | bytes 196616 | tf_op jit(solution)/shard_map/ppermute | solution.py:322
  5.1 5.8 %collective-permute-start.2 = (bf16[1,256,128]{2,1,0:T(8,128)(2,1)}, bf16[1,256,128]{2,1,0:T(8,128)(2,1)S(1)}, u32[]{:S(2)}, u32[]{:S(2)}) collective-permute-start(bf16[1,256,128]{2,1,0:T(8,128)(2,1)} %bitcast.10), channel_id=1, source_target_pairs={{0,16},{2,18},{4,20},{6,22},{8,24},{10,26},{12,28},{14,30},{16,0},... | collective-permute-start | bytes 196616 | tf_op jit(solution)/shard_map/ppermute | solution.py:322
  5.6 5.3 %copy-start.1 = (bf16[8,32,128]{2,1,0:T(8,128)(2,1)S(1)}, bf16[8,32,128]{2,1,0:T(8,128)(2,1)}, u32[]{:S(2)}) copy-start(bf16[8,32,128]{2,1,0:T(8,128)(2,1)} %param.5) | copy-start | bytes 196612
  10.9 3.6 %collective-permute-start.3 = (bf16[72,64,128]{2,1,0:T(8,128)(2,1)S(1)}, bf16[72,64,128]{2,1,0:T(8,128)(2,1)S(1)}, u32[]{:S(2)}, u32[]{:S(2)}) collective-permute-start(bf16[72,64,128]{2,1,0:T(8,128)(2,1)S(1)} %prep.1.refs_0_), channel_id=1, source_target_pairs={{0,1},{1,0},{2,3},{3,2},{4,5},{5,4},{6,7},{7,6},{8,9},{9,8},{10,11... | collective-permute-start | bytes 3538952 | tf_op jit(solution)/shard_map/ppermute | solution.py:335
  11.0 8.8 %collective-permute-start.6 = (bf16[4,256,128]{2,1,0:T(8,128)(2,1)S(1)}, bf16[4,256,128]{2,1,0:T(8,128)(2,1)S(1)}, u32[]{:S(2)}, u32[]{:S(2)}) collective-permute-start(bf16[4,256,128]{2,1,0:T(8,128)(2,1)S(1)} %pad_maximum_fusion.refs_2_), channel_id=1, source_target_pairs={{0,4},{2,6},{4,0},{6,2},{8,12},{10,14},{12,8},{14,10},{16,20},{18,... | collective-permute-start | bytes 786440 | tf_op jit(solution)/shard_map/ppermute | solution.py:322
  12.6 11.8 %collective-permute-start.5 = (bf16[4,256,128]{2,1,0:T(8,128)(2,1)S(1)}, bf16[4,256,128]{2,1,0:T(8,128)(2,1)S(1)}, u32[]{:S(2)}, u32[]{:S(2)}) collective-permute-start(bf16[4,256,128]{2,1,0:T(8,128)(2,1)S(1)} %pad_maximum_fusion.refs_2_), channel_id=1, source_target_pairs={{0,2},{2,0},{4,6},{6,4},{8,10},{10,8},{12,14},{14,12},{16,18},{18,... | collective-permute-start | bytes 786440 | tf_op jit(solution)/shard_map/ppermute | solution.py:322
  14.0 14.9 %collective-permute-start.4 = (bf16[4,256,128]{2,1,0:T(8,128)(2,1)S(1)}, bf16[4,256,128]{2,1,0:T(8,128)(2,1)S(1)}, u32[]{:S(2)}, u32[]{:S(2)}) collective-permute-start(bf16[4,256,128]{2,1,0:T(8,128)(2,1)S(1)} %pad_maximum_fusion.refs_2_), channel_id=1, source_target_pairs={{0,6},{2,4},{4,2},{6,0},{8,14},{10,12},{12,10},{14,8},{16,22},{18,... | collective-permute-start | bytes 786440 | tf_op jit(solution)/shard_map/ppermute | solution.py:322
  28.9 12.7 %copy-start.2 = (s32[8,256,1]{1,2,0:T(1,128)S(1)}, s32[8,256,1]{1,2,0:T(1,128)}, u32[]{:S(2)}) copy-start(s32[8,256,1]{1,2,0:T(1,128)} %param.6) | copy-start | bytes 24580
  28.9 15.6 %copy-start = (s32[8,256]{1,0:T(8,128)S(1)}, s32[8,256]{1,0:T(8,128)}, u32[]{:S(2)}) copy-start(s32[8,256]{1,0:T(8,128)} %local_ref.1) | copy-start | bytes 24580
  34.2 10.3 %all-to-all-start = ((f32[16,8,128]{2,1,0:T(8,128)}), f32[16,8,128]{2,1,0:T(8,128)S(1)}, u32[]{:S(2)}, u32[]{:S(2)}) async-start(f32[16,8,128]{2,1,0:T(8,128)} %score.7), calls=%async_computation | async-start | bytes 131072 | tf_op jit(solution)/shard_map/all_to_all | solution.py:348

commit v10 on v9

--- a/solution.py
+++ b/solution.py
@@ -8,7 +8,6 @@
 from jax.sharding import PartitionSpec as P
 
 VMEM = pl.BlockSpec(memory_space=pltpu.VMEM)
-SMEM = pl.BlockSpec(memory_space=pltpu.SMEM)
 TOKENS = 32
 BLOCKS = 4
 GROUPS = 3
@@ -298,14 +297,14 @@
     )(*scalars, *operands)
 
 
-def pick_kernel(core_ref, table_ref, shard_ref, local_ref, out_ref):
+def pick_kernel(table_ref, shard_ref, local_ref, out_ref):
     chips, rows, width = table_ref.shape
     store = width // 2
     for half in range(shard_ref.shape[1] // LANES):
         lanes = slice(half * LANES, half * LANES + LANES)
         shard = shard_ref[:, lanes]
         chip = chips - 1 - shard // 2
-        lane = ((shard % 2) ^ core_ref[0]) * store + local_ref[:, lanes]
+        lane = ((shard % 2) ^ lax.axis_index("qry")) * store + local_ref[:, lanes]
         total = jnp.zeros(lane.shape, jnp.float32)
         for k in range(chips):
             found = jnp.take_along_axis(table_ref[k], lane, axis=1)
@@ -314,7 +313,6 @@
 
 
 def body(queries, cand_shard, cand_local, passages, lengths):
-    core = lax.axis_index("qry").reshape(1).astype(jnp.int32)
     chips = lax.axis_size("psg")
     local, qlen, dim = queries.shape
 
@@ -352,11 +350,11 @@
     return pl.pallas_call(
         pick_kernel,
         out_shape=jax.ShapeDtypeStruct(cand_local.shape, jnp.float32),
-        in_specs=[SMEM, VMEM, VMEM, VMEM],
+        in_specs=[VMEM, VMEM, VMEM],
         out_specs=VMEM,
         compiler_params=pltpu.CompilerParams(vmem_limit_bytes=4 << 20),
         name="pick",
-    )(core, returned, cand_shard[:, :, 0], cand_local)
+    )(returned, cand_shard[:, :, 0], cand_local)
 
 
 def solution(mesh):

time: 45.4 us -> 45.4 us (level)
  no operation moved by 1% of the time
where the time goes in v10:
time: 45.4 us; the launch traced here: 45.3 us
  Pallas kernels  21.3 us (47%)
  starting transfers between devices  16.6 us (37%)
  waiting for transfers between devices  7 us (15%)
    pallas_call x4, Pallas kernels, score(): pl.pallas_call(functools.partial(score_kernel, first, len(earlier), rows_...  18.8 us
    ppermute x6, starting transfers between devices, swap(): return lax.ppermute(a, 'psg', [(i, i ^ bits) for i in range(chips)])  9.17 us
    all_to_all x1, starting transfers between devices, body(): lax.all_to_all(table, 'psg', split_axis=0, concat_axis=0, tiled=True, axi...  7.42 us
    ppermute x6, waiting for transfers between devices, swap(): return lax.ppermute(a, 'psg', [(i, i ^ bits) for i in range(chips)])  4.06 us
    all_to_all x1, waiting for transfers between devices, body(): lax.all_to_all(table, 'psg', split_axis=0, concat_axis=0, tiled=True, axi...  2.93 us
    pallas_call x1, Pallas kernels, prep(): pl.pallas_call(prep_kernel, out_shape=jax.ShapeDtypeStruct((slots + 2, st...  1.78 us
  transfers between devices with their start and end apart: 8, of which 5 were waited for; matrix products, arithmetic and copies ran while one was open for 1% of the time, Pallas kernels for 34%

profile of v10, /device:TPU:0, one launch (start us, length us, event | category | flops | bytes accessed | tf_op | source)
XLA Modules:
  0.0 45.3 jit_solution(9564588683326001354)
XLA Ops:
  0.0 5.0 %collective-permute-start = (bf16[1,256,128]{2,1,0:T(8,128)(2,1)}, bf16[1,256,128]{2,1,0:T(8,128)(2,1)S(1)}, u32[]{:S(2)}, u32[]{:S(2)}) collective-permute-start(bf16[1,256,128]{2,1,0:T(8,128)(2,1)} %bitcast.7), channel_id=1, source_target_pairs={{0,24},{2,26},{4,28},{6,30},{8,16},{10,18},{12,20},{14,22},{16,8},... | collective-permute-start | bytes 196616 | tf_op jit(solution)/shard_map/ppermute | solution.py:320
  5.0 0.0 collective-permute-start.1
  5.1 0.6 %collective-permute-start.2 = (bf16[1,256,128]{2,1,0:T(8,128)(2,1)}, bf16[1,256,128]{2,1,0:T(8,128)(2,1)S(1)}, u32[]{:S(2)}, u32[]{:S(2)}) collective-permute-start(bf16[1,256,128]{2,1,0:T(8,128)(2,1)} %bitcast.9), channel_id=1, source_target_pairs={{0,16},{2,18},{4,20},{6,22},{8,24},{10,26},{12,28},{14,30},{16,0},... | collective-permute-start | bytes 196616 | tf_op jit(solution)/shard_map/ppermute | solution.py:320
  5.6 0.0 copy-start.1
  5.6 1.8 %prep.1.refs_0_ = bf16[72,64,128]{2,1,0:T(8,128)(2,1)S(1)} custom-call(s32[1,64]{1,0:T(1,128)} %bitcast.12, bf16[70,64,128]{2,1,0:T(8,128)(2,1)} %bitcast.11), custom_call_target="tpu_custom_call" | custom-call | flops 2348810240 | bytes 2293760 | tf_op jit(solution)/shard_map/prep/pallas_call | solution.py:63
  7.4 0.7 %collective-permute-done = bf16[1,256,128]{2,1,0:T(8,128)(2,1)S(1)} collective-permute-done((bf16[1,256,128]{2,1,0:T(8,128)(2,1)}, bf16[1,256,128]{2,1,0:T(8,128)(2,1)S(1)}, u32[]{:S(2)}, u32[]{:S(2)}) %collective-permute-start) | collective-permute-done | bytes 65568 | tf_op jit(solution)/shard_map/ppermute | solution.py:320
  8.2 1.8 %collective-permute-done.1 = bf16[1,256,128]{2,1,0:T(8,128)(2,1)S(1)} collective-permute-done((bf16[1,256,128]{2,1,0:T(8,128)(2,1)}, bf16[1,256,128]{2,1,0:T(8,128)(2,1)S(1)}, u32[]{:S(2)}, u32[]{:S(2)}) %collective-permute-start.1) | collective-permute-done | bytes 65568 | tf_op jit(solution)/shard_map/ppermute | solution.py:320
  9.9 1.0 %collective-permute-done.2 = bf16[1,256,128]{2,1,0:T(8,128)(2,1)S(1)} collective-permute-done((bf16[1,256,128]{2,1,0:T(8,128)(2,1)}, bf16[1,256,128]{2,1,0:T(8,128)(2,1)S(1)}, u32[]{:S(2)}, u32[]{:S(2)}) %collective-permute-start.2) | collective-permute-done | bytes 65568 | tf_op jit(solution)/shard_map/ppermute | solution.py:320
  10.9 0.0 collective-permute-start.3
  10.9 0.0 copy-done.1
  11.0 1.6 %collective-permute-start.6 = (bf16[4,256,128]{2,1,0:T(8,128)(2,1)S(1)}, bf16[4,256,128]{2,1,0:T(8,128)(2,1)S(1)}, u32[]{:S(2)}, u32[]{:S(2)}) collective-permute-start(bf16[4,256,128]{2,1,0:T(8,128)(2,1)S(1)} %pad_maximum_fusion.refs_2_), channel_id=1, source_target_pairs={{0,4},{2,6},{4,0},{6,2},{8,12},{10,14},{12,8},{14,10},{16,20},{18,... | collective-permute-start | bytes 786440 | tf_op jit(solution)/shard_map/ppermute | solution.py:320
  12.6 1.5 %collective-permute-start.5 = (bf16[4,256,128]{2,1,0:T(8,128)(2,1)S(1)}, bf16[4,256,128]{2,1,0:T(8,128)(2,1)S(1)}, u32[]{:S(2)}, u32[]{:S(2)}) collective-permute-start(bf16[4,256,128]{2,1,0:T(8,128)(2,1)S(1)} %pad_maximum_fusion.refs_2_), channel_id=1, source_target_pairs={{0,2},{2,0},{4,6},{6,4},{8,10},{10,8},{12,14},{14,12},{16,18},{18,... | collective-permute-start | bytes 786440 | tf_op jit(solution)/shard_map/ppermute | solution.py:320
  14.0 0.5 %collective-permute-start.4 = (bf16[4,256,128]{2,1,0:T(8,128)(2,1)S(1)}, bf16[4,256,128]{2,1,0:T(8,128)(2,1)S(1)}, u32[]{:S(2)}, u32[]{:S(2)}) collective-permute-start(bf16[4,256,128]{2,1,0:T(8,128)(2,1)S(1)} %pad_maximum_fusion.refs_2_), channel_id=1, source_target_pairs={{0,6},{2,4},{4,2},{6,0},{8,14},{10,12},{12,10},{14,8},{16,22},{18,... | collective-permute-start | bytes 786440 | tf_op jit(solution)/shard_map/ppermute | solution.py:320
  14.5 0.0 collective-permute-done.3.refs_1_
  14.6 0.1 maximum_reduce_fusion
  14.7 4.5 %score.4.refs_3_ = f32[4,8,128]{2,1,0:T(8,128)S(1)} custom-call(s32[4]{0:T(128)S(1)} %fusion.counts_ref, bf16[72,64,128]{2,1,0:T(8,128)(2,1)S(1)} %prep.1.refs_0_, bf16[72,64,128]{2,1,0:T(8,128)(2,1)S(1)} %collective-permute-done.3.refs_1_, bf16[4,256,128]{2,1,0:T(8,128)(2,1)S(1)} %pad_maximum_fusion.refs_2_), custom_call_target="tpu_custom_call" | custom-call | flops 4831838208 | bytes 2359296 | tf_op jit(solution)/shard_map/score/pallas_call | solution.py:277
  19.2 0.6 %collective-permute-done.6.refs_2_ = bf16[4,256,128]{2,1,0:T(8,128)(2,1)S(1)} collective-permute-done((bf16[4,256,128]{2,1,0:T(8,128)(2,1)S(1)}, bf16[4,256,128]{2,1,0:T(8,128)(2,1)S(1)}, u32[]{:S(2)}, u32[]{:S(2)}) %collective-permute-start.6) | collective-permute-done | bytes 262176 | tf_op jit(solution)/shard_map/ppermute | solution.py:320
  19.8 4.6 %score.6.refs_5_ = f32[4,8,128]{2,1,0:T(8,128)S(1)} custom-call(s32[4]{0:T(128)S(1)} %fusion.counts_ref, bf16[72,64,128]{2,1,0:T(8,128)(2,1)S(1)} %prep.1.refs_0_, bf16[72,64,128]{2,1,0:T(8,128)(2,1)S(1)} %collective-permute-done.3.refs_1_, bf16[4,256,128]{2,1,0:T(8,128)(2,1)S(1)} %collective-permute-done.6.refs_2_), custom_call_target="tpu_custom_call" | custom-call | flops 4831838208 | bytes 2359296 | tf_op jit(solution)/shard_map/score/pallas_call | solution.py:277
  24.3 0.0 collective-permute-done.5.refs_2_
  24.3 4.6 %score.5.refs_4_ = f32[4,8,128]{2,1,0:T(8,128)S(1)} custom-call(s32[4]{0:T(128)S(1)} %fusion.counts_ref, bf16[72,64,128]{2,1,0:T(8,128)(2,1)S(1)} %prep.1.refs_0_, bf16[72,64,128]{2,1,0:T(8,128)(2,1)S(1)} %collective-permute-done.3.refs_1_, bf16[4,256,128]{2,1,0:T(8,128)(2,1)S(1)} %collective-permute-done.5.refs_2_), custom_call_target="tpu_custom_call" | custom-call | flops 4831838208 | bytes 2359296 | tf_op jit(solution)/shard_map/score/pallas_call | solution.py:277
  28.9 0.0 copy-start.2
  28.9 0.0 copy-start
  28.9 0.0 collective-permute-done.4.refs_2_
  28.9 5.2 %score.7 = f32[16,8,128]{2,1,0:T(8,128)} custom-call(s32[4]{0:T(128)S(1)} %fusion.counts_ref, bf16[72,64,128]{2,1,0:T(8,128)(2,1)S(1)} %prep.1.refs_0_, bf16[72,64,128]{2,1,0:T(8,128)(2,1)S(1)} %collective-permute-done.3.refs_1_, bf16[4,256,128]{2,1,0:T(8,128)(2,1)S(1)} %collective-permute-done.4.refs_2_, f32[4,8,128]{2,1,0:T(8,128)S(1)} %score.4.refs_3_, ...), custom_call_target="tpu_custom_call" | custom-call | flops 4831838208 | bytes 2359296 | tf_op jit(solution)/shard_map/score/pallas_call | solution.py:277
  34.2 7.4 %all-to-all-start = ((f32[16,8,128]{2,1,0:T(8,128)}), f32[16,8,128]{2,1,0:T(8,128)S(1)}, u32[]{:S(2)}, u32[]{:S(2)}) async-start(f32[16,8,128]{2,1,0:T(8,128)} %score.7), calls=%async_computation | async-start | bytes 131072 | tf_op jit(solution)/shard_map/all_to_all | solution.py:346
  41.6 0.0 copy-done.2
  41.6 2.9 %all-to-all-done.table_ref = f32[16,8,128]{2,1,0:T(8,128)S(1)} async-done(((f32[16,8,128]{2,1,0:T(8,128)}), f32[16,8,128]{2,1,0:T(8,128)S(1)}, u32[]{:S(2)}, u32[]{:S(2)}) %all-to-all-start) | async-done | bytes 65568 | tf_op jit(solution)/shard_map/all_to_all | solution.py:346
  44.5 0.0 copy-done
  44.5 0.7 %pick.1 = f32[8,256]{1,0:T(8,128)} custom-call(f32[16,8,128]{2,1,0:T(8,128)S(1)} %all-to-all-done.table_ref, s32[8,256]{1,0:T(8,128)S(1)} %bitcast.6, s32[8,256]{1,0:T(8,128)S(1)} %copy-done), custom_call_target="tpu_custom_call" | custom-call | tf_op jit(solution)/shard_map/pick/pallas_call | solution.py:350
  (5 shorter events, 0.1 us)
Async XLA Ops:
  0.0 8.2 %collective-permute-start = (bf16[1,256,128]{2,1,0:T(8,128)(2,1)}, bf16[1,256,128]{2,1,0:T(8,128)(2,1)S(1)}, u32[]{:S(2)}, u32[]{:S(2)}) collective-permute-start(bf16[1,256,128]{2,1,0:T(8,128)(2,1)} %bitcast.7), channel_id=1, source_target_pairs={{0,24},{2,26},{4,28},{6,30},{8,16},{10,18},{12,20},{14,22},{16,8},... | collective-permute-start | bytes 196616 | tf_op jit(solution)/shard_map/ppermute | solution.py:320
  5.0 4.9 %collective-permute-start.1 = (bf16[1,256,128]{2,1,0:T(8,128)(2,1)}, bf16[1,256,128]{2,1,0:T(8,128)(2,1)S(1)}, u32[]{:S(2)}, u32[]{:S(2)}) collective-permute-start(bf16[1,256,128]{2,1,0:T(8,128)(2,1)} %bitcast.8), channel_id=1, source_target_pairs={{0,8},{2,10},{4,12},{6,14},{8,0},{10,2},{12,4},{14,6},{16,24},{18,... | collective-permute-start | bytes 196616 | tf_op jit(solution)/shard_map/ppermute | solution.py:320
  5.1 5.8 %collective-permute-start.2 = (bf16[1,256,128]{2,1,0:T(8,128)(2,1)}, bf16[1,256,128]{2,1,0:T(8,128)(2,1)S(1)}, u32[]{:S(2)}, u32[]{:S(2)}) collective-permute-start(bf16[1,256,128]{2,1,0:T(8,128)(2,1)} %bitcast.9), channel_id=1, source_target_pairs={{0,16},{2,18},{4,20},{6,22},{8,24},{10,26},{12,28},{14,30},{16,0},... | collective-permute-start | bytes 196616 | tf_op jit(solution)/shard_map/ppermute | solution.py:320
  5.6 5.3 %copy-start.1 = (bf16[8,32,128]{2,1,0:T(8,128)(2,1)S(1)}, bf16[8,32,128]{2,1,0:T(8,128)(2,1)}, u32[]{:S(2)}) copy-start(bf16[8,32,128]{2,1,0:T(8,128)(2,1)} %param.5) | copy-start | bytes 196612
  10.9 3.6 %collective-permute-start.3 = (bf16[72,64,128]{2,1,0:T(8,128)(2,1)S(1)}, bf16[72,64,128]{2,1,0:T(8,128)(2,1)S(1)}, u32[]{:S(2)}, u32[]{:S(2)}) collective-permute-start(bf16[72,64,128]{2,1,0:T(8,128)(2,1)S(1)} %prep.1.refs_0_), channel_id=1, source_target_pairs={{0,1},{1,0},{2,3},{3,2},{4,5},{5,4},{6,7},{7,6},{8,9},{9,8},{10,11... | collective-permute-start | bytes 3538952 | tf_op jit(solution)/shard_map/ppermute | solution.py:333
  11.0 8.8 %collective-permute-start.6 = (bf16[4,256,128]{2,1,0:T(8,128)(2,1)S(1)}, bf16[4,256,128]{2,1,0:T(8,128)(2,1)S(1)}, u32[]{:S(2)}, u32[]{:S(2)}) collective-permute-start(bf16[4,256,128]{2,1,0:T(8,128)(2,1)S(1)} %pad_maximum_fusion.refs_2_), channel_id=1, source_target_pairs={{0,4},{2,6},{4,0},{6,2},{8,12},{10,14},{12,8},{14,10},{16,20},{18,... | collective-permute-start | bytes 786440 | tf_op jit(solution)/shard_map/ppermute | solution.py:320
  12.6 11.8 %collective-permute-start.5 = (bf16[4,256,128]{2,1,0:T(8,128)(2,1)S(1)}, bf16[4,256,128]{2,1,0:T(8,128)(2,1)S(1)}, u32[]{:S(2)}, u32[]{:S(2)}) collective-permute-start(bf16[4,256,128]{2,1,0:T(8,128)(2,1)S(1)} %pad_maximum_fusion.refs_2_), channel_id=1, source_target_pairs={{0,2},{2,0},{4,6},{6,4},{8,10},{10,8},{12,14},{14,12},{16,18},{18,... | collective-permute-start | bytes 786440 | tf_op jit(solution)/shard_map/ppermute | solution.py:320
  14.0 14.9 %collective-permute-start.4 = (bf16[4,256,128]{2,1,0:T(8,128)(2,1)S(1)}, bf16[4,256,128]{2,1,0:T(8,128)(2,1)S(1)}, u32[]{:S(2)}, u32[]{:S(2)}) collective-permute-start(bf16[4,256,128]{2,1,0:T(8,128)(2,1)S(1)} %pad_maximum_fusion.refs_2_), channel_id=1, source_target_pairs={{0,6},{2,4},{4,2},{6,0},{8,14},{10,12},{12,10},{14,8},{16,22},{18,... | collective-permute-start | bytes 786440 | tf_op jit(solution)/shard_map/ppermute | solution.py:320
  28.9 12.7 %copy-start.2 = (s32[8,256,1]{1,2,0:T(1,128)S(1)}, s32[8,256,1]{1,2,0:T(1,128)}, u32[]{:S(2)}) copy-start(s32[8,256,1]{1,2,0:T(1,128)} %param.6) | copy-start | bytes 24580
  28.9 15.6 %copy-start = (s32[8,256]{1,0:T(8,128)S(1)}, s32[8,256]{1,0:T(8,128)}, u32[]{:S(2)}) copy-start(s32[8,256]{1,0:T(8,128)} %local_ref.1) | copy-start | bytes 24580
  34.2 10.4 %all-to-all-start = ((f32[16,8,128]{2,1,0:T(8,128)}), f32[16,8,128]{2,1,0:T(8,128)S(1)}, u32[]{:S(2)}, u32[]{:S(2)}) async-start(f32[16,8,128]{2,1,0:T(8,128)} %score.7), calls=%async_computation | async-start | bytes 131072 | tf_op jit(solution)/shard_map/all_to_all | solution.py:346
